TPU v7x, 128 devices: a whole 4x4x4 slice. The times are simulated.
128 devices in a mesh: grp: 4 (over x), dev: 32 (over y, z, core).
Axes of the slice: x: 4, y: 4, z: 4, core: 2. Of those that a mesh axis runs over, the one named last changes fastest.
Arguments:
- tile_list: int32 [256, 3], replicated, may hold values from 0 to 127, as said below
- holder: int32 [128], replicated, may hold values from 0 to 127, each once
- coordinates: float32 [3, 131072], P(None, ('grp', 'dev')), may hold values from -6 to 6
- dissim: bfloat16 [512, 1024, 1024], P(('grp', 'dev')), may hold values from 0.5 to 4
Outputs:
- guttman: float32 [3, 131072], P(None, ('grp', 'dev'))
- stress: float32 [], replicated
Inputs may be any that keep to these rules, and one draw needn't show every extreme that they name: `tile_list`: rows are distinct pairs with row block less than column block; every block is in exactly 4 tiles; each device owns 1, 2 or 4 tiles, a quarter of the devices own 4.
All inputs are finite; a program needn't handle non-finite values.
Results may differ from a plain program's by a relative error of at most 0.0003.
Values sent between devices are 32-bit elements; how exact they have to be, the bound alone decides.
No kernel may reach another device: no remote copies, remote signals or barrier semaphores. Data moves between devices by JAX's collectives and lax.ppermute only.
A program may use at most 192 MiB of HBM per device.

v0:
```python
import jax
import jax.numpy as jnp
from jax import lax
from jax.sharding import PartitionSpec as P

dist_floor = 0.25


def tile_ranks(tile_list):
    owners = tile_list[:, 2]
    indices = jnp.arange(owners.shape[0], dtype=jnp.int32)
    same_owner = owners[:, None] == owners[None, :]
    earlier = indices[None, :] < indices[:, None]
    return jnp.sum((same_owner & earlier).astype(jnp.int32), axis=1)


def tile_terms(row_coords, col_coords, target):
    squared = jnp.zeros(target.shape, jnp.float32)
    for comp in range(row_coords.shape[0]):
        gap = row_coords[comp][:, None] - col_coords[comp][None, :]
        squared = squared + gap * gap
    distance = jnp.maximum(jnp.sqrt(squared), dist_floor)
    ratio = target / distance
    row_sums = jnp.sum(ratio, axis=1)
    col_sums = jnp.sum(ratio, axis=0)
    row_cross = lax.dot_general(
        col_coords, ratio, (((1,), (1,)), ((), ())), precision=lax.Precision.HIGHEST
    )
    col_cross = lax.dot_general(
        row_coords, ratio, (((1,), (0,)), ((), ())), precision=lax.Precision.HIGHEST
    )
    row_part = row_coords * row_sums[None, :] - row_cross
    col_part = col_coords * col_sums[None, :] - col_cross
    error = target - distance
    return (row_part, col_part, jnp.sum(error * error))


def add_block(buffer, part, position):
    current = lax.dynamic_slice_in_dim(buffer, position, part.shape[1], 1)
    return lax.dynamic_update_slice_in_dim(buffer, current + part, position, 1)


def on_device(tile_list, holder, coordinates, dissim):
    devices = lax.axis_size(("grp", "dev"))
    device_self = lax.axis_index(("grp", "dev"))
    block_width = coordinates.shape[1]
    slot_count = dissim.shape[0]
    tile_rank = tile_ranks(tile_list)
    row_blocks = tile_list[:, 0]
    col_blocks = tile_list[:, 1]
    owners = tile_list[:, 2]
    everything = lax.all_gather(coordinates, ("grp", "dev"), axis=1, tiled=True)

    def block_of(block):
        position = holder[block] * block_width
        return lax.dynamic_slice_in_dim(everything, position, block_width, 1)

    row_buffer = jnp.zeros((coordinates.shape[0], devices * block_width), jnp.float32)
    col_buffer = jnp.zeros((coordinates.shape[0], devices * block_width), jnp.float32)
    local_stress = jnp.zeros((), jnp.float32)
    for slot_index in range(slot_count):
        chosen = (owners == device_self) & (tile_rank == slot_index)
        present = jnp.any(chosen).astype(jnp.float32)
        row_block = jnp.sum(jnp.where(chosen, row_blocks, 0))
        col_block = jnp.sum(jnp.where(chosen, col_blocks, 0))
        target = dissim[slot_index].astype(jnp.float32)
        row_part, col_part, tile_stress = tile_terms(
            block_of(row_block), block_of(col_block), target
        )
        row_buffer = add_block(row_buffer, row_part * present, holder[row_block] * block_width)
        col_buffer = add_block(col_buffer, col_part * present, holder[col_block] * block_width)
        local_stress = local_stress + tile_stress * present
    summed = lax.psum_scatter(row_buffer, ("grp", "dev"), scatter_dimension=1, tiled=True)
    summed = summed + lax.psum_scatter(col_buffer, ("grp", "dev"), scatter_dimension=1, tiled=True)
    stress_sum = lax.psum(local_stress, ("grp", "dev"))
    return (summed * (1.0 / block_width), stress_sum)


def solution(mesh):
    placed = (P(), P(), P(None, ("grp", "dev")), P(("grp", "dev"), None, None))
    return jax.shard_map(
        on_device,
        mesh=mesh,
        in_specs=placed,
        out_specs=(P(None, ("grp", "dev")), P()),
        check_vma=False,
    )
```

profile of v0, /device:TPU:0, one launch (start us, length us, event | category | flops | bytes accessed | tf_op | source)
XLA Modules:
  0.0 917.9 jit_solution(15905418540632310277)
XLA Ops:
  7.2 0.0 all-gather.2.cloned.1.call-start
  7.2 0.7 all-gather.2.cloned.1.call-update
  7.9 0.0 reduce-scatter.4.cloned.1.call-start
  7.9 0.8 fusion.55
  8.8 0.2 convert_reduce_fusion
  8.9 0.6 fusion.51
  9.6 0.7 fusion.53
  10.3 0.8 select_reduce_fusion.1
  25.7 1.6 fusion.56
  34.9 44.0 %all-gather.2.cloned.1.call-done = f32[3,131072]{1,0:T(4,128)} async-done(((f32[3,1024]{1,0:T(4,128)}), f32[3,131072]{1,0:T(4,128)}) %all-gather.2.cloned.1.call-update) | async-done | bytes 1572880 | tf_op jit(solution)/shard_map/all_gather | solution.py:52
  78.9 1.6 constant_dynamic-slice_fusion.5
  80.6 0.0 copy-start
  80.6 10.9 %fusion.7 = (f32[]{:T(128)}, f32[]{:T(128)}, f32[1024]{0:T(1024)S(1)}, f32[1024]{0:T(1024)S(1)}, f32[1024,1024]{1,0:T(8,128)S(1)}, /*index=5*/f32[1024]{0:T(1024)S(1)}, f32[1024]{0:T(1024)S(1)}, f32[1024,1024]{1,0:T(8,128)S(1)}) fusion(f32[1024]{0:T(1024)S(1)} %bitcast.79, f32[1024]{0:T(1024)S(1)} %bitcast.80, f32[1024]{0:T(1024)S(1)} %bitcast.81, ...), kind=kLoop, calls=%fused_computation.15 | loop fusion | flops 33550336 | bytes 12648456 | tf_op jit(solution)/shard_map/reduce_sum | solution.py:35
  91.4 0.0 copy-done
  91.4 9.9 %fusion.5 = (f32[]{:T(128)}, f32[]{:T(128)}, f32[1024]{0:T(1024)S(1)}, f32[1024]{0:T(1024)S(1)}, f32[1024,1024]{1,0:T(8,128)S(1)}, /*index=5*/f32[1024]{0:T(1024)S(1)}, f32[1024]{0:T(1024)S(1)}, f32[1024,1024]{1,0:T(8,128)S(1)}) fusion(f32[1024]{0:T(1024)S(1)} %bitcast.66, f32[1024]{0:T(1024)S(1)} %bitcast.67, f32[1024]{0:T(1024)S(1)} %bitcast.68, ...), kind=kLoop, calls=%fused_computation.13 | loop fusion | flops 33550336 | bytes 12648456 | tf_op jit(solution)/shard_map/reduce_sum | solution.py:35
  101.3 0.3 broadcast.18.clone
  101.6 4.3 fusion.29
  105.9 0.3 broadcast.18.clone.1
  106.2 2.8 fusion.18
  109.0 4.3 fusion.27
  113.3 2.9 fusion.16
  116.2 3.1 fusion.13
  119.3 4.4 fusion.24
  123.7 4.4 fusion.21
  128.1 2.9 fusion.10
  131.0 0.5 add.168
  131.5 30.7 %copy.6 = f32[3,131072]{0,1:T(8,128)} copy(f32[3,131072]{1,0:T(4,128)S(1)} %add.168) | data formatting | bytes 3145728
  162.2 0.0 reduce-scatter.4.cloned.1.call-update
  167.2 69.8 %psum.7 = f32[]{:T(128)} all-reduce(f32[]{:T(128)S(6)} %add.167), channel_id=1, replica_groups=mesh['grp'=4,'dev'=32] {'grp','dev'}, use_global_device_ids=true, to_apply=%region_27.28 | all-reduce | flops 1 | bytes 8 | tf_op jit(solution)/shard_map/psum | solution.py:75
  237.1 672.1 %reduce-scatter.4.cloned.1.call-done = f32[1024,3]{1,0:T(8,128)} async-done(((f32[131072,3]{1,0:T(8,128)}), f32[1024,3]{1,0:T(8,128)}) %reduce-scatter.4.cloned.1.call-update) | async-done | bytes 12304
  909.2 1.2 copy.7
  910.4 0.6 broadcast_multiply_fusion
Async XLA Ops:
  7.2 71.8 %all-gather.2.cloned.1.call-start = ((), (), s32[]{:S(2)}) async-start(), calls=%async_computation.1 | async-start | bytes 2113536 | tf_op jit(solution)/shard_map/all_gather | solution.py:52
  7.9 901.3 %reduce-scatter.4.cloned.1.call-start = ((), (), s32[]{:S(2)}) async-start(), calls=%async_computation.2 | async-start | bytes 67633152
  80.6 10.9 %copy-start = (bf16[4,1024,1024]{2,1,0:T(8,128)(2,1)S(1)}, bf16[4,1024,1024]{2,1,0:T(8,128)(2,1)}, u32[]{:S(2)}) copy-start(bf16[4,1024,1024]{2,1,0:T(8,128)(2,1)} %param.7) | copy-start | bytes 25165828
Sparse Core Ops, SparseCore 0:
  11.1 67.7 all-gather.1
  162.4 746.7 reduce-scatter.3
where the time goes:
time: 920 us; the launch traced here: 918 us
  waiting for transfers between devices  717 us (78%)
  blocking collectives  69.8 us (8%)
  between operations  41.2 us (4%)
  local copies, waits for them, and re-layouts  36.6 us (4%)
  matrix products  29.1 us (3%)
  other arithmetic  24.3 us (3%)
    unnamed x3, waiting for transfers between devices  673 us
    psum x1, blocking collectives, on_device(): stress_sum = lax.psum(local_stress, ('grp', 'dev'))  69.8 us
    all_gather x1, waiting for transfers between devices, on_device(): everything = lax.all_gather(coordinates, ('grp', 'dev'), axis=1, tiled=True)  44 us
    unnamed x4, local copies, waits for them, and re-layouts  31.9 us
    reduce_sum x2, other arithmetic, tile_terms(): return (row_part, col_part, jnp.sum(error * error))  20.7 us
  transfers between devices with their start and end apart: 2, of which 2 were waited for; matrix products, arithmetic and copies ran while one was open for 1% of the time, Pallas kernels for 0%

commit v1 on v0

v1 whole, which is shorter than its diff:
```python
import functools

import jax
import jax.numpy as jnp
from jax import lax
from jax.experimental import pallas as pl
from jax.experimental.pallas import tpu as pltpu
from jax.sharding import PartitionSpec as P

AXES = ("grp", "dev")
FLOOR_SQUARED = 0.0625
LANES = 128
DIM = 3
VMEM_LIMIT = 40 * 1024 * 1024


def line_perm(groups, devs, shift):
    return [
        (((g + shift) % groups) * devs + d, g * devs + d)
        for g in range(groups)
        for d in range(devs)
    ]


def core_perm(devices):
    return [(i, i ^ 1) for i in range(devices)]


def plane_groups(groups, devs):
    return [
        [g * devs + 2 * chip + core for chip in range(devs // 2)]
        for g in range(groups)
        for core in range(2)
    ]


def from_line(array, groups, devs):
    own = [array] + [
        lax.ppermute(array, AXES, line_perm(groups, devs, d)) for d in range(1, groups)
    ]
    twin = [lax.ppermute(a, AXES, core_perm(groups * devs)) for a in own]
    return own + twin


def tile_body(rows, width, sc, delta_hbm, *refs):
    sources = refs[:8]
    parts, delta, blocks, wide, row_acc, delta_sem, block_sem = refs[8:]
    slots = delta.shape[0]
    chunks = width // LANES
    half = chunks // 2

    def delta_copy(k):
        return pltpu.make_async_copy(delta_hbm.at[k], delta.at[k], delta_sem.at[k])

    for k in range(slots):
        pl.when(sc[k] > 0)(lambda k=k: delta_copy(k).start())

    def block_copy(s, i, at):
        return pltpu.make_async_copy(sources[s].at[at], blocks.at[i], block_sem.at[i])

    for i in range(2 * slots):
        for s in range(8):
            pl.when(sc[slots + i] == s)(
                lambda i=i, s=s: block_copy(s, i, sc[3 * slots + i]).start()
            )
    for i in range(2 * slots):
        block_copy(0, i, 0).wait()

    parts[2 * slots * DIM * chunks :, :] = jnp.zeros((8, LANES), jnp.float32)

    def one_tile(k, _):
        @pl.when(sc[k] > 0)
        def _():
            delta_copy(k).wait()
            for c in range(DIM):
                for j in range(chunks):
                    row = blocks[2 * k, pl.ds(c * chunks + j, 1), :]
                    wide[c, pl.ds(j * LANES, LANES), :] = jnp.transpose(
                        jnp.broadcast_to(row, (LANES, LANES))
                    )
            stress = jnp.zeros((16, LANES), jnp.float32)
            for h in range(2):
                first = h * half
                cols = [
                    [
                        jnp.broadcast_to(
                            blocks[2 * k + 1, pl.ds(c * chunks + first + j, 1), :],
                            (16, LANES),
                        )
                        for j in range(half)
                    ]
                    for c in range(DIM)
                ]

                def step(p, carry, h=h, first=first, cols=cols):
                    stress, acc = carry
                    at = pl.ds(pl.multiple_of(p * 16, 16), 16)
                    xa = [wide[c, at, :] for c in range(DIM)]
                    acc = [list(a) for a in acc]
                    sums = [None] * DIM
                    for j in range(half):
                        target = delta[
                            k, at, pl.ds((first + j) * LANES, LANES)
                        ].astype(jnp.float32)
                        gaps = [xa[c] - cols[c][j] for c in range(DIM)]
                        squared = gaps[0] * gaps[0]
                        for c in range(1, DIM):
                            squared = squared + gaps[c] * gaps[c]
                        squared = jnp.maximum(squared, FLOOR_SQUARED)
                        inverse = lax.rsqrt(squared)
                        error = target - squared * inverse
                        stress = stress + error * error
                        ratio = target * inverse
                        for c in range(DIM):
                            moved = ratio * gaps[c]
                            acc[c][j] = acc[c][j] + moved
                            sums[c] = moved if sums[c] is None else sums[c] + moved
                    for c in range(DIM):
                        if h == 0:
                            row_acc[c, at, :] = sums[c]
                        else:
                            row_acc[c, at, :] += sums[c]
                    return stress, tuple(tuple(a) for a in acc)

                zero = jnp.zeros((16, LANES), jnp.float32)
                stress, acc = lax.fori_loop(
                    0,
                    rows // 16,
                    step,
                    (stress, tuple(tuple(zero for _ in range(half)) for _ in range(DIM))),
                )
                for c in range(DIM):
                    for j in range(half):
                        parts[pl.ds((2 * k + 1) * DIM * chunks + c * chunks + first + j, 1), :] = (
                            -jnp.sum(acc[c][j], axis=0, keepdims=True)
                        )
            for c in range(DIM):
                for j in range(chunks):
                    turned = jnp.transpose(row_acc[c, pl.ds(j * LANES, LANES), :])
                    parts[pl.ds(2 * k * DIM * chunks + c * chunks + j, 1), :] = jnp.sum(
                        turned, axis=0, keepdims=True
                    )
            parts[2 * slots * DIM * chunks :, :] += stress[:8] + stress[8:]

        return 0

    lax.fori_loop(0, slots, one_tile, 0)


def tile_parts(scalars, dissim, sources):
    slots, rows, width = dissim.shape
    block_rows = DIM * width // LANES
    return pl.pallas_call(
        functools.partial(tile_body, rows, width),
        out_shape=jax.ShapeDtypeStruct((2 * slots * block_rows + 8, LANES), jnp.float32),
        in_specs=[pl.BlockSpec(memory_space=pltpu.SMEM)]
        + [pl.BlockSpec(memory_space=pl.ANY)] * 9,
        out_specs=pl.BlockSpec(memory_space=pltpu.VMEM),
        scratch_shapes=[
            pltpu.VMEM((slots, rows, width), jnp.bfloat16),
            pltpu.VMEM((2 * slots, block_rows, LANES), jnp.float32),
            pltpu.VMEM((DIM, rows, LANES), jnp.float32),
            pltpu.VMEM((DIM, rows, LANES), jnp.float32),
            pltpu.SemaphoreType.DMA((slots,)),
            pltpu.SemaphoreType.DMA((2 * slots,)),
        ],
        compiler_params=pltpu.CompilerParams(vmem_limit_bytes=VMEM_LIMIT),
        name="tile_parts",
    )(scalars, dissim, *sources)


def gather_body(count, block_rows, where, *refs):
    sources, out = refs[:-1], refs[-1]
    stress = sources[0][count * block_rows :, :]
    for s in range(1, len(sources)):
        stress = stress + sources[s][count * block_rows :, :]
    for chip in range(out.shape[0]):
        out[chip, :block_rows, :] = jnp.zeros((block_rows, LANES), jnp.float32)
        out[chip, block_rows:, :] = stress
    for s in range(len(sources)):
        for i in range(count):
            chip = where[s * count + i]

            @pl.when(chip >= 0)
            def _(s=s, i=i, chip=chip):
                out[chip, :block_rows, :] += sources[s][
                    i * block_rows : (i + 1) * block_rows, :
                ]


def by_chip(where, sources, chips):
    rows = sources[0].shape[0] - 8
    count = where.shape[0] // len(sources)
    block_rows = rows // count
    return pl.pallas_call(
        functools.partial(gather_body, count, block_rows),
        out_shape=jax.ShapeDtypeStruct((chips, block_rows + 8, LANES), jnp.float32),
        in_specs=[pl.BlockSpec(memory_space=pltpu.SMEM)]
        + [pl.BlockSpec(memory_space=pltpu.VMEM)] * len(sources),
        out_specs=pl.BlockSpec(memory_space=pltpu.VMEM),
        compiler_params=pltpu.CompilerParams(vmem_limit_bytes=VMEM_LIMIT),
        name="by_chip",
    )(where, *sources)


def total_body(width, pieces, out, stress):
    block_rows = pieces.shape[1] - 8
    chunks = width // LANES
    total = pieces[0]
    for i in range(1, pieces.shape[0]):
        total = total + pieces[i]
    for c in range(DIM):
        for j in range(chunks):
            r = c * chunks + j
            out[c : c + 1, j * LANES : (j + 1) * LANES] = total[r : r + 1, :] * (1.0 / width)
    stress[0, 0] = jnp.sum(total[block_rows:, :])


def total_of(pieces, width):
    return pl.pallas_call(
        functools.partial(total_body, width),
        out_shape=(
            jax.ShapeDtypeStruct((DIM, width), jnp.float32),
            jax.ShapeDtypeStruct((1, 1), jnp.float32),
        ),
        in_specs=[pl.BlockSpec(memory_space=pltpu.VMEM)],
        out_specs=(
            pl.BlockSpec(memory_space=pltpu.VMEM),
            pl.BlockSpec(memory_space=pltpu.SMEM),
        ),
        name="total",
    )(pieces)


def tables(tile_list, holder, groups, devs, slots):
    group, dev = lax.axis_index("grp"), lax.axis_index("dev")
    owners = tile_list[:, 2]
    indices = jnp.arange(owners.shape[0], dtype=jnp.int32)
    earlier = (owners[:, None] == owners[None, :]) & (indices[None, :] < indices[:, None])
    rank = jnp.sum(earlier.astype(jnp.int32), axis=1)
    blocks = jnp.arange(holder.shape[0], dtype=jnp.int32)
    position = jnp.sum(
        jnp.where(tile_list[:, :2, None] == blocks, holder, 0), axis=2
    )
    order = jnp.arange(2 * groups, dtype=jnp.int32)
    line = (group + order) % groups * devs + (dev ^ (order // groups))
    wanted = (line[:, None] * slots + jnp.arange(slots, dtype=jnp.int32)).reshape(-1)
    chosen = wanted[:, None] == (owners * slots + rank)[None, :]
    held = jnp.sum(jnp.where(chosen[:, :, None], position + 1, 0), axis=1).reshape(-1) - 1
    mine = held[: 2 * slots]
    present = (mine[::2] >= 0).astype(jnp.int32)
    at = jnp.maximum(mine, 0)
    source = (at // devs - group) % groups + groups * ((at % 2) ^ (dev % 2))
    for_tiles = jnp.concatenate([present, source, at % devs // 2])
    here = (held >= 0) & (held // devs == group) & (held % 2 == dev % 2)
    where = jnp.where(here, held % devs // 2, -1)
    return for_tiles, where


def on_device(tile_list, holder, coordinates, dissim):
    groups, devs = lax.axis_size("grp"), lax.axis_size("dev")
    chips = devs // 2
    width = coordinates.shape[1]
    slots = dissim.shape[0]
    block_rows = DIM * width // LANES
    plane = plane_groups(groups, devs)
    for_tiles, where = tables(tile_list, holder, groups, devs, slots)
    sent = jnp.broadcast_to(
        coordinates.reshape(1, block_rows, LANES), (chips, block_rows, LANES)
    )
    own = lax.all_to_all(sent, AXES, 0, 0, tiled=True, axis_index_groups=plane)
    parts = tile_parts(for_tiles, dissim, from_line(own, groups, devs))
    pieces = by_chip(where, from_line(parts, groups, devs), chips)
    pieces = lax.all_to_all(pieces, AXES, 0, 0, tiled=True, axis_index_groups=plane)
    guttman, stress = total_of(pieces, width)
    return guttman, stress[0, 0]


def solution(mesh):
    placed = (P(), P(), P(None, AXES), P(AXES, None, None))
    return jax.shard_map(
        on_device,
        mesh=mesh,
        in_specs=placed,
        out_specs=(P(None, AXES), P()),
        check_vma=False,
    )
```

time: 920 us -> 86.2 us (0.09)
  waiting for transfers between devices: 717 us -> 15 us
  blocking collectives: 69.8 us -> 13.5 us
  between operations: 41.2 us -> 0.75 us
  starting transfers between devices: 0.08 us -> 38.4 us
  local copies, waits for them, and re-layouts: 36.6 us -> 6.73 us
  matrix products: 29.1 us -> 0 us
  other arithmetic: 24.3 us -> 1.49 us
  Pallas kernels: 0 us -> 10 us
    unnamed x3 -> x0, waiting for transfers between devices: 673 us -> none
    psum x1 -> x0, blocking collectives: 69.8 us -> none  [on_device(): stress_sum = lax.psum(local_stress, ('grp', 'dev'))]
    all_gather x1 -> x0, waiting for transfers between devices: 44 us -> none  [on_device(): everything = lax.all_gather(coordinates, ('grp', 'dev'), axis=1, tiled=True)]
    ppermute x0 -> x14, starting transfers between devices: none -> 30.3 us  [the longest x6 28.6 us: from_line(): lax.ppermute(array, AXES, line_perm(groups, devs, d))]
    dot_general x8 -> x0, matrix products: 29.1 us -> none  [the longest x4 17.3 us: tile_terms(): lax.dot_general(col_coords, ratio, (((1,), (1,)), ((), ())), precision=la...]
    unnamed x4 -> x2, local copies, waits for them, and re-layouts: 31.9 us -> 3.38 us
    reduce_sum x4 -> x3, other arithmetic: 21.7 us -> 1.19 us  [the longest x1 0.9 us: tables(): jnp.sum(jnp.where(tile_list[:, :2, None] == blocks, holder, 0), axis=2)]
    all_to_all x0 -> x1, blocking collectives: none -> 13.5 us  [on_device(): lax.all_to_all(pieces, AXES, 0, 0, tiled=True, axis_index_groups=plane)]
  transfers between devices with their start and end apart: 2 -> 15, of which waited for: 2 -> 8; matrix products, arithmetic and copies ran while one was open for 1% -> 4% of each run, Pallas kernels for 0% -> 0%
where the time goes in v1:
time: 86.2 us; the launch traced here: 85.9 us
  starting transfers between devices  38.4 us (45%)
  waiting for transfers between devices  15 us (17%)
  blocking collectives  13.5 us (16%)
  Pallas kernels  10 us (12%)
  local copies, waits for them, and re-layouts  6.73 us (8%)
  other arithmetic  1.49 us (2%)
    ppermute x6, starting transfers between devices, from_line(): lax.ppermute(array, AXES, line_perm(groups, devs, d))  28.6 us
    all_to_all x1, blocking collectives, on_device(): lax.all_to_all(pieces, AXES, 0, 0, tiled=True, axis_index_groups=plane)  13.5 us
    all_to_all x1, starting transfers between devices, on_device(): own = lax.all_to_all(sent, AXES, 0, 0, tiled=True, axis_index_groups=plane)  8.13 us
    ppermute x6, waiting for transfers between devices, from_line(): lax.ppermute(array, AXES, line_perm(groups, devs, d))  7.94 us
    pallas_call x1, Pallas kernels, tile_parts(): pl.pallas_call(functools.partial(tile_body, rows, width), out_shape=jax.S...  7.36 us
    all_to_all x1, waiting for transfers between devices, on_device(): own = lax.all_to_all(sent, AXES, 0, 0, tiled=True, axis_index_groups=plane)  5.03 us
    unnamed x2, local copies, waits for them, and re-layouts  3.38 us
    ppermute x8, waiting for transfers between devices, from_line(): twin = [lax.ppermute(a, AXES, core_perm(groups * devs)) for a in own]  2.04 us
  transfers between devices with their start and end apart: 15, of which 8 were waited for; matrix products, arithmetic and copies ran while one was open for 4% of the time, Pallas kernels for 0%

profile of v1, /device:TPU:0, one launch (start us, length us, event | category | flops | bytes accessed | tf_op | source)
XLA Modules:
  0.0 85.9 jit_solution(16338570745493335481)
XLA Ops:
  0.6 0.7 broadcast_in_dim.46
  1.4 0.7 broadcast_in_dim.47
  2.0 8.1 %all-to-all-start = ((f32[16,24,128]{2,1,0:T(8,128)}), f32[16,24,128]{2,1,0:T(8,128)S(1)}, u32[]{:S(2)}, u32[]{:S(2)}) async-start(f32[16,24,128]{2,1,0:T(8,128)} %broadcast_in_dim.47), calls=%async_computation | async-start | bytes 393216 | tf_op jit(solution)/shard_map/all_to_all | solution.py:271
  10.2 0.7 slice.15
  10.9 0.7 slice.16
  11.6 0.2 convert_reduce_fusion
  11.8 0.9 %select_reduce_fusion = s32[256,2]{0,1:T(2,128)S(1)} fusion(s32[128]{0:T(128)} %param.5, s32[256,2]{0,1:T(2,128)S(1)} %slice.16), kind=kLoop, calls=%fused_computation | loop fusion | flops 196096 | bytes 4608 | tf_op jit(solution)/shard_map/reduce_sum | solution.py:242
  12.7 0.1 iota_add_fusion
  12.8 0.1 add.108
  12.8 0.1 broadcast_compare_fusion
  12.9 0.1 select_reduce_fusion.1
  13.1 0.1 copy.9
  13.1 0.1 slice.18
  13.2 0.1 slice.19
  13.3 5.0 %all-to-all-done.refs_0_ = f32[16,24,128]{2,1,0:T(8,128)S(1)} async-done(((f32[16,24,128]{2,1,0:T(8,128)}), f32[16,24,128]{2,1,0:T(8,128)S(1)}, u32[]{:S(2)}, u32[]{:S(2)}) %all-to-all-start) | async-done | bytes 196640 | tf_op jit(solution)/shard_map/all_to_all | solution.py:271
  18.4 1.5 %collective-permute-start.2 = (f32[16,24,128]{2,1,0:T(8,128)S(1)}, f32[16,24,128]{2,1,0:T(8,128)S(1)}, u32[]{:S(2)}, u32[]{:S(2)}) collective-permute-start(f32[16,24,128]{2,1,0:T(8,128)S(1)} %all-to-all-done.refs_0_), channel_id=1, source_target_pairs={{96,0},{97,1},{98,2},{99,3},{100,4},{101,5},{102,6},{103,7},{104,8... | collective-permute-start | bytes 589832 | tf_op jit(solution)/shard_map/ppermute | solution.py:39
  19.9 2.7 %collective-permute-start.1 = (f32[16,24,128]{2,1,0:T(8,128)S(1)}, f32[16,24,128]{2,1,0:T(8,128)S(1)}, u32[]{:S(2)}, u32[]{:S(2)}) collective-permute-start(f32[16,24,128]{2,1,0:T(8,128)S(1)} %all-to-all-done.refs_0_), channel_id=1, source_target_pairs={{64,0},{65,1},{66,2},{67,3},{68,4},{69,5},{70,6},{71,7},{72,8},{73... | collective-permute-start | bytes 589832 | tf_op jit(solution)/shard_map/ppermute | solution.py:39
  22.6 1.4 %collective-permute-start = (f32[16,24,128]{2,1,0:T(8,128)S(1)}, f32[16,24,128]{2,1,0:T(8,128)S(1)}, u32[]{:S(2)}, u32[]{:S(2)}) collective-permute-start(f32[16,24,128]{2,1,0:T(8,128)S(1)} %all-to-all-done.refs_0_), channel_id=1, source_target_pairs={{32,0},{33,1},{34,2},{35,3},{36,4},{37,5},{38,6},{39,7},{40,8},{41... | collective-permute-start | bytes 589832 | tf_op jit(solution)/shard_map/ppermute | solution.py:39
  24.0 0.1 collective-permute-start.3
  24.1 3.0 %collective-permute-done.2.refs_3_ = f32[16,24,128]{2,1,0:T(8,128)S(1)} collective-permute-done((f32[16,24,128]{2,1,0:T(8,128)S(1)}, f32[16,24,128]{2,1,0:T(8,128)S(1)}, u32[]{:S(2)}, u32[]{:S(2)}) %collective-permute-start.2) | collective-permute-done | bytes 196640 | tf_op jit(solution)/shard_map/ppermute | solution.py:39
  27.1 0.0 collective-permute-start.6
  27.1 3.0 %collective-permute-done.1.refs_2_ = f32[16,24,128]{2,1,0:T(8,128)S(1)} collective-permute-done((f32[16,24,128]{2,1,0:T(8,128)S(1)}, f32[16,24,128]{2,1,0:T(8,128)S(1)}, u32[]{:S(2)}, u32[]{:S(2)}) %collective-permute-start.1) | collective-permute-done | bytes 196640 | tf_op jit(solution)/shard_map/ppermute | solution.py:39
  30.1 0.0 collective-permute-start.5
  30.1 0.0 collective-permute-done.refs_1_
  30.1 0.5 collective-permute-start.4
  30.6 0.1 pad_add_fusion.sc
  30.7 0.0 collective-permute-done.3.refs_4_
  30.7 0.0 collective-permute-done.6.refs_7_
  30.7 0.8 collective-permute-done.5.refs_6_
  31.5 0.3 collective-permute-done.4.refs_5_
  31.8 3.4 %copy-done = bf16[4,1024,1024]{2,1,0:T(8,128)(2,1)S(1)} copy-done((bf16[4,1024,1024]{2,1,0:T(8,128)(2,1)S(1)}, bf16[4,1024,1024]{2,1,0:T(8,128)(2,1)}, u32[]{:S(2)}) %copy-start) | copy-done | bytes 8388632
  35.2 7.4 %tile_parts.1.refs_0_ = f32[200,128]{1,0:T(8,128)S(1)} custom-call(s32[20]{0:T(128)S(1)} %pad_add_fusion.sc, bf16[4,1024,1024]{2,1,0:T(8,128)(2,1)S(1)} %copy-done, f32[16,24,128]{2,1,0:T(8,128)S(1)} %all-to-all-done.refs_0_, f32[16,24,128]{2,1,0:T(8,128)S(1)} %collective-permute-done.refs_1_, f32[16,24,128]{2,1,0:T(8,128)S(1)} %collective-permute-done.1.refs_2_, ...), custom_call_target="tpu_custom_call" | custom-call | tf_op jit(solution)/shard_map/tile_parts/pallas_call | solution.py:153
  42.6 1.1 %collective-permute-start.9 = (f32[200,128]{1,0:T(8,128)S(1)}, f32[200,128]{1,0:T(8,128)S(1)}, u32[]{:S(2)}, u32[]{:S(2)}) collective-permute-start(f32[200,128]{1,0:T(8,128)S(1)} %tile_parts.1.refs_0_), channel_id=1, source_target_pairs={{96,0},{97,1},{98,2},{99,3},{100,4},{101,5},{102,6},{103,7},{104,8... | collective-permute-start | bytes 307208 | tf_op jit(solution)/shard_map/ppermute | solution.py:39
  43.7 19.3 %collective-permute-start.8 = (f32[200,128]{1,0:T(8,128)S(1)}, f32[200,128]{1,0:T(8,128)S(1)}, u32[]{:S(2)}, u32[]{:S(2)}) collective-permute-start(f32[200,128]{1,0:T(8,128)S(1)} %tile_parts.1.refs_0_), channel_id=1, source_target_pairs={{64,0},{65,1},{66,2},{67,3},{68,4},{69,5},{70,6},{71,7},{72,8},{73... | collective-permute-start | bytes 307208 | tf_op jit(solution)/shard_map/ppermute | solution.py:39
  63.0 2.5 %collective-permute-start.7 = (f32[200,128]{1,0:T(8,128)S(1)}, f32[200,128]{1,0:T(8,128)S(1)}, u32[]{:S(2)}, u32[]{:S(2)}) collective-permute-start(f32[200,128]{1,0:T(8,128)S(1)} %tile_parts.1.refs_0_), channel_id=1, source_target_pairs={{32,0},{33,1},{34,2},{35,3},{36,4},{37,5},{38,6},{39,7},{40,8},{41... | collective-permute-start | bytes 307208 | tf_op jit(solution)/shard_map/ppermute | solution.py:39
  65.5 0.1 copy.8
  65.6 0.1 sub.32
  65.7 0.1 collective-permute-start.10
  65.8 0.5 collective-permute-start.13
  66.3 2.0 %collective-permute-done.8.refs_2_ = f32[200,128]{1,0:T(8,128)S(1)} collective-permute-done((f32[200,128]{1,0:T(8,128)S(1)}, f32[200,128]{1,0:T(8,128)S(1)}, u32[]{:S(2)}, u32[]{:S(2)}) %collective-permute-start.8) | collective-permute-done | bytes 102432 | tf_op jit(solution)/shard_map/ppermute | solution.py:39
  68.3 0.5 collective-permute-start.11
  68.8 0.0 collective-permute-done.10.refs_4_
  68.8 0.0 collective-permute-done.13.refs_7_
  68.8 0.8 collective-permute-done.12.refs_6_
  69.6 0.2 collective-permute-done.11.refs_5_
  69.7 1.1 %by_chip.1 = f32[16,32,128]{2,1,0:T(8,128)S(1)} custom-call(s32[64]{0:T(128)S(1)} %and_select_fusion.7.where, f32[200,128]{1,0:T(8,128)S(1)} %tile_parts.1.refs_0_, f32[200,128]{1,0:T(8,128)S(1)} %collective-permute-done.7.refs_1_, f32[200,128]{1,0:T(8,128)S(1)} %collective-permute-done.8.refs_2_, f32[200,128]{1,0:T(8,128)S(1)} %collective-permute-done.9.refs_3_, ...), custom_call_target="tpu_custom_call" | custom-call | tf_op jit(solution)/shard_map/by_chip/pallas_call | solution.py:195
  70.8 13.5 %all_to_all.10.pieces = f32[16,32,128]{2,1,0:T(8,128)} all-to-all(f32[16,32,128]{2,1,0:T(8,128)S(1)} %by_chip.1), channel_id=1, replica_groups={{0,2,4,6,8,10,12,14,16,18,20,22,24,26,28,30},{1,3,5,7,9,11,13,15,17,19,..., dimensions={0} | all-to-all | bytes 524288 | tf_op jit(solution)/shard_map/all_to_all | solution.py:274
  84.3 1.6 %total.1 = (f32[3,1024]{1,0:T(4,128)}, f32[1,1]{1,0:T(1,128)}) custom-call(f32[16,32,128]{2,1,0:T(8,128)} %all_to_all.10.pieces), custom_call_target="tpu_custom_call" | custom-call | tf_op jit(solution)/shard_map/total/pallas_call | solution.py:220
  (11 shorter events, 0.1 us)
Async XLA Ops:
  2.0 16.3 %all-to-all-start = ((f32[16,24,128]{2,1,0:T(8,128)}), f32[16,24,128]{2,1,0:T(8,128)S(1)}, u32[]{:S(2)}, u32[]{:S(2)}) async-start(f32[16,24,128]{2,1,0:T(8,128)} %broadcast_in_dim.47), calls=%async_computation | async-start | bytes 393216 | tf_op jit(solution)/shard_map/all_to_all | solution.py:271
  18.4 8.7 %collective-permute-start.2 = (f32[16,24,128]{2,1,0:T(8,128)S(1)}, f32[16,24,128]{2,1,0:T(8,128)S(1)}, u32[]{:S(2)}, u32[]{:S(2)}) collective-permute-start(f32[16,24,128]{2,1,0:T(8,128)S(1)} %all-to-all-done.refs_0_), channel_id=1, source_target_pairs={{96,0},{97,1},{98,2},{99,3},{100,4},{101,5},{102,6},{103,7},{104,8... | collective-permute-start | bytes 589832 | tf_op jit(solution)/shard_map/ppermute | solution.py:39
  19.9 10.3 %collective-permute-start.1 = (f32[16,24,128]{2,1,0:T(8,128)S(1)}, f32[16,24,128]{2,1,0:T(8,128)S(1)}, u32[]{:S(2)}, u32[]{:S(2)}) collective-permute-start(f32[16,24,128]{2,1,0:T(8,128)S(1)} %all-to-all-done.refs_0_), channel_id=1, source_target_pairs={{64,0},{65,1},{66,2},{67,3},{68,4},{69,5},{70,6},{71,7},{72,8},{73... | collective-permute-start | bytes 589832 | tf_op jit(solution)/shard_map/ppermute | solution.py:39
  22.6 7.5 %collective-permute-start = (f32[16,24,128]{2,1,0:T(8,128)S(1)}, f32[16,24,128]{2,1,0:T(8,128)S(1)}, u32[]{:S(2)}, u32[]{:S(2)}) collective-permute-start(f32[16,24,128]{2,1,0:T(8,128)S(1)} %all-to-all-done.refs_0_), channel_id=1, source_target_pairs={{32,0},{33,1},{34,2},{35,3},{36,4},{37,5},{38,6},{39,7},{40,8},{41... | collective-permute-start | bytes 589832 | tf_op jit(solution)/shard_map/ppermute | solution.py:39
  24.0 6.7 %collective-permute-start.3 = (f32[16,24,128]{2,1,0:T(8,128)S(1)}, f32[16,24,128]{2,1,0:T(8,128)S(1)}, u32[]{:S(2)}, u32[]{:S(2)}) collective-permute-start(f32[16,24,128]{2,1,0:T(8,128)S(1)} %all-to-all-done.refs_0_), channel_id=1, source_target_pairs={{0,1},{1,0},{2,3},{3,2},{4,5},{5,4},{6,7},{7,6},{8,9},{9,8},{10,11... | collective-permute-start | bytes 589832 | tf_op jit(solution)/shard_map/ppermute | solution.py:41
  27.1 3.6 %collective-permute-start.6 = (f32[16,24,128]{2,1,0:T(8,128)S(1)}, f32[16,24,128]{2,1,0:T(8,128)S(1)}, u32[]{:S(2)}, u32[]{:S(2)}) collective-permute-start(f32[16,24,128]{2,1,0:T(8,128)S(1)} %collective-permute-done.2.refs_3_), channel_id=1, source_target_pairs={{0,1},{1,0},{2,3},{3,2},{4,5},{5,4},{6,7},{7,6},{8,9},{9,8},{10,11... | collective-permute-start | bytes 589832 | tf_op jit(solution)/shard_map/ppermute | solution.py:41
  30.1 1.4 %collective-permute-start.5 = (f32[16,24,128]{2,1,0:T(8,128)S(1)}, f32[16,24,128]{2,1,0:T(8,128)S(1)}, u32[]{:S(2)}, u32[]{:S(2)}) collective-permute-start(f32[16,24,128]{2,1,0:T(8,128)S(1)} %collective-permute-done.1.refs_2_), channel_id=1, source_target_pairs={{0,1},{1,0},{2,3},{3,2},{4,5},{5,4},{6,7},{7,6},{8,9},{9,8},{10,11... | collective-permute-start | bytes 589832 | tf_op jit(solution)/shard_map/ppermute | solution.py:41
  30.1 1.7 %collective-permute-start.4 = (f32[16,24,128]{2,1,0:T(8,128)S(1)}, f32[16,24,128]{2,1,0:T(8,128)S(1)}, u32[]{:S(2)}, u32[]{:S(2)}) collective-permute-start(f32[16,24,128]{2,1,0:T(8,128)S(1)} %collective-permute-done.refs_1_), channel_id=1, source_target_pairs={{0,1},{1,0},{2,3},{3,2},{4,5},{5,4},{6,7},{7,6},{8,9},{9,8},{10,11... | collective-permute-start | bytes 589832 | tf_op jit(solution)/shard_map/ppermute | solution.py:41
  31.8 3.4 %copy-start = (bf16[4,1024,1024]{2,1,0:T(8,128)(2,1)S(1)}, bf16[4,1024,1024]{2,1,0:T(8,128)(2,1)}, u32[]{:S(2)}) copy-start(bf16[4,1024,1024]{2,1,0:T(8,128)(2,1)} %delta_hbm.1) | copy-start | bytes 25165828
  42.6 23.2 %collective-permute-start.9 = (f32[200,128]{1,0:T(8,128)S(1)}, f32[200,128]{1,0:T(8,128)S(1)}, u32[]{:S(2)}, u32[]{:S(2)}) collective-permute-start(f32[200,128]{1,0:T(8,128)S(1)} %tile_parts.1.refs_0_), channel_id=1, source_target_pairs={{96,0},{97,1},{98,2},{99,3},{100,4},{101,5},{102,6},{103,7},{104,8... | collective-permute-start | bytes 307208 | tf_op jit(solution)/shard_map/ppermute | solution.py:39
  43.7 24.6 %collective-permute-start.8 = (f32[200,128]{1,0:T(8,128)S(1)}, f32[200,128]{1,0:T(8,128)S(1)}, u32[]{:S(2)}, u32[]{:S(2)}) collective-permute-start(f32[200,128]{1,0:T(8,128)S(1)} %tile_parts.1.refs_0_), channel_id=1, source_target_pairs={{64,0},{65,1},{66,2},{67,3},{68,4},{69,5},{70,6},{71,7},{72,8},{73... | collective-permute-start | bytes 307208 | tf_op jit(solution)/shard_map/ppermute | solution.py:39
  63.0 5.3 %collective-permute-start.7 = (f32[200,128]{1,0:T(8,128)S(1)}, f32[200,128]{1,0:T(8,128)S(1)}, u32[]{:S(2)}, u32[]{:S(2)}) collective-permute-start(f32[200,128]{1,0:T(8,128)S(1)} %tile_parts.1.refs_0_), channel_id=1, source_target_pairs={{32,0},{33,1},{34,2},{35,3},{36,4},{37,5},{38,6},{39,7},{40,8},{41... | collective-permute-start | bytes 307208 | tf_op jit(solution)/shard_map/ppermute | solution.py:39
  65.7 3.1 %collective-permute-start.10 = (f32[200,128]{1,0:T(8,128)S(1)}, f32[200,128]{1,0:T(8,128)S(1)}, u32[]{:S(2)}, u32[]{:S(2)}) collective-permute-start(f32[200,128]{1,0:T(8,128)S(1)} %tile_parts.1.refs_0_), channel_id=1, source_target_pairs={{0,1},{1,0},{2,3},{3,2},{4,5},{5,4},{6,7},{7,6},{8,9},{9,8},{10,11... | collective-permute-start | bytes 307208 | tf_op jit(solution)/shard_map/ppermute | solution.py:41
  65.8 3.0 %collective-permute-start.13 = (f32[200,128]{1,0:T(8,128)S(1)}, f32[200,128]{1,0:T(8,128)S(1)}, u32[]{:S(2)}, u32[]{:S(2)}) collective-permute-start(f32[200,128]{1,0:T(8,128)S(1)} %collective-permute-done.9.refs_3_), channel_id=1, source_target_pairs={{0,1},{1,0},{2,3},{3,2},{4,5},{5,4},{6,7},{7,6},{8,9},{9,8},{10,11... | collective-permute-start | bytes 307208 | tf_op jit(solution)/shard_map/ppermute | solution.py:41
  68.3 1.3 %collective-permute-start.12 = (f32[200,128]{1,0:T(8,128)S(1)}, f32[200,128]{1,0:T(8,128)S(1)}, u32[]{:S(2)}, u32[]{:S(2)}) collective-permute-start(f32[200,128]{1,0:T(8,128)S(1)} %collective-permute-done.8.refs_2_), channel_id=1, source_target_pairs={{0,1},{1,0},{2,3},{3,2},{4,5},{5,4},{6,7},{7,6},{8,9},{9,8},{10,11... | collective-permute-start | bytes 307208 | tf_op jit(solution)/shard_map/ppermute | solution.py:41
  68.3 1.5 %collective-permute-start.11 = (f32[200,128]{1,0:T(8,128)S(1)}, f32[200,128]{1,0:T(8,128)S(1)}, u32[]{:S(2)}, u32[]{:S(2)}) collective-permute-start(f32[200,128]{1,0:T(8,128)S(1)} %collective-permute-done.7.refs_1_), channel_id=1, source_target_pairs={{0,1},{1,0},{2,3},{3,2},{4,5},{5,4},{6,7},{7,6},{8,9},{9,8},{10,11... | collective-permute-start | bytes 307208 | tf_op jit(solution)/shard_map/ppermute | solution.py:41

commit v2 on v1

v2 whole, which is shorter than its diff:
```python
import functools

import jax
import jax.numpy as jnp
from jax import lax
from jax.experimental import pallas as pl
from jax.experimental.pallas import tpu as pltpu
from jax.sharding import PartitionSpec as P

AXES = ("grp", "dev")
FLOOR_SQUARED = 0.0625
LANES = 128
DIM = 3
VMEM_LIMIT = 32 * 1024 * 1024
KDIM = 128
STEP = 128
FETCH = 1024
DEPTH = 512
AHEAD = 1
LAG = 1


def line_perm(groups, devs, shift):
    return [
        (((g + shift) % groups) * devs + d, g * devs + d)
        for g in range(groups)
        for d in range(devs)
    ]


def core_perm(devices):
    return [(i, i ^ 1) for i in range(devices)]


def core_groups(groups, devs, planes):
    blocks = [range(g * devs, (g + 1) * devs) for g in range(groups)]
    if not planes:
        blocks = [range(groups * devs)]
    return [[d for d in b if d % 2 == core] for b in blocks for core in range(2)]


def to_twin(array, devices):
    return lax.ppermute(array, AXES, core_perm(devices))


def from_line(array, groups, devs):
    own = [array] + [
        lax.ppermute(array, AXES, line_perm(groups, devs, d)) for d in range(1, groups)
    ]
    return own + [to_twin(a, groups * devs) for a in own]


def split3(x):
    high = x.astype(jnp.bfloat16)
    rest = x - high.astype(jnp.float32)
    middle = rest.astype(jnp.bfloat16)
    low = (rest - middle.astype(jnp.float32)).astype(jnp.bfloat16)
    return high, middle, low


def tile_body(rows, width, sc, delta, *refs):
    sources = refs[:2]
    parts, blocks, near, far, left, right, block_sem = refs[2:]
    slots = delta.shape[0]
    chunks = width // LANES
    f32, bf16 = jnp.float32, jnp.bfloat16

    def block_copy(s, i, at):
        return pltpu.make_async_copy(sources[s].at[at], blocks.at[i], block_sem.at[i])

    for i in range(2 * slots):
        for s in range(2):
            pl.when(sc[slots + i] == s)(
                lambda i=i, s=s: block_copy(s, i, sc[3 * slots + i]).start()
            )

    for i in range(2 * slots):
        block_copy(0, i, 0).wait()

    parts[2 * slots * DIM * chunks :, :] = jnp.zeros((8, LANES), f32)

    def one_tile(k, _):
        @pl.when(sc[k] > 0)
        def _():
            def spread(i):
                return [blocks[i, c * chunks : (c + 1) * chunks, :] for c in range(DIM)]

            xa, xb = spread(2 * k), spread(2 * k + 1)
            mean = [jnp.sum(a, keepdims=True) * (1.0 / width) for a in xa]
            xa = [a - m for a, m in zip(xa, mean)]
            xb = [b - m for b, m in zip(xb, mean)]

            def fill(ref, x, scale, norm_first):
                pieces = [split3(v) for v in x]
                norm = x[0] * x[0] + x[1] * x[1] + x[2] * x[2]
                norms = split3(norm)
                one = jnp.ones((chunks, LANES), bf16)
                out = []
                for c in range(DIM):
                    for s in range(3):
                        for t in range(3):
                            out.append(pieces[c][s] * scale if norm_first else pieces[c][t])
                for s in range(3):
                    out.append(norms[s] if norm_first else one)
                for s in range(3):
                    out.append(one if norm_first else norms[s])
                return out

            la = fill(None, xa, -2.0, True)
            lb = fill(None, xb, 1.0, False)
            one = jnp.ones((chunks, LANES), bf16)
            va = [p for v in xa for p in split3(v)] + [one]
            vb = [p for v in xb for p in split3(v)] + [one]
            for ref, rows_ in ((left, la), (right, lb), (near, va), (far, vb)):
                ref[...] = jnp.zeros(ref.shape, f32)
                for n, v in enumerate(rows_):
                    v = v.astype(f32)
                    for j in range(chunks):
                        ref[n : n + 1, j * LANES : (j + 1) * LANES] = v[j : j + 1, :]
            cols = right[...].astype(bf16)
            weights = far[...].astype(bf16)

            lhs = jnp.transpose(left[...]).astype(bf16)
            mine = near[...].astype(bf16)
            count = rows // STEP
            pieces = width // DEPTH
            stress = jnp.zeros((16, LANES), f32)
            row, col = [None] * count, [None] * pieces

            def front(n, g):
                lanes = slice(g * DEPTH, (g + 1) * DEPTH)
                return lax.dot_general(
                    lhs[n * STEP : (n + 1) * STEP], cols[:, lanes], (((1,), (0,)), ((), ())), preferred_element_type=f32
                )

            def back(n, g, squared, stress):
                lanes = slice(g * DEPTH, (g + 1) * DEPTH)
                own = mine[:, n * STEP : (n + 1) * STEP]
                own = jnp.concatenate([own, own], axis=1)
                target = delta[k, n * STEP : (n + 1) * STEP, lanes].astype(f32)
                squared = jnp.maximum(squared, FLOOR_SQUARED)
                inverse = lax.rsqrt(squared)
                error = target - squared * inverse
                error = error * error
                for a in range(0, STEP, 16):
                    for b in range(0, DEPTH, LANES):
                        stress = stress + error[a : a + 16, b : b + LANES]
                ratio = target * inverse
                high = ratio.astype(bf16)
                low = (ratio - high.astype(f32)).astype(bf16)
                both = jnp.concatenate([high, low], axis=0)
                return stress, both

            def last(n, g, both):
                lanes = slice(g * DEPTH, (g + 1) * DEPTH)
                own = mine[:, n * STEP : (n + 1) * STEP]
                own = jnp.concatenate([own, own], axis=1)
                a = lax.dot_general(
                    weights[:, lanes], both, (((1,), (1,)), ((), ())), preferred_element_type=f32
                )
                row[n] = a if row[n] is None else row[n] + a
                a = lax.dot_general(own, both, (((1,), (0,)), ((), ())), preferred_element_type=f32)
                col[g] = a if col[g] is None else col[g] + a

            order = [(n, g) for n in range(count) for g in range(pieces)]
            ahead = [front(*order[t]) for t in range(AHEAD)]
            held = []
            for t, (n, g) in enumerate(order):
                if t + AHEAD < len(order):
                    ahead.append(front(*order[t + AHEAD]))
                if len(held) > LAG - 1:
                    last(*held.pop(0))
                stress, both = back(n, g, ahead.pop(0), stress)
                held.append((n, g, both))
            for h in held:
                last(*h)
            row = jnp.concatenate([r[:, :STEP] + r[:, STEP:] for r in row], axis=1)
            col = jnp.concatenate(col, axis=1)
            for side, own, total in ((0, near, row), (1, far, col)):
                for c in range(DIM):
                    cross = total[3 * c : 3 * c + 1] + total[3 * c + 1 : 3 * c + 2] + total[3 * c + 2 : 3 * c + 3]
                    x = own[3 * c : 3 * c + 1, :] + own[3 * c + 1 : 3 * c + 2, :] + own[3 * c + 2 : 3 * c + 3, :]
                    value = x * total[9:10] - cross
                    for j in range(chunks):
                        parts[pl.ds((2 * k + side) * DIM * chunks + c * chunks + j, 1), :] = value[:, j * LANES : (j + 1) * LANES]
            parts[2 * slots * DIM * chunks :, :] += stress[:8] + stress[8:]

        return 0

    lax.fori_loop(0, slots, one_tile, 0)


def fetch_body(source, out, sem):
    copy = pltpu.make_async_copy(source, out, sem)
    copy.start()
    copy.wait()


def fetch(dissim):
    return pl.pallas_call(
        fetch_body,
        out_shape=pltpu.VMEM(dissim.shape, dissim.dtype),
        in_specs=[pl.BlockSpec(memory_space=pl.ANY)],
        out_specs=pl.BlockSpec(memory_space=pltpu.VMEM),
        scratch_shapes=[pltpu.SemaphoreType.DMA],
        cost_estimate=pl.CostEstimate(
            flops=0, bytes_accessed=2 * dissim.size * dissim.dtype.itemsize, transcendentals=0
        ),
        compiler_params=pltpu.CompilerParams(vmem_limit_bytes=8 * 1024 * 1024),
        name="fetch",
    )(dissim)


def tile_parts(scalars, dissim, sources):
    slots, rows, width = dissim.shape
    block_rows = DIM * width // LANES
    return pl.pallas_call(
        functools.partial(tile_body, rows, width),
        out_shape=jax.ShapeDtypeStruct((2 * slots * block_rows + 8, LANES), jnp.float32),
        in_specs=[pl.BlockSpec(memory_space=pltpu.SMEM), pl.BlockSpec(memory_space=pltpu.VMEM)]
        + [pl.BlockSpec(memory_space=pl.ANY)] * 2,
        out_specs=pl.BlockSpec(memory_space=pltpu.VMEM),
        scratch_shapes=[
            pltpu.VMEM((2 * slots, block_rows, LANES), jnp.float32),
            pltpu.VMEM((16, rows), jnp.float32),
            pltpu.VMEM((16, width), jnp.float32),
            pltpu.VMEM((KDIM, rows), jnp.float32),
            pltpu.VMEM((KDIM, width), jnp.float32),
            pltpu.SemaphoreType.DMA((2 * slots,)),
        ],
        compiler_params=pltpu.CompilerParams(vmem_limit_bytes=VMEM_LIMIT),
        name="tile_parts",
    )(scalars, pltpu.with_memory_space_constraint(dissim, pltpu.VMEM), *sources)


def gather_body(count, block_rows, where, *refs):
    sources, out = refs[:-1], refs[-1]
    stress = sources[0][count * block_rows :, :]
    for s in range(1, len(sources)):
        stress = stress + sources[s][count * block_rows :, :]
    for chip in range(out.shape[0]):
        out[chip, :block_rows, :] = jnp.zeros((block_rows, LANES), jnp.float32)
        out[chip, block_rows:, :] = stress
    for s in range(len(sources)):
        for i in range(count):
            chip = where[s * count + i]

            @pl.when(chip >= 0)
            def _(s=s, i=i, chip=chip):
                out[chip, :block_rows, :] += sources[s][
                    i * block_rows : (i + 1) * block_rows, :
                ]


def by_chip(where, sources, chips):
    rows = sources[0].shape[0] - 8
    count = where.shape[0] // len(sources)
    block_rows = rows // count
    return pl.pallas_call(
        functools.partial(gather_body, count, block_rows),
        out_shape=jax.ShapeDtypeStruct((chips, block_rows + 8, LANES), jnp.float32),
        in_specs=[pl.BlockSpec(memory_space=pltpu.SMEM)]
        + [pl.BlockSpec(memory_space=pltpu.VMEM)] * len(sources),
        out_specs=pl.BlockSpec(memory_space=pltpu.VMEM),
        compiler_params=pltpu.CompilerParams(vmem_limit_bytes=VMEM_LIMIT),
        name="by_chip",
    )(where, *sources)


def total_body(width, pieces, out, stress):
    block_rows = pieces.shape[1] - 8
    chunks = width // LANES
    total = pieces[0]
    for i in range(1, pieces.shape[0]):
        total = total + pieces[i]
    for c in range(DIM):
        for j in range(chunks):
            r = c * chunks + j
            out[c : c + 1, j * LANES : (j + 1) * LANES] = total[r : r + 1, :] * (1.0 / width)
    stress[0, 0] = jnp.sum(total[block_rows:, :])


def total_of(pieces, width):
    return pl.pallas_call(
        functools.partial(total_body, width),
        out_shape=(
            jax.ShapeDtypeStruct((DIM, width), jnp.float32),
            jax.ShapeDtypeStruct((1, 1), jnp.float32),
        ),
        in_specs=[pl.BlockSpec(memory_space=pltpu.VMEM)],
        out_specs=(
            pl.BlockSpec(memory_space=pltpu.VMEM),
            pl.BlockSpec(memory_space=pltpu.SMEM),
        ),
        name="total",
    )(pieces)


def tables(tile_list, holder, groups, devs, slots):
    group, dev = lax.axis_index("grp"), lax.axis_index("dev")
    owners = tile_list[:, 2]
    indices = jnp.arange(owners.shape[0], dtype=jnp.int32)
    earlier = (owners[:, None] == owners[None, :]) & (indices[None, :] < indices[:, None])
    rank = jnp.sum(earlier.astype(jnp.int32), axis=1)
    blocks = jnp.arange(holder.shape[0], dtype=jnp.int32)
    position = jnp.sum(
        jnp.where(tile_list[:, :2, None] == blocks, holder, 0), axis=2
    )
    order = jnp.arange(2 * groups, dtype=jnp.int32)
    line = (group + order) % groups * devs + (dev ^ (order // groups))
    wanted = (line[:, None] * slots + jnp.arange(slots, dtype=jnp.int32)).reshape(-1)
    chosen = wanted[:, None] == (owners * slots + rank)[None, :]
    held = jnp.sum(jnp.where(chosen[:, :, None], position + 1, 0), axis=1).reshape(-1) - 1
    mine = held[: 2 * slots]
    present = (mine[::2] >= 0).astype(jnp.int32)
    at = jnp.maximum(mine, 0)
    for_tiles = jnp.concatenate([present, at % 2 ^ dev % 2, at // 2])
    here = (held >= 0) & (held // devs == group) & (held % 2 == dev % 2)
    where = jnp.where(here, held % devs // 2, -1)
    return for_tiles, where


def on_device(tile_list, holder, coordinates, dissim):
    groups, devs = lax.axis_size("grp"), lax.axis_size("dev")
    chips = devs // 2
    width = coordinates.shape[1]
    slots = dissim.shape[0]
    block_rows = DIM * width // LANES
    for_tiles, where = tables(tile_list, holder, groups, devs, slots)
    delta = fetch(dissim)
    sent = jnp.broadcast_to(
        coordinates.reshape(1, block_rows, LANES), (groups * chips, block_rows, LANES)
    )
    own = lax.all_to_all(
        sent, AXES, 0, 0, tiled=True, axis_index_groups=core_groups(groups, devs, False)
    )
    parts = tile_parts(for_tiles, delta, [own, to_twin(own, groups * devs)])
    pieces = by_chip(where, from_line(parts, groups, devs), chips)
    pieces = lax.all_to_all(
        pieces, AXES, 0, 0, tiled=True, axis_index_groups=core_groups(groups, devs, True)
    )
    guttman, stress = total_of(pieces, width)
    return guttman, stress[0, 0]


def solution(mesh):
    placed = (P(), P(), P(None, AXES), P(AXES, None, None))
    return jax.shard_map(
        on_device,
        mesh=mesh,
        in_specs=placed,
        out_specs=(P(None, AXES), P()),
        check_vma=False,
    )
```

time: 86.2 us -> 78.4 us (0.910)
  starting transfers between devices: 38.4 us -> 28.4 us
  local copies, waits for them, and re-layouts: 6.73 us -> 13.6 us
  Pallas kernels: 10 us -> 7.27 us
  blocking collectives: 13.5 us -> 12.6 us
    ppermute x6 -> x3, starting transfers between devices: 28.6 us -> 12.5 us  [from_line(): lax.ppermute(array, AXES, line_perm(groups, devs, d))]
    all_to_all x1, waiting for transfers between devices: 5.03 us -> 13.1 us  [on_device(): lax.all_to_all(sent, AXES, 0, 0, tiled=True, axis_index_groups=core_group...]
    ppermute x6 -> x3, waiting for transfers between devices: 7.94 us -> 0.15 us  [from_line(): lax.ppermute(array, AXES, line_perm(groups, devs, d))]
    unnamed x2 -> x6, local copies, waits for them, and re-layouts: 3.38 us -> 9.99 us
    all_to_all x1, starting transfers between devices: 8.13 us -> 11.5 us  [on_device(): lax.all_to_all(sent, AXES, 0, 0, tiled=True, axis_index_groups=core_group...]
    pallas_call x1, Pallas kernels: 7.36 us -> 4.01 us  [tile_parts(): pl.pallas_call(functools.partial(tile_body, rows, width), out_shape=jax.S...]
    ppermute x8 -> x5, starting transfers between devices: 1.68 us -> 4.37 us  [to_twin(): return lax.ppermute(array, AXES, core_perm(devices))]
    ppermute x8 -> x5, waiting for transfers between devices: 2.04 us -> 0.92 us  [to_twin(): return lax.ppermute(array, AXES, core_perm(devices))]
  transfers between devices with their start and end apart: 15 -> 9, of which waited for: 8 -> 5; matrix products, arithmetic and copies ran while one was open for 4% -> 4% of each run, Pallas kernels for 0% -> 1%
where the time goes in v2:
time: 78.4 us; the launch traced here: 78.2 us
  starting transfers between devices  28.4 us (36%)
  waiting for transfers between devices  14.2 us (18%)
  local copies, waits for them, and re-layouts  13.6 us (17%)
  blocking collectives  12.6 us (16%)
  Pallas kernels  7.27 us (9%)
  other arithmetic  1.48 us (2%)
    all_to_all x1, waiting for transfers between devices, on_device(): lax.all_to_all(sent, AXES, 0, 0, tiled=True, axis_index_groups=core_group...  13.1 us
    all_to_all x1, blocking collectives, on_device(): lax.all_to_all(pieces, AXES, 0, 0, tiled=True, axis_index_groups=core_gro...  12.6 us
    ppermute x3, starting transfers between devices, from_line(): lax.ppermute(array, AXES, line_perm(groups, devs, d))  12.5 us
    all_to_all x1, starting transfers between devices, on_device(): lax.all_to_all(sent, AXES, 0, 0, tiled=True, axis_index_groups=core_group...  11.5 us
    unnamed x6, local copies, waits for them, and re-layouts  9.99 us
    ppermute x5, starting transfers between devices, to_twin(): return lax.ppermute(array, AXES, core_perm(devices))  4.37 us
    pallas_call x1, Pallas kernels, tile_parts(): pl.pallas_call(functools.partial(tile_body, rows, width), out_shape=jax.S...  4.01 us
    broadcast_in_dim x2, local copies, waits for them, and re-layouts, on_device(): jnp.broadcast_to(coordinates.reshape(1, block_rows, LANES), (groups * chi...  1.67 us
  transfers between devices with their start and end apart: 9, of which 5 were waited for; matrix products, arithmetic and copies ran while one was open for 4% of the time, Pallas kernels for 1%

profile of v2, /device:TPU:0, one launch (start us, length us, event | category | flops | bytes accessed | tf_op | source)
XLA Modules:
  0.0 78.2 jit_solution(5422336213519210522)
XLA Ops:
  0.6 0.7 broadcast_in_dim.46
  1.4 0.9 %broadcast_in_dim.47 = f32[64,24,128]{2,1,0:T(8,128)} broadcast(f32[24,128]{1,0:T(8,128)S(1)} %broadcast_in_dim.46), dimensions={1,2} | broadcast | bytes 798720 | tf_op jit(solution)/shard_map/broadcast_in_dim | solution.py:331
  2.3 11.5 %all-to-all-start = ((f32[64,24,128]{2,1,0:T(8,128)}), f32[64,24,128]{2,1,0:T(8,128)S(1)}, u32[]{:S(2)}, u32[]{:S(2)}) async-start(f32[64,24,128]{2,1,0:T(8,128)} %broadcast_in_dim.47), calls=%async_computation | async-start | bytes 1572864 | tf_op jit(solution)/shard_map/all_to_all | solution.py:334
  13.8 0.7 slice.15
  14.5 0.7 slice.16
  15.2 0.1 iota_add_fusion
  15.3 0.1 add.96
  15.4 0.9 %select_reduce_fusion = s32[256,2]{0,1:T(2,128)S(1)} fusion(s32[128]{0:T(128)} %param.5, s32[256,2]{0,1:T(2,128)S(1)} %slice.16), kind=kLoop, calls=%fused_computation | loop fusion | flops 196096 | bytes 4608 | tf_op jit(solution)/shard_map/reduce_sum | solution.py:306
  16.3 0.2 convert_reduce_fusion
  16.5 0.1 broadcast_compare_fusion
  16.5 13.1 %all-to-all-done.refs_0_ = f32[64,24,128]{2,1,0:T(8,128)S(1)} async-done(((f32[64,24,128]{2,1,0:T(8,128)}), f32[64,24,128]{2,1,0:T(8,128)S(1)}, u32[]{:S(2)}, u32[]{:S(2)}) %all-to-all-start) | async-done | bytes 786464 | tf_op jit(solution)/shard_map/all_to_all | solution.py:334
  29.7 0.0 collective-permute-start
  29.7 0.1 select_reduce_fusion.1
  29.8 0.1 copy.9
  29.9 0.1 slice.18
  30.0 0.1 slice.19
  30.1 0.0 copy-start.2
  30.1 3.4 %copy-done.2 = bf16[4,1024,1024]{2,1,0:T(8,128)(2,1)S(1)} copy-done((bf16[4,1024,1024]{2,1,0:T(8,128)(2,1)S(1)}, bf16[4,1024,1024]{2,1,0:T(8,128)(2,1)}, u32[]{:S(2)}) %copy-start.2) | copy-done | bytes 8388632
  33.5 0.6 fetch.1.delta
  34.0 0.0 copy-start
  34.1 3.2 %copy-done = bf16[4,1024,1024]{2,1,0:T(8,128)(2,1)} copy-done((bf16[4,1024,1024]{2,1,0:T(8,128)(2,1)}, bf16[4,1024,1024]{2,1,0:T(8,128)(2,1)S(1)}, u32[]{:S(2)}) %copy-start) | copy-done | bytes 8388632
  37.3 0.1 pad_add_fusion.sc
  37.4 0.0 collective-permute-done.refs_1_
  37.4 0.0 copy-start.1
  37.4 3.4 %copy-done.1 = bf16[4,1024,1024]{2,1,0:T(8,128)(2,1)S(1)} copy-done((bf16[4,1024,1024]{2,1,0:T(8,128)(2,1)S(1)}, bf16[4,1024,1024]{2,1,0:T(8,128)(2,1)}, u32[]{:S(2)}) %copy-start.1) | copy-done | bytes 8388632
  40.7 4.0 %tile_parts.1.refs_0_ = f32[200,128]{1,0:T(8,128)S(1)} custom-call(s32[20]{0:T(128)S(1)} %pad_add_fusion.sc, bf16[4,1024,1024]{2,1,0:T(8,128)(2,1)S(1)} %copy-done.1, f32[64,24,128]{2,1,0:T(8,128)S(1)} %all-to-all-done.refs_0_, f32[64,24,128]{2,1,0:T(8,128)S(1)} %collective-permute-done.refs_1_), custom_call_target="tpu_custom_call" | custom-call | tf_op jit(solution)/shard_map/tile_parts/pallas_call | solution.py:217
  44.8 9.8 %collective-permute-start.3 = (f32[200,128]{1,0:T(8,128)S(1)}, f32[200,128]{1,0:T(8,128)S(1)}, u32[]{:S(2)}, u32[]{:S(2)}) collective-permute-start(f32[200,128]{1,0:T(8,128)S(1)} %tile_parts.1.refs_0_), channel_id=1, source_target_pairs={{96,0},{97,1},{98,2},{99,3},{100,4},{101,5},{102,6},{103,7},{104,8... | collective-permute-start | bytes 307208 | tf_op jit(solution)/shard_map/ppermute | solution.py:48
  54.5 0.0 collective-permute-start.2
  54.5 2.8 %collective-permute-start.1 = (f32[200,128]{1,0:T(8,128)S(1)}, f32[200,128]{1,0:T(8,128)S(1)}, u32[]{:S(2)}, u32[]{:S(2)}) collective-permute-start(f32[200,128]{1,0:T(8,128)S(1)} %tile_parts.1.refs_0_), channel_id=1, source_target_pairs={{32,0},{33,1},{34,2},{35,3},{36,4},{37,5},{38,6},{39,7},{40,8},{41... | collective-permute-start | bytes 307208 | tf_op jit(solution)/shard_map/ppermute | solution.py:48
  57.3 0.1 copy.8
  57.4 0.1 sub.25
  57.5 0.1 collective-permute-start.4
  57.6 0.1 collective-permute-done.3.refs_3_
  57.7 3.8 %collective-permute-start.7 = (f32[200,128]{1,0:T(8,128)S(1)}, f32[200,128]{1,0:T(8,128)S(1)}, u32[]{:S(2)}, u32[]{:S(2)}) collective-permute-start(f32[200,128]{1,0:T(8,128)S(1)} %collective-permute-done.3.refs_3_), channel_id=1, source_target_pairs={{0,1},{1,0},{2,3},{3,2},{4,5},{5,4},{6,7},{7,6},{8,9},{9,8},{10,11... | collective-permute-start | bytes 307208 | tf_op jit(solution)/shard_map/ppermute | solution.py:43
  61.5 0.0 collective-permute-done.2.refs_2_
  61.5 0.0 collective-permute-start.6
  61.5 0.0 collective-permute-done.1.refs_1_
  61.5 0.5 collective-permute-start.5
  62.1 0.0 collective-permute-done.4.refs_4_
  62.1 0.4 collective-permute-done.7.refs_7_
  62.5 0.4 collective-permute-done.6.refs_6_
  62.8 0.2 collective-permute-done.5.refs_5_
  63.0 1.1 %by_chip.1 = f32[16,32,128]{2,1,0:T(8,128)S(1)} custom-call(s32[64]{0:T(128)S(1)} %and_select_fusion.4.where, f32[200,128]{1,0:T(8,128)S(1)} %tile_parts.1.refs_0_, f32[200,128]{1,0:T(8,128)S(1)} %collective-permute-done.1.refs_1_, f32[200,128]{1,0:T(8,128)S(1)} %collective-permute-done.2.refs_2_, f32[200,128]{1,0:T(8,128)S(1)} %collective-permute-done.3.refs_3_, ...), custom_call_target="tpu_custom_call" | custom-call | tf_op jit(solution)/shard_map/by_chip/pallas_call | solution.py:259
  64.1 12.6 %all_to_all.10.pieces = f32[16,32,128]{2,1,0:T(8,128)} all-to-all(f32[16,32,128]{2,1,0:T(8,128)S(1)} %by_chip.1), channel_id=1, replica_groups={{0,2,4,6,8,10,12,14,16,18,20,22,24,26,28,30},{1,3,5,7,9,11,13,15,17,19,..., dimensions={0} | all-to-all | bytes 524288 | tf_op jit(solution)/shard_map/all_to_all | solution.py:339
  76.6 1.6 %total.1 = (f32[3,1024]{1,0:T(4,128)}, f32[1,1]{1,0:T(1,128)}) custom-call(f32[16,32,128]{2,1,0:T(8,128)} %all_to_all.10.pieces), custom_call_target="tpu_custom_call" | custom-call | tf_op jit(solution)/shard_map/total/pallas_call | solution.py:284
  (7 shorter events, 0.1 us)
Async XLA Ops:
  2.3 27.4 %all-to-all-start = ((f32[64,24,128]{2,1,0:T(8,128)}), f32[64,24,128]{2,1,0:T(8,128)S(1)}, u32[]{:S(2)}, u32[]{:S(2)}) async-start(f32[64,24,128]{2,1,0:T(8,128)} %broadcast_in_dim.47), calls=%async_computation | async-start | bytes 1572864 | tf_op jit(solution)/shard_map/all_to_all | solution.py:334
  29.7 7.7 %collective-permute-start = (f32[64,24,128]{2,1,0:T(8,128)S(1)}, f32[64,24,128]{2,1,0:T(8,128)S(1)}, u32[]{:S(2)}, u32[]{:S(2)}) collective-permute-start(f32[64,24,128]{2,1,0:T(8,128)S(1)} %all-to-all-done.refs_0_), channel_id=1, source_target_pairs={{0,1},{1,0},{2,3},{3,2},{4,5},{5,4},{6,7},{7,6},{8,9},{9,8},{10,11... | collective-permute-start | bytes 2359304 | tf_op jit(solution)/shard_map/ppermute | solution.py:43
  30.1 3.4 %copy-start.2 = (bf16[4,1024,1024]{2,1,0:T(8,128)(2,1)S(1)}, bf16[4,1024,1024]{2,1,0:T(8,128)(2,1)}, u32[]{:S(2)}) copy-start(bf16[4,1024,1024]{2,1,0:T(8,128)(2,1)} %source.1) | copy-start | bytes 25165828
  34.0 3.2 %copy-start = (bf16[4,1024,1024]{2,1,0:T(8,128)(2,1)}, bf16[4,1024,1024]{2,1,0:T(8,128)(2,1)S(1)}, u32[]{:S(2)}) copy-start(bf16[4,1024,1024]{2,1,0:T(8,128)(2,1)S(1)} %fetch.1.delta) | copy-start | bytes 25165828
  37.4 3.4 %copy-start.1 = (bf16[4,1024,1024]{2,1,0:T(8,128)(2,1)S(1)}, bf16[4,1024,1024]{2,1,0:T(8,128)(2,1)}, u32[]{:S(2)}) copy-start(bf16[4,1024,1024]{2,1,0:T(8,128)(2,1)} %copy-done) | copy-start | bytes 25165828
  44.8 13.0 %collective-permute-start.3 = (f32[200,128]{1,0:T(8,128)S(1)}, f32[200,128]{1,0:T(8,128)S(1)}, u32[]{:S(2)}, u32[]{:S(2)}) collective-permute-start(f32[200,128]{1,0:T(8,128)S(1)} %tile_parts.1.refs_0_), channel_id=1, source_target_pairs={{96,0},{97,1},{98,2},{99,3},{100,4},{101,5},{102,6},{103,7},{104,8... | collective-permute-start | bytes 307208 | tf_op jit(solution)/shard_map/ppermute | solution.py:48
  54.5 7.0 %collective-permute-start.2 = (f32[200,128]{1,0:T(8,128)S(1)}, f32[200,128]{1,0:T(8,128)S(1)}, u32[]{:S(2)}, u32[]{:S(2)}) collective-permute-start(f32[200,128]{1,0:T(8,128)S(1)} %tile_parts.1.refs_0_), channel_id=1, source_target_pairs={{64,0},{65,1},{66,2},{67,3},{68,4},{69,5},{70,6},{71,7},{72,8},{73... | collective-permute-start | bytes 307208 | tf_op jit(solution)/shard_map/ppermute | solution.py:48
  54.5 7.0 %collective-permute-start.1 = (f32[200,128]{1,0:T(8,128)S(1)}, f32[200,128]{1,0:T(8,128)S(1)}, u32[]{:S(2)}, u32[]{:S(2)}) collective-permute-start(f32[200,128]{1,0:T(8,128)S(1)} %tile_parts.1.refs_0_), channel_id=1, source_target_pairs={{32,0},{33,1},{34,2},{35,3},{36,4},{37,5},{38,6},{39,7},{40,8},{41... | collective-permute-start | bytes 307208 | tf_op jit(solution)/shard_map/ppermute | solution.py:48
  57.5 4.6 %collective-permute-start.4 = (f32[200,128]{1,0:T(8,128)S(1)}, f32[200,128]{1,0:T(8,128)S(1)}, u32[]{:S(2)}, u32[]{:S(2)}) collective-permute-start(f32[200,128]{1,0:T(8,128)S(1)} %tile_parts.1.refs_0_), channel_id=1, source_target_pairs={{0,1},{1,0},{2,3},{3,2},{4,5},{5,4},{6,7},{7,6},{8,9},{9,8},{10,11... | collective-permute-start | bytes 307208 | tf_op jit(solution)/shard_map/ppermute | solution.py:43
  57.7 4.7 %collective-permute-start.7 = (f32[200,128]{1,0:T(8,128)S(1)}, f32[200,128]{1,0:T(8,128)S(1)}, u32[]{:S(2)}, u32[]{:S(2)}) collective-permute-start(f32[200,128]{1,0:T(8,128)S(1)} %collective-permute-done.3.refs_3_), channel_id=1, source_target_pairs={{0,1},{1,0},{2,3},{3,2},{4,5},{5,4},{6,7},{7,6},{8,9},{9,8},{10,11... | collective-permute-start | bytes 307208 | tf_op jit(solution)/shard_map/ppermute | solution.py:43
  61.5 1.3 %collective-permute-start.6 = (f32[200,128]{1,0:T(8,128)S(1)}, f32[200,128]{1,0:T(8,128)S(1)}, u32[]{:S(2)}, u32[]{:S(2)}) collective-permute-start(f32[200,128]{1,0:T(8,128)S(1)} %collective-permute-done.2.refs_2_), channel_id=1, source_target_pairs={{0,1},{1,0},{2,3},{3,2},{4,5},{5,4},{6,7},{7,6},{8,9},{9,8},{10,11... | collective-permute-start | bytes 307208 | tf_op jit(solution)/shard_map/ppermute | solution.py:43
  61.5 1.5 %collective-permute-start.5 = (f32[200,128]{1,0:T(8,128)S(1)}, f32[200,128]{1,0:T(8,128)S(1)}, u32[]{:S(2)}, u32[]{:S(2)}) collective-permute-start(f32[200,128]{1,0:T(8,128)S(1)} %collective-permute-done.1.refs_1_), channel_id=1, source_target_pairs={{0,1},{1,0},{2,3},{3,2},{4,5},{5,4},{6,7},{7,6},{8,9},{9,8},{10,11... | collective-permute-start | bytes 307208 | tf_op jit(solution)/shard_map/ppermute | solution.py:43

commit v3 on v2

--- a/solution.py
+++ b/solution.py
@@ -11,10 +11,10 @@
 FLOOR_SQUARED = 0.0625
 LANES = 128
 DIM = 3
-VMEM_LIMIT = 32 * 1024 * 1024
+VMEM_LIMIT = 24 * 1024 * 1024
+SMALL_LIMIT = 8 * 1024 * 1024
 KDIM = 128
 STEP = 128
-FETCH = 1024
 DEPTH = 512
 AHEAD = 1
 LAG = 1
@@ -32,11 +32,12 @@
     return [(i, i ^ 1) for i in range(devices)]
 
 
-def core_groups(groups, devs, planes):
-    blocks = [range(g * devs, (g + 1) * devs) for g in range(groups)]
-    if not planes:
-        blocks = [range(groups * devs)]
-    return [[d for d in b if d % 2 == core] for b in blocks for core in range(2)]
+def plane_groups(groups, devs):
+    return [
+        [g * devs + 2 * chip + core for chip in range(devs // 2)]
+        for g in range(groups)
+        for core in range(2)
+    ]
 
 
 def to_twin(array, devices):
@@ -44,10 +45,35 @@
 
 
 def from_line(array, groups, devs):
-    own = [array] + [
+    return [array] + [
         lax.ppermute(array, AXES, line_perm(groups, devs, d)) for d in range(1, groups)
     ]
-    return own + [to_twin(a, groups * devs) for a in own]
+
+
+def spread_body(*refs):
+    sources, out = refs[:-1], refs[-1]
+    chunks = sources[0].shape[1] // LANES
+    rows = [
+        s[c : c + 1, j * LANES : (j + 1) * LANES]
+        for s in sources
+        for c in range(DIM)
+        for j in range(chunks)
+    ]
+    block = jnp.concatenate(rows, axis=0)
+    for chip in range(out.shape[0]):
+        out[chip] = block
+
+
+def spread(sources, chips):
+    rows = len(sources) * sources[0].size // LANES
+    return pl.pallas_call(
+        spread_body,
+        out_shape=jax.ShapeDtypeStruct((chips, rows, LANES), jnp.float32),
+        in_specs=[pl.BlockSpec(memory_space=pltpu.VMEM)] * len(sources),
+        out_specs=pl.BlockSpec(memory_space=pltpu.VMEM),
+        compiler_params=pltpu.CompilerParams(vmem_limit_bytes=SMALL_LIMIT),
+        name="spread",
+    )(*sources)
 
 
 def split3(x):
@@ -58,32 +84,31 @@
     return high, middle, low
 
 
-def tile_body(rows, width, sc, delta, *refs):
+def tile_body(rows, width, sc, delta_hbm, *refs):
     sources = refs[:2]
-    parts, blocks, near, far, left, right, block_sem = refs[2:]
+    parts, delta, near, far, left, right, delta_sem = refs[2:]
     slots = delta.shape[0]
     chunks = width // LANES
     f32, bf16 = jnp.float32, jnp.bfloat16
 
-    def block_copy(s, i, at):
-        return pltpu.make_async_copy(sources[s].at[at], blocks.at[i], block_sem.at[i])
-
-    for i in range(2 * slots):
-        for s in range(2):
-            pl.when(sc[slots + i] == s)(
-                lambda i=i, s=s: block_copy(s, i, sc[3 * slots + i]).start()
-            )
-
-    for i in range(2 * slots):
-        block_copy(0, i, 0).wait()
+    def delta_copy(k):
+        return pltpu.make_async_copy(delta_hbm.at[k], delta.at[k], delta_sem.at[k])
+
+    pl.when(sc[0] > 0)(lambda: delta_copy(0).start())
 
     parts[2 * slots * DIM * chunks :, :] = jnp.zeros((8, LANES), f32)
 
     def one_tile(k, _):
         @pl.when(sc[k] > 0)
         def _():
+            delta_copy(k).wait()
+            later = jnp.minimum(k + 1, slots - 1)
+            pl.when((k + 1 < slots) & (sc[later] > 0))(lambda: delta_copy(later).start())
+
             def spread(i):
-                return [blocks[i, c * chunks : (c + 1) * chunks, :] for c in range(DIM)]
+                twin, at = sc[slots + i] > 0, sc[3 * slots + i]
+                found = jnp.where(twin, sources[1][at], sources[0][at])
+                return [found[c * chunks : (c + 1) * chunks, :] for c in range(DIM)]
 
             xa, xb = spread(2 * k), spread(2 * k + 1)
             mean = [jnp.sum(a, keepdims=True) * (1.0 / width) for a in xa]
@@ -190,47 +215,26 @@
     lax.fori_loop(0, slots, one_tile, 0)
 
 
-def fetch_body(source, out, sem):
-    copy = pltpu.make_async_copy(source, out, sem)
-    copy.start()
-    copy.wait()
-
-
-def fetch(dissim):
-    return pl.pallas_call(
-        fetch_body,
-        out_shape=pltpu.VMEM(dissim.shape, dissim.dtype),
-        in_specs=[pl.BlockSpec(memory_space=pl.ANY)],
-        out_specs=pl.BlockSpec(memory_space=pltpu.VMEM),
-        scratch_shapes=[pltpu.SemaphoreType.DMA],
-        cost_estimate=pl.CostEstimate(
-            flops=0, bytes_accessed=2 * dissim.size * dissim.dtype.itemsize, transcendentals=0
-        ),
-        compiler_params=pltpu.CompilerParams(vmem_limit_bytes=8 * 1024 * 1024),
-        name="fetch",
-    )(dissim)
-
-
 def tile_parts(scalars, dissim, sources):
     slots, rows, width = dissim.shape
     block_rows = DIM * width // LANES
     return pl.pallas_call(
         functools.partial(tile_body, rows, width),
         out_shape=jax.ShapeDtypeStruct((2 * slots * block_rows + 8, LANES), jnp.float32),
-        in_specs=[pl.BlockSpec(memory_space=pltpu.SMEM), pl.BlockSpec(memory_space=pltpu.VMEM)]
-        + [pl.BlockSpec(memory_space=pl.ANY)] * 2,
+    in_specs=[pl.BlockSpec(memory_space=pltpu.SMEM), pl.BlockSpec(memory_space=pltpu.HBM)]
+        + [pl.BlockSpec(memory_space=pltpu.VMEM)] * 2,
         out_specs=pl.BlockSpec(memory_space=pltpu.VMEM),
         scratch_shapes=[
-            pltpu.VMEM((2 * slots, block_rows, LANES), jnp.float32),
+            pltpu.VMEM((slots, rows, width), jnp.bfloat16),
             pltpu.VMEM((16, rows), jnp.float32),
             pltpu.VMEM((16, width), jnp.float32),
             pltpu.VMEM((KDIM, rows), jnp.float32),
             pltpu.VMEM((KDIM, width), jnp.float32),
-            pltpu.SemaphoreType.DMA((2 * slots,)),
+            pltpu.SemaphoreType.DMA((slots,)),
         ],
         compiler_params=pltpu.CompilerParams(vmem_limit_bytes=VMEM_LIMIT),
         name="tile_parts",
-    )(scalars, pltpu.with_memory_space_constraint(dissim, pltpu.VMEM), *sources)
+    )(scalars, pltpu.with_memory_space_constraint(dissim, pltpu.HBM), *sources)
 
 
 def gather_body(count, block_rows, where, *refs):
@@ -262,7 +266,7 @@
         in_specs=[pl.BlockSpec(memory_space=pltpu.SMEM)]
         + [pl.BlockSpec(memory_space=pltpu.VMEM)] * len(sources),
         out_specs=pl.BlockSpec(memory_space=pltpu.VMEM),
-        compiler_params=pltpu.CompilerParams(vmem_limit_bytes=VMEM_LIMIT),
+        compiler_params=pltpu.CompilerParams(vmem_limit_bytes=SMALL_LIMIT),
         name="by_chip",
     )(where, *sources)
 
@@ -292,6 +296,7 @@
             pl.BlockSpec(memory_space=pltpu.VMEM),
             pl.BlockSpec(memory_space=pltpu.SMEM),
         ),
+        compiler_params=pltpu.CompilerParams(vmem_limit_bytes=SMALL_LIMIT),
         name="total",
     )(pieces)
 
@@ -314,7 +319,8 @@
     mine = held[: 2 * slots]
     present = (mine[::2] >= 0).astype(jnp.int32)
     at = jnp.maximum(mine, 0)
-    for_tiles = jnp.concatenate([present, at % 2 ^ dev % 2, at // 2])
+    place = at % devs // 2 * groups + (at // devs - group) % groups
+    for_tiles = jnp.concatenate([present, at % 2 ^ dev % 2, place])
     here = (held >= 0) & (held // devs == group) & (held % 2 == dev % 2)
     where = jnp.where(here, held % devs // 2, -1)
     return for_tiles, where
@@ -327,18 +333,15 @@
     slots = dissim.shape[0]
     block_rows = DIM * width // LANES
     for_tiles, where = tables(tile_list, holder, groups, devs, slots)
-    delta = fetch(dissim)
-    sent = jnp.broadcast_to(
-        coordinates.reshape(1, block_rows, LANES), (groups * chips, block_rows, LANES)
-    )
-    own = lax.all_to_all(
-        sent, AXES, 0, 0, tiled=True, axis_index_groups=core_groups(groups, devs, False)
-    )
-    parts = tile_parts(for_tiles, delta, [own, to_twin(own, groups * devs)])
-    pieces = by_chip(where, from_line(parts, groups, devs), chips)
-    pieces = lax.all_to_all(
-        pieces, AXES, 0, 0, tiled=True, axis_index_groups=core_groups(groups, devs, True)
-    )
+    plane = plane_groups(groups, devs)
+    sent = spread(from_line(coordinates, groups, devs), chips)
+    own = lax.all_to_all(sent, AXES, 0, 0, tiled=True, axis_index_groups=plane)
+    own = own.reshape(groups * chips, block_rows, LANES)
+    parts = tile_parts(for_tiles, dissim, [own, to_twin(own, groups * devs)])
+    line = from_line(parts, groups, devs)
+    line = line + [to_twin(a, groups * devs) for a in line]
+    pieces = by_chip(where, line, chips)
+    pieces = lax.all_to_all(pieces, AXES, 0, 0, tiled=True, axis_index_groups=plane)
     guttman, stress = total_of(pieces, width)
     return guttman, stress[0, 0]
 

time: 78.4 us -> 72.4 us (0.923)
  local copies, waits for them, and re-layouts: 13.6 us -> 2.65 us
  Pallas kernels: 7.27 us -> 10.9 us
  waiting for transfers between devices: 14.2 us -> 16.8 us
  starting transfers between devices: 28.4 us -> 26.6 us
    unnamed x6 -> x2, local copies, waits for them, and re-layouts: 9.99 us -> 0.72 us
    pallas_call x1, Pallas kernels: 4.01 us -> 8.18 us  [tile_parts(): pl.pallas_call(functools.partial(tile_body, rows, width), out_shape=jax.S...]
    all_to_all x1, starting transfers between devices: 11.5 us -> 8.05 us  [on_device(): own = lax.all_to_all(sent, AXES, 0, 0, tiled=True, axis_index_groups=plane)]
    ppermute x5, waiting for transfers between devices: 0.92 us -> 2.69 us  [to_twin(): return lax.ppermute(array, AXES, core_perm(devices))]
    broadcast_in_dim x2 -> x0, local copies, waits for them, and re-layouts: 1.67 us -> none  [on_device(): jnp.broadcast_to(coordinates.reshape(1, block_rows, LANES), (groups * chi...]
    ppermute x3 -> x6, waiting for transfers between devices: 0.15 us -> 1.82 us  [from_line(): lax.ppermute(array, AXES, line_perm(groups, devs, d))]
    ppermute x3 -> x6, starting transfers between devices: 12.5 us -> 13.7 us  [from_line(): lax.ppermute(array, AXES, line_perm(groups, devs, d))]
    pallas_call x1, Pallas kernels: 1.6 us -> 0.65 us  [total_of(): pl.pallas_call(functools.partial(total_body, width), out_shape=(jax.Shape...]
  transfers between devices with their start and end apart: 9 -> 12, of which waited for: 5 -> 6; matrix products, arithmetic and copies ran while one was open for 4% -> 5% of each run, Pallas kernels for 1% -> 0%
where the time goes in v3:
time: 72.4 us; the launch traced here: 72.1 us
  starting transfers between devices  26.6 us (37%)
  waiting for transfers between devices  16.8 us (23%)
  blocking collectives  12.9 us (18%)
  Pallas kernels  10.9 us (15%)
  local copies, waits for them, and re-layouts  2.65 us (4%)
  other arithmetic  1.48 us (2%)
    ppermute x6, starting transfers between devices, from_line(): lax.ppermute(array, AXES, line_perm(groups, devs, d))  13.7 us
    all_to_all x1, blocking collectives, on_device(): lax.all_to_all(pieces, AXES, 0, 0, tiled=True, axis_index_groups=plane)  12.9 us
    all_to_all x1, waiting for transfers between devices, on_device(): own = lax.all_to_all(sent, AXES, 0, 0, tiled=True, axis_index_groups=plane)  12.3 us
    pallas_call x1, Pallas kernels, tile_parts(): pl.pallas_call(functools.partial(tile_body, rows, width), out_shape=jax.S...  8.18 us
    all_to_all x1, starting transfers between devices, on_device(): own = lax.all_to_all(sent, AXES, 0, 0, tiled=True, axis_index_groups=plane)  8.05 us
    ppermute x5, starting transfers between devices, to_twin(): return lax.ppermute(array, AXES, core_perm(devices))  4.93 us
    ppermute x5, waiting for transfers between devices, to_twin(): return lax.ppermute(array, AXES, core_perm(devices))  2.69 us
    ppermute x6, waiting for transfers between devices, from_line(): lax.ppermute(array, AXES, line_perm(groups, devs, d))  1.82 us
  transfers between devices with their start and end apart: 12, of which 6 were waited for; matrix products, arithmetic and copies ran while one was open for 5% of the time, Pallas kernels for 0%

profile of v3, /device:TPU:0, one launch (start us, length us, event | category | flops | bytes accessed | tf_op | source)
XLA Modules:
  0.0 72.1 jit_solution(737812800741539802)
XLA Ops:
  0.6 3.2 %collective-permute-start.1 = (f32[3,1024]{1,0:T(4,128)}, f32[3,1024]{1,0:T(4,128)S(1)}, u32[]{:S(2)}, u32[]{:S(2)}) collective-permute-start(f32[3,1024]{1,0:T(4,128)} %refs_0_.1), channel_id=1, source_target_pairs={{64,0},{65,1},{66,2},{67,3},{68,4},{69,5},{70,6},{71,7},{72,8},{73... | collective-permute-start | bytes 36872 | tf_op jit(solution)/shard_map/ppermute | solution.py:49
  3.8 1.1 %collective-permute-start = (f32[3,1024]{1,0:T(4,128)}, f32[3,1024]{1,0:T(4,128)S(1)}, u32[]{:S(2)}, u32[]{:S(2)}) collective-permute-start(f32[3,1024]{1,0:T(4,128)} %refs_0_.1), channel_id=1, source_target_pairs={{32,0},{33,1},{34,2},{35,3},{36,4},{37,5},{38,6},{39,7},{40,8},{41... | collective-permute-start | bytes 36872 | tf_op jit(solution)/shard_map/ppermute | solution.py:49
  5.0 0.9 %collective-permute-start.2 = (f32[3,1024]{1,0:T(4,128)}, f32[3,1024]{1,0:T(4,128)S(1)}, u32[]{:S(2)}, u32[]{:S(2)}) collective-permute-start(f32[3,1024]{1,0:T(4,128)} %refs_0_.1), channel_id=1, source_target_pairs={{96,0},{97,1},{98,2},{99,3},{100,4},{101,5},{102,6},{103,7},{104,8... | collective-permute-start | bytes 36872 | tf_op jit(solution)/shard_map/ppermute | solution.py:49
  5.8 0.7 slice.16
  6.5 0.1 iota_add_fusion
  6.6 0.9 %select_reduce_fusion = s32[256,2]{0,1:T(2,128)S(1)} fusion(s32[128]{0:T(128)} %param.5, s32[256,2]{0,1:T(2,128)S(1)} %slice.16), kind=kLoop, calls=%fused_computation | loop fusion | flops 196096 | bytes 4608 | tf_op jit(solution)/shard_map/reduce_sum | solution.py:311
  7.5 0.7 slice.15
  8.2 0.1 add.108
  8.3 0.0 collective-permute-done.1.refs_2_
  8.3 0.0 collective-permute-done.refs_1_
  8.3 1.8 %collective-permute-done.2.refs_3_ = f32[3,1024]{1,0:T(4,128)S(1)} collective-permute-done((f32[3,1024]{1,0:T(4,128)}, f32[3,1024]{1,0:T(4,128)S(1)}, u32[]{:S(2)}, u32[]{:S(2)}) %collective-permute-start.2) | collective-permute-done | bytes 12320 | tf_op jit(solution)/shard_map/ppermute | solution.py:49
  10.1 0.0 copy-start
  10.1 0.7 copy-done
  10.8 1.0 %spread.1 = f32[16,96,128]{2,1,0:T(8,128)} custom-call(f32[3,1024]{1,0:T(4,128)S(1)} %copy-done, f32[3,1024]{1,0:T(4,128)S(1)} %collective-permute-done.refs_1_, f32[3,1024]{1,0:T(4,128)S(1)} %collective-permute-done.1.refs_2_, f32[3,1024]{1,0:T(4,128)S(1)} %collective-permute-done.2.refs_3_), custom_call_target="tpu_custom_call" | custom-call | tf_op jit(solution)/shard_map/spread/pallas_call | solution.py:69
  11.8 8.0 %all-to-all-start = ((f32[16,96,128]{2,1,0:T(8,128)}), f32[16,96,128]{2,1,0:T(8,128)S(1)}, u32[]{:S(2)}, u32[]{:S(2)}) async-start(f32[16,96,128]{2,1,0:T(8,128)} %spread.1), calls=%async_computation | async-start | bytes 1572864 | tf_op jit(solution)/shard_map/all_to_all | solution.py:338
  19.9 0.2 convert_reduce_fusion
  20.1 0.1 broadcast_compare_fusion
  20.1 12.3 %all-to-all-done = f32[16,96,128]{2,1,0:T(8,128)S(1)} async-done(((f32[16,96,128]{2,1,0:T(8,128)}), f32[16,96,128]{2,1,0:T(8,128)S(1)}, u32[]{:S(2)}, u32[]{:S(2)}) %all-to-all-start) | async-done | bytes 786464 | tf_op jit(solution)/shard_map/all_to_all | solution.py:338
  32.4 0.0 collective-permute-start.3
  32.4 0.1 select_reduce_fusion.1
  32.6 0.1 copy.9
  32.7 0.1 slice.18
  32.8 0.1 slice.19
  32.9 0.1 pad_add_fusion.sc
  33.0 1.8 %collective-permute-done.3.refs_1_ = f32[64,24,128]{2,1,0:T(8,128)S(1)} collective-permute-done((f32[64,24,128]{2,1,0:T(8,128)S(1)}, f32[64,24,128]{2,1,0:T(8,128)S(1)}, u32[]{:S(2)}, u32[]{:S(2)}) %collective-permute-start.3) | collective-permute-done | bytes 786464 | tf_op jit(solution)/shard_map/ppermute | solution.py:44
  34.7 8.2 %tile_parts.1.refs_0_ = f32[200,128]{1,0:T(8,128)S(1)} custom-call(s32[20]{0:T(128)S(1)} %pad_add_fusion.sc, bf16[4,1024,1024]{2,1,0:T(8,128)(2,1)} %delta_hbm.1, f32[64,24,128]{2,1,0:T(8,128)S(1)} %bitcast.5, f32[64,24,128]{2,1,0:T(8,128)S(1)} %collective-permute-done.3.refs_1_), custom_call_target="tpu_custom_call" | custom-call | tf_op jit(solution)/shard_map/tile_parts/pallas_call | solution.py:221
  42.9 5.7 %collective-permute-start.6 = (f32[200,128]{1,0:T(8,128)S(1)}, f32[200,128]{1,0:T(8,128)S(1)}, u32[]{:S(2)}, u32[]{:S(2)}) collective-permute-start(f32[200,128]{1,0:T(8,128)S(1)} %tile_parts.1.refs_0_), channel_id=1, source_target_pairs={{96,0},{97,1},{98,2},{99,3},{100,4},{101,5},{102,6},{103,7},{104,8... | collective-permute-start | bytes 307208 | tf_op jit(solution)/shard_map/ppermute | solution.py:49
  48.6 0.0 collective-permute-start.5
  48.6 2.8 %collective-permute-start.4 = (f32[200,128]{1,0:T(8,128)S(1)}, f32[200,128]{1,0:T(8,128)S(1)}, u32[]{:S(2)}, u32[]{:S(2)}) collective-permute-start(f32[200,128]{1,0:T(8,128)S(1)} %tile_parts.1.refs_0_), channel_id=1, source_target_pairs={{32,0},{33,1},{34,2},{35,3},{36,4},{37,5},{38,6},{39,7},{40,8},{41... | collective-permute-start | bytes 307208 | tf_op jit(solution)/shard_map/ppermute | solution.py:49
  51.4 0.1 copy.8
  51.5 0.1 sub.32
  51.6 0.5 collective-permute-start.7
  52.0 0.0 collective-permute-done.6.refs_3_
  52.0 4.0 %collective-permute-start.10 = (f32[200,128]{1,0:T(8,128)S(1)}, f32[200,128]{1,0:T(8,128)S(1)}, u32[]{:S(2)}, u32[]{:S(2)}) collective-permute-start(f32[200,128]{1,0:T(8,128)S(1)} %collective-permute-done.6.refs_3_), channel_id=1, source_target_pairs={{0,1},{1,0},{2,3},{3,2},{4,5},{5,4},{6,7},{7,6},{8,9},{9,8},{10,11... | collective-permute-start | bytes 307208 | tf_op jit(solution)/shard_map/ppermute | solution.py:44
  56.0 0.0 collective-permute-done.5.refs_2_
  56.0 0.0 collective-permute-start.9
  56.0 0.0 collective-permute-done.4.refs_1_
  56.0 0.5 collective-permute-start.8
  56.5 0.0 collective-permute-done.7.refs_4_
  56.5 0.4 collective-permute-done.10.refs_7_
  56.9 0.4 collective-permute-done.9.refs_6_
  57.3 0.2 collective-permute-done.8.refs_5_
  57.5 1.1 %by_chip.1 = f32[16,32,128]{2,1,0:T(8,128)S(1)} custom-call(s32[64]{0:T(128)S(1)} %and_select_fusion.7.where, f32[200,128]{1,0:T(8,128)S(1)} %tile_parts.1.refs_0_, f32[200,128]{1,0:T(8,128)S(1)} %collective-permute-done.4.refs_1_, f32[200,128]{1,0:T(8,128)S(1)} %collective-permute-done.5.refs_2_, f32[200,128]{1,0:T(8,128)S(1)} %collective-permute-done.6.refs_3_, ...), custom_call_target="tpu_custom_call" | custom-call | tf_op jit(solution)/shard_map/by_chip/pallas_call | solution.py:263
  58.5 12.9 %all_to_all.10.pieces = f32[16,32,128]{2,1,0:T(8,128)S(1)} all-to-all(f32[16,32,128]{2,1,0:T(8,128)S(1)} %by_chip.1), channel_id=1, replica_groups={{0,2,4,6,8,10,12,14,16,18,20,22,24,26,28,30},{1,3,5,7,9,11,13,15,17,19,..., dimensions={0} | all-to-all | bytes 524288 | tf_op jit(solution)/shard_map/all_to_all | solution.py:344
  71.4 0.6 total.1
  (7 shorter events, 0.1 us)
Async XLA Ops:
  0.6 7.7 %collective-permute-start.1 = (f32[3,1024]{1,0:T(4,128)}, f32[3,1024]{1,0:T(4,128)S(1)}, u32[]{:S(2)}, u32[]{:S(2)}) collective-permute-start(f32[3,1024]{1,0:T(4,128)} %refs_0_.1), channel_id=1, source_target_pairs={{64,0},{65,1},{66,2},{67,3},{68,4},{69,5},{70,6},{71,7},{72,8},{73... | collective-permute-start | bytes 36872 | tf_op jit(solution)/shard_map/ppermute | solution.py:49
  3.8 4.5 %collective-permute-start = (f32[3,1024]{1,0:T(4,128)}, f32[3,1024]{1,0:T(4,128)S(1)}, u32[]{:S(2)}, u32[]{:S(2)}) collective-permute-start(f32[3,1024]{1,0:T(4,128)} %refs_0_.1), channel_id=1, source_target_pairs={{32,0},{33,1},{34,2},{35,3},{36,4},{37,5},{38,6},{39,7},{40,8},{41... | collective-permute-start | bytes 36872 | tf_op jit(solution)/shard_map/ppermute | solution.py:49
  5.0 5.2 %collective-permute-start.2 = (f32[3,1024]{1,0:T(4,128)}, f32[3,1024]{1,0:T(4,128)S(1)}, u32[]{:S(2)}, u32[]{:S(2)}) collective-permute-start(f32[3,1024]{1,0:T(4,128)} %refs_0_.1), channel_id=1, source_target_pairs={{96,0},{97,1},{98,2},{99,3},{100,4},{101,5},{102,6},{103,7},{104,8... | collective-permute-start | bytes 36872 | tf_op jit(solution)/shard_map/ppermute | solution.py:49
  10.1 0.7 copy-start
  11.8 20.6 %all-to-all-start = ((f32[16,96,128]{2,1,0:T(8,128)}), f32[16,96,128]{2,1,0:T(8,128)S(1)}, u32[]{:S(2)}, u32[]{:S(2)}) async-start(f32[16,96,128]{2,1,0:T(8,128)} %spread.1), calls=%async_computation | async-start | bytes 1572864 | tf_op jit(solution)/shard_map/all_to_all | solution.py:338
  32.4 2.3 %collective-permute-start.3 = (f32[64,24,128]{2,1,0:T(8,128)S(1)}, f32[64,24,128]{2,1,0:T(8,128)S(1)}, u32[]{:S(2)}, u32[]{:S(2)}) collective-permute-start(f32[64,24,128]{2,1,0:T(8,128)S(1)} %bitcast.4), channel_id=1, source_target_pairs={{0,1},{1,0},{2,3},{3,2},{4,5},{5,4},{6,7},{7,6},{8,9},{9,8},{10,11... | collective-permute-start | bytes 2359304 | tf_op jit(solution)/shard_map/ppermute | solution.py:44
  42.9 9.1 %collective-permute-start.6 = (f32[200,128]{1,0:T(8,128)S(1)}, f32[200,128]{1,0:T(8,128)S(1)}, u32[]{:S(2)}, u32[]{:S(2)}) collective-permute-start(f32[200,128]{1,0:T(8,128)S(1)} %tile_parts.1.refs_0_), channel_id=1, source_target_pairs={{96,0},{97,1},{98,2},{99,3},{100,4},{101,5},{102,6},{103,7},{104,8... | collective-permute-start | bytes 307208 | tf_op jit(solution)/shard_map/ppermute | solution.py:49
  48.6 7.4 %collective-permute-start.5 = (f32[200,128]{1,0:T(8,128)S(1)}, f32[200,128]{1,0:T(8,128)S(1)}, u32[]{:S(2)}, u32[]{:S(2)}) collective-permute-start(f32[200,128]{1,0:T(8,128)S(1)} %tile_parts.1.refs_0_), channel_id=1, source_target_pairs={{64,0},{65,1},{66,2},{67,3},{68,4},{69,5},{70,6},{71,7},{72,8},{73... | collective-permute-start | bytes 307208 | tf_op jit(solution)/shard_map/ppermute | solution.py:49
  48.6 7.4 %collective-permute-start.4 = (f32[200,128]{1,0:T(8,128)S(1)}, f32[200,128]{1,0:T(8,128)S(1)}, u32[]{:S(2)}, u32[]{:S(2)}) collective-permute-start(f32[200,128]{1,0:T(8,128)S(1)} %tile_parts.1.refs_0_), channel_id=1, source_target_pairs={{32,0},{33,1},{34,2},{35,3},{36,4},{37,5},{38,6},{39,7},{40,8},{41... | collective-permute-start | bytes 307208 | tf_op jit(solution)/shard_map/ppermute | solution.py:49
  51.6 5.0 %collective-permute-start.7 = (f32[200,128]{1,0:T(8,128)S(1)}, f32[200,128]{1,0:T(8,128)S(1)}, u32[]{:S(2)}, u32[]{:S(2)}) collective-permute-start(f32[200,128]{1,0:T(8,128)S(1)} %tile_parts.1.refs_0_), channel_id=1, source_target_pairs={{0,1},{1,0},{2,3},{3,2},{4,5},{5,4},{6,7},{7,6},{8,9},{9,8},{10,11... | collective-permute-start | bytes 307208 | tf_op jit(solution)/shard_map/ppermute | solution.py:44
  52.0 4.9 %collective-permute-start.10 = (f32[200,128]{1,0:T(8,128)S(1)}, f32[200,128]{1,0:T(8,128)S(1)}, u32[]{:S(2)}, u32[]{:S(2)}) collective-permute-start(f32[200,128]{1,0:T(8,128)S(1)} %collective-permute-done.6.refs_3_), channel_id=1, source_target_pairs={{0,1},{1,0},{2,3},{3,2},{4,5},{5,4},{6,7},{7,6},{8,9},{9,8},{10,11... | collective-permute-start | bytes 307208 | tf_op jit(solution)/shard_map/ppermute | solution.py:44
  56.0 1.3 %collective-permute-start.9 = (f32[200,128]{1,0:T(8,128)S(1)}, f32[200,128]{1,0:T(8,128)S(1)}, u32[]{:S(2)}, u32[]{:S(2)}) collective-permute-start(f32[200,128]{1,0:T(8,128)S(1)} %collective-permute-done.5.refs_2_), channel_id=1, source_target_pairs={{0,1},{1,0},{2,3},{3,2},{4,5},{5,4},{6,7},{7,6},{8,9},{9,8},{10,11... | collective-permute-start | bytes 307208 | tf_op jit(solution)/shard_map/ppermute | solution.py:44
  56.0 1.5 %collective-permute-start.8 = (f32[200,128]{1,0:T(8,128)S(1)}, f32[200,128]{1,0:T(8,128)S(1)}, u32[]{:S(2)}, u32[]{:S(2)}) collective-permute-start(f32[200,128]{1,0:T(8,128)S(1)} %collective-permute-done.4.refs_1_), channel_id=1, source_target_pairs={{0,1},{1,0},{2,3},{3,2},{4,5},{5,4},{6,7},{7,6},{8,9},{9,8},{10,11... | collective-permute-start | bytes 307208 | tf_op jit(solution)/shard_map/ppermute | solution.py:44

commit v4 on v3

--- a/solution.py
+++ b/solution.py
@@ -13,11 +13,11 @@
 DIM = 3
 VMEM_LIMIT = 24 * 1024 * 1024
 SMALL_LIMIT = 8 * 1024 * 1024
-KDIM = 128
+KDIM = 48
 STEP = 128
-DEPTH = 512
-AHEAD = 1
-LAG = 1
+DEPTH = 256
+AHEAD = 6
+LAG = 2
 
 
 def line_perm(groups, devs, shift):
@@ -52,14 +52,14 @@
 
 def spread_body(*refs):
     sources, out = refs[:-1], refs[-1]
-    chunks = sources[0].shape[1] // LANES
+    chunks = sources[1].shape[1] // LANES
     rows = [
         s[c : c + 1, j * LANES : (j + 1) * LANES]
-        for s in sources
+        for s in sources[1:]
         for c in range(DIM)
         for j in range(chunks)
     ]
-    block = jnp.concatenate(rows, axis=0)
+    block = jnp.concatenate([sources[0][...]] + rows, axis=0)
     for chip in range(out.shape[0]):
         out[chip] = block
 
@@ -77,14 +77,14 @@
 
 
 def split3(x):
-    high = x.astype(jnp.bfloat16)
-    rest = x - high.astype(jnp.float32)
-    middle = rest.astype(jnp.bfloat16)
-    low = (rest - middle.astype(jnp.float32)).astype(jnp.bfloat16)
+    high = x.astype(jnp.bfloat16).astype(jnp.float32)
+    rest = x - high
+    middle = rest.astype(jnp.bfloat16).astype(jnp.float32)
+    low = (rest - middle).astype(jnp.bfloat16).astype(jnp.float32)
     return high, middle, low
 
 
-def tile_body(rows, width, sc, delta_hbm, *refs):
+def tile_body(rows, width, sc, delta_hbm, first, *refs):
     sources = refs[:2]
     parts, delta, near, far, left, right, delta_sem = refs[2:]
     slots = delta.shape[0]
@@ -94,9 +94,14 @@
     def delta_copy(k):
         return pltpu.make_async_copy(delta_hbm.at[k], delta.at[k], delta_sem.at[k])
 
-    pl.when(sc[0] > 0)(lambda: delta_copy(0).start())
+    @pl.when(sc[0] > 0)
+    def _():
+        pltpu.make_async_copy(first, delta.at[0], delta_sem.at[0]).start()
+
 
     parts[2 * slots * DIM * chunks :, :] = jnp.zeros((8, LANES), f32)
+    for ref in (near, far, left, right):
+        ref[...] = jnp.zeros(ref.shape, f32)
 
     def one_tile(k, _):
         @pl.when(sc[k] > 0)
@@ -105,63 +110,55 @@
             later = jnp.minimum(k + 1, slots - 1)
             pl.when((k + 1 < slots) & (sc[later] > 0))(lambda: delta_copy(later).start())
 
-            def spread(i):
+            def block(i):
                 twin, at = sc[slots + i] > 0, sc[3 * slots + i]
                 found = jnp.where(twin, sources[1][at], sources[0][at])
                 return [found[c * chunks : (c + 1) * chunks, :] for c in range(DIM)]
 
-            xa, xb = spread(2 * k), spread(2 * k + 1)
+            xa, xb = block(2 * k), block(2 * k + 1)
             mean = [jnp.sum(a, keepdims=True) * (1.0 / width) for a in xa]
             xa = [a - m for a, m in zip(xa, mean)]
             xb = [b - m for b, m in zip(xb, mean)]
-
-            def fill(ref, x, scale, norm_first):
+            one = jnp.ones((chunks, LANES), f32)
+
+            def terms(x):
                 pieces = [split3(v) for v in x]
-                norm = x[0] * x[0] + x[1] * x[1] + x[2] * x[2]
-                norms = split3(norm)
-                one = jnp.ones((chunks, LANES), bf16)
-                out = []
-                for c in range(DIM):
-                    for s in range(3):
-                        for t in range(3):
-                            out.append(pieces[c][s] * scale if norm_first else pieces[c][t])
-                for s in range(3):
-                    out.append(norms[s] if norm_first else one)
-                for s in range(3):
-                    out.append(one if norm_first else norms[s])
-                return out
-
-            la = fill(None, xa, -2.0, True)
-            lb = fill(None, xb, 1.0, False)
-            one = jnp.ones((chunks, LANES), bf16)
-            va = [p for v in xa for p in split3(v)] + [one]
-            vb = [p for v in xb for p in split3(v)] + [one]
-            for ref, rows_ in ((left, la), (right, lb), (near, va), (far, vb)):
-                ref[...] = jnp.zeros(ref.shape, f32)
-                for n, v in enumerate(rows_):
-                    v = v.astype(f32)
-                    for j in range(chunks):
-                        ref[n : n + 1, j * LANES : (j + 1) * LANES] = v[j : j + 1, :]
-            cols = right[...].astype(bf16)
-            weights = far[...].astype(bf16)
-
-            lhs = jnp.transpose(left[...]).astype(bf16)
-            mine = near[...].astype(bf16)
+                norms = split3(x[0] * x[0] + x[1] * x[1] + x[2] * x[2])
+                return pieces, list(norms)
+
+            (pa, na), (pb, nb) = terms(xa), terms(xb)
+            pairs = [(s, t) for s in range(3) for t in range(3)]
+            la = [p[s] * -2.0 for p in pa for s, _ in pairs] + na + [one] * 3
+            lb = [p[t] for p in pb for _, t in pairs] + [one] * 3 + nb
+            va = [v for p in pa for v in p] + [one]
+            vb = [v for p in pb for v in p] + [one]
+            for ref, values in ((left, la), (right, lb), (near, va), (far, vb)):
+                for n, v in enumerate(values):
+                    ref[n] = v
             count = rows // STEP
             pieces = width // DEPTH
+
+            def wide(ref, g):
+                each = DEPTH // LANES
+                return jnp.concatenate(
+                    [ref[:, g * each + e, :] for e in range(each)], axis=1
+                ).astype(bf16)
+
+            lhs = [jnp.transpose(left[:, n, :]).astype(bf16) for n in range(count)]
+            mine = [near[:, n, :].astype(bf16) for n in range(count)]
+            mine = [jnp.concatenate([m, m], axis=1) for m in mine]
+            cols = [wide(right, g) for g in range(pieces)]
+            weights = [wide(far, g) for g in range(pieces)]
             stress = jnp.zeros((16, LANES), f32)
             row, col = [None] * count, [None] * pieces
 
             def front(n, g):
-                lanes = slice(g * DEPTH, (g + 1) * DEPTH)
                 return lax.dot_general(
-                    lhs[n * STEP : (n + 1) * STEP], cols[:, lanes], (((1,), (0,)), ((), ())), preferred_element_type=f32
+                    lhs[n], cols[g], (((1,), (0,)), ((), ())), preferred_element_type=f32
                 )
 
             def back(n, g, squared, stress):
                 lanes = slice(g * DEPTH, (g + 1) * DEPTH)
-                own = mine[:, n * STEP : (n + 1) * STEP]
-                own = jnp.concatenate([own, own], axis=1)
                 target = delta[k, n * STEP : (n + 1) * STEP, lanes].astype(f32)
                 squared = jnp.maximum(squared, FLOOR_SQUARED)
                 inverse = lax.rsqrt(squared)
@@ -173,19 +170,17 @@
                 ratio = target * inverse
                 high = ratio.astype(bf16)
                 low = (ratio - high.astype(f32)).astype(bf16)
-                both = jnp.concatenate([high, low], axis=0)
-                return stress, both
+                return stress, jnp.concatenate([high, low], axis=0)
 
             def last(n, g, both):
-                lanes = slice(g * DEPTH, (g + 1) * DEPTH)
-                own = mine[:, n * STEP : (n + 1) * STEP]
-                own = jnp.concatenate([own, own], axis=1)
                 a = lax.dot_general(
-                    weights[:, lanes], both, (((1,), (1,)), ((), ())), preferred_element_type=f32
+                    mine[n], both, (((1,), (0,)), ((), ())), preferred_element_type=f32
+                )
+                col[g] = a if col[g] is None else col[g] + a
+                a = lax.dot_general(
+                    weights[g], both, (((1,), (1,)), ((), ())), preferred_element_type=f32
                 )
                 row[n] = a if row[n] is None else row[n] + a
-                a = lax.dot_general(own, both, (((1,), (0,)), ((), ())), preferred_element_type=f32)
-                col[g] = a if col[g] is None else col[g] + a
 
             order = [(n, g) for n in range(count) for g in range(pieces)]
             ahead = [front(*order[t]) for t in range(AHEAD)]
@@ -199,15 +194,16 @@
                 held.append((n, g, both))
             for h in held:
                 last(*h)
-            row = jnp.concatenate([r[:, :STEP] + r[:, STEP:] for r in row], axis=1)
-            col = jnp.concatenate(col, axis=1)
-            for side, own, total in ((0, near, row), (1, far, col)):
+            row = [r[:, :STEP] + r[:, STEP:] for r in row]
+            col = [c[:, e * LANES : (e + 1) * LANES] for c in col for e in range(DEPTH // LANES)]
+            for side, own, total in ((0, xa, row), (1, xb, col)):
+                first_row = (2 * k + side) * DIM * chunks
                 for c in range(DIM):
-                    cross = total[3 * c : 3 * c + 1] + total[3 * c + 1 : 3 * c + 2] + total[3 * c + 2 : 3 * c + 3]
-                    x = own[3 * c : 3 * c + 1, :] + own[3 * c + 1 : 3 * c + 2, :] + own[3 * c + 2 : 3 * c + 3, :]
-                    value = x * total[9:10] - cross
                     for j in range(chunks):
-                        parts[pl.ds((2 * k + side) * DIM * chunks + c * chunks + j, 1), :] = value[:, j * LANES : (j + 1) * LANES]
+                        t = total[j]
+                        cross = t[3 * c : 3 * c + 1] + t[3 * c + 1 : 3 * c + 2] + t[3 * c + 2 : 3 * c + 3]
+                        value = own[c][j : j + 1] * t[9:10] - cross
+                        parts[pl.ds(first_row + c * chunks + j, 1), :] = value
             parts[2 * slots * DIM * chunks :, :] += stress[:8] + stress[8:]
 
         return 0
@@ -215,26 +211,49 @@
     lax.fori_loop(0, slots, one_tile, 0)
 
 
-def tile_parts(scalars, dissim, sources):
+def fetch_body(source, out, sem):
+    copy = pltpu.make_async_copy(source.at[0], out, sem)
+    copy.start()
+    copy.wait()
+
+
+def first_tile(dissim):
+    return pl.pallas_call(
+        fetch_body,
+        out_shape=pltpu.VMEM(dissim.shape[1:], dissim.dtype),
+        in_specs=[pl.BlockSpec(memory_space=pltpu.HBM)],
+        out_specs=pl.BlockSpec(memory_space=pltpu.VMEM),
+        scratch_shapes=[pltpu.SemaphoreType.DMA],
+        compiler_params=pltpu.CompilerParams(vmem_limit_bytes=SMALL_LIMIT),
+        name="first_tile",
+    )(pltpu.with_memory_space_constraint(dissim, pltpu.HBM))
+
+
+def tile_parts(scalars, dissim, first, sources):
     slots, rows, width = dissim.shape
     block_rows = DIM * width // LANES
     return pl.pallas_call(
         functools.partial(tile_body, rows, width),
         out_shape=jax.ShapeDtypeStruct((2 * slots * block_rows + 8, LANES), jnp.float32),
     in_specs=[pl.BlockSpec(memory_space=pltpu.SMEM), pl.BlockSpec(memory_space=pltpu.HBM)]
-        + [pl.BlockSpec(memory_space=pltpu.VMEM)] * 2,
+        + [pl.BlockSpec(memory_space=pltpu.VMEM)] * 3,
         out_specs=pl.BlockSpec(memory_space=pltpu.VMEM),
         scratch_shapes=[
             pltpu.VMEM((slots, rows, width), jnp.bfloat16),
-            pltpu.VMEM((16, rows), jnp.float32),
-            pltpu.VMEM((16, width), jnp.float32),
-            pltpu.VMEM((KDIM, rows), jnp.float32),
-            pltpu.VMEM((KDIM, width), jnp.float32),
+            pltpu.VMEM((16, rows // LANES, LANES), jnp.float32),
+            pltpu.VMEM((16, width // LANES, LANES), jnp.float32),
+            pltpu.VMEM((KDIM, rows // LANES, LANES), jnp.float32),
+            pltpu.VMEM((KDIM, width // LANES, LANES), jnp.float32),
             pltpu.SemaphoreType.DMA((slots,)),
         ],
         compiler_params=pltpu.CompilerParams(vmem_limit_bytes=VMEM_LIMIT),
         name="tile_parts",
-    )(scalars, pltpu.with_memory_space_constraint(dissim, pltpu.HBM), *sources)
+    )(
+        scalars,
+        pltpu.with_memory_space_constraint(dissim, pltpu.HBM),
+        pltpu.with_memory_space_constraint(first, pltpu.VMEM),
+        *sources,
+    )
 
 
 def gather_body(count, block_rows, where, *refs):
@@ -334,10 +353,14 @@
     block_rows = DIM * width // LANES
     for_tiles, where = tables(tile_list, holder, groups, devs, slots)
     plane = plane_groups(groups, devs)
-    sent = spread(from_line(coordinates, groups, devs), chips)
+    line = from_line(coordinates, groups, devs)
+    line[0] = coordinates.reshape(block_rows, LANES)
+    sent = spread(line, chips)
     own = lax.all_to_all(sent, AXES, 0, 0, tiled=True, axis_index_groups=plane)
+    own, dissim = lax.optimization_barrier((own, dissim))
     own = own.reshape(groups * chips, block_rows, LANES)
-    parts = tile_parts(for_tiles, dissim, [own, to_twin(own, groups * devs)])
+    twin = to_twin(own, groups * devs)
+    parts = tile_parts(for_tiles, dissim, first_tile(dissim), [own, twin])
     line = from_line(parts, groups, devs)
     line = line + [to_twin(a, groups * devs) for a in line]
     pieces = by_chip(where, line, chips)

time: 72.4 us -> 69.5 us (0.960)
  Pallas kernels: 10.9 us -> 7.86 us
  blocking collectives: 12.9 us -> 11.9 us
  waiting for transfers between devices: 16.8 us -> 17.8 us
    pallas_call x1, Pallas kernels: 8.18 us -> 3.54 us  [tile_parts(): pl.pallas_call(functools.partial(tile_body, rows, width), out_shape=jax.S...]
    ppermute x5, starting transfers between devices: 4.93 us -> 0.51 us  [to_twin(): return lax.ppermute(array, AXES, core_perm(devices))]
    ppermute x6, starting transfers between devices: 13.7 us -> 18.1 us  [from_line(): lax.ppermute(array, AXES, line_perm(groups, devs, d))]
    pallas_call x0 -> x1, Pallas kernels: none -> 1.6 us  [first_tile(): pl.pallas_call(fetch_body, out_shape=pltpu.VMEM(dissim.shape[1:], dissim....]
    ppermute x6, waiting for transfers between devices: 1.82 us -> 3.21 us  [from_line(): lax.ppermute(array, AXES, line_perm(groups, devs, d))]
    ppermute x5, waiting for transfers between devices: 2.69 us -> 1.4 us  [to_twin(): return lax.ppermute(array, AXES, core_perm(devices))]
    all_to_all x1, blocking collectives: 12.9 us -> 11.9 us  [on_device(): lax.all_to_all(pieces, AXES, 0, 0, tiled=True, axis_index_groups=plane)]
    all_to_all x1, waiting for transfers between devices: 12.3 us -> 13.2 us  [on_device(): own = lax.all_to_all(sent, AXES, 0, 0, tiled=True, axis_index_groups=plane)]
  transfers between devices with their start and end apart: 12 -> 12, of which waited for: 6 -> 7; matrix products, arithmetic and copies ran while one was open for 5% -> 6% of each run, Pallas kernels for 0% -> 2%
where the time goes in v4:
time: 69.5 us; the launch traced here: 69.1 us
  starting transfers between devices  26.6 us (38%)
  waiting for transfers between devices  17.8 us (26%)
  blocking collectives  11.9 us (17%)
  Pallas kernels  7.86 us (11%)
  local copies, waits for them, and re-layouts  2.66 us (4%)
  other arithmetic  1.48 us (2%)
  between operations  0.75 us (1%)
    ppermute x6, starting transfers between devices, from_line(): lax.ppermute(array, AXES, line_perm(groups, devs, d))  18.1 us
    all_to_all x1, waiting for transfers between devices, on_device(): own = lax.all_to_all(sent, AXES, 0, 0, tiled=True, axis_index_groups=plane)  13.2 us
    all_to_all x1, blocking collectives, on_device(): lax.all_to_all(pieces, AXES, 0, 0, tiled=True, axis_index_groups=plane)  11.9 us
    all_to_all x1, starting transfers between devices, on_device(): own = lax.all_to_all(sent, AXES, 0, 0, tiled=True, axis_index_groups=plane)  8.05 us
    pallas_call x1, Pallas kernels, tile_parts(): pl.pallas_call(functools.partial(tile_body, rows, width), out_shape=jax.S...  3.54 us
    ppermute x6, waiting for transfers between devices, from_line(): lax.ppermute(array, AXES, line_perm(groups, devs, d))  3.21 us
    pallas_call x1, Pallas kernels, first_tile(): pl.pallas_call(fetch_body, out_shape=pltpu.VMEM(dissim.shape[1:], dissim....  1.6 us
    ppermute x5, waiting for transfers between devices, to_twin(): return lax.ppermute(array, AXES, core_perm(devices))  1.4 us
  transfers between devices with their start and end apart: 12, of which 7 were waited for; matrix products, arithmetic and copies ran while one was open for 6% of the time, Pallas kernels for 2%

profile of v4, /device:TPU:0, one launch (start us, length us, event | category | flops | bytes accessed | tf_op | source)
XLA Modules:
  0.0 69.1 jit_solution(1292603844570516579)
XLA Ops:
  0.6 2.9 %collective-permute-start = (f32[3,1024]{1,0:T(4,128)}, f32[3,1024]{1,0:T(4,128)S(1)}, u32[]{:S(2)}, u32[]{:S(2)}) collective-permute-start(f32[3,1024]{1,0:T(4,128)} %param.6), channel_id=1, source_target_pairs={{32,0},{33,1},{34,2},{35,3},{36,4},{37,5},{38,6},{39,7},{40,8},{41... | collective-permute-start | bytes 36872 | tf_op jit(solution)/shard_map/ppermute | solution.py:49
  3.5 0.0 collective-permute-start.2
  3.5 2.3 %collective-permute-start.1 = (f32[3,1024]{1,0:T(4,128)}, f32[3,1024]{1,0:T(4,128)S(1)}, u32[]{:S(2)}, u32[]{:S(2)}) collective-permute-start(f32[3,1024]{1,0:T(4,128)} %param.6), channel_id=1, source_target_pairs={{64,0},{65,1},{66,2},{67,3},{68,4},{69,5},{70,6},{71,7},{72,8},{73... | collective-permute-start | bytes 36872 | tf_op jit(solution)/shard_map/ppermute | solution.py:49
  5.8 0.7 slice.16
  6.5 0.1 iota_add_fusion
  6.6 0.9 %select_reduce_fusion = s32[256,2]{0,1:T(2,128)S(1)} fusion(s32[128]{0:T(128)} %param.5, s32[256,2]{0,1:T(2,128)S(1)} %slice.16), kind=kLoop, calls=%fused_computation | loop fusion | flops 196096 | bytes 4608 | tf_op jit(solution)/shard_map/reduce_sum | solution.py:330
  7.5 0.7 %slice.15 = s32[256,1]{0,1:T(1,128)S(1)} slice(s32[256,3]{0,1:T(4,128)} %param.4), slice={[0:256], [2:3]} | slice | bytes 2048 | tf_op jit(solution)/shard_map/slice | solution.py:325
  8.2 0.7 %reshape.96.refs_0_ = f32[24,128]{1,0:T(8,128)S(1)} reshape(f32[3,1024]{1,0:T(4,128)} %param.6) | data formatting | bytes 24576 | tf_op jit(solution)/shard_map/reshape | solution.py:357
  8.9 0.1 add.108
  9.0 0.0 collective-permute-done.refs_1_
  9.0 0.0 collective-permute-done.2.refs_3_
  9.0 0.0 collective-permute-done.1.refs_2_
  9.0 1.0 %spread.1 = f32[16,96,128]{2,1,0:T(8,128)} custom-call(f32[24,128]{1,0:T(8,128)S(1)} %reshape.96.refs_0_, f32[3,1024]{1,0:T(4,128)S(1)} %collective-permute-done.refs_1_, f32[3,1024]{1,0:T(4,128)S(1)} %collective-permute-done.1.refs_2_, f32[3,1024]{1,0:T(4,128)S(1)} %collective-permute-done.2.refs_3_), custom_call_target="tpu_custom_call" | custom-call | tf_op jit(solution)/shard_map/spread/pallas_call | solution.py:69
  10.0 8.0 %all-to-all-start = ((f32[16,96,128]{2,1,0:T(8,128)}), f32[16,96,128]{2,1,0:T(8,128)S(1)}, u32[]{:S(2)}, u32[]{:S(2)}) async-start(f32[16,96,128]{2,1,0:T(8,128)} %spread.1), calls=%async_computation | async-start | bytes 1572864 | tf_op jit(solution)/shard_map/all_to_all | solution.py:359
  18.1 0.2 convert_reduce_fusion
  18.3 0.1 broadcast_compare_fusion
  18.3 13.2 %all-to-all-done = f32[16,96,128]{2,1,0:T(8,128)S(1)} async-done(((f32[16,96,128]{2,1,0:T(8,128)}), f32[16,96,128]{2,1,0:T(8,128)S(1)}, u32[]{:S(2)}, u32[]{:S(2)}) %all-to-all-start) | async-done | bytes 786464 | tf_op jit(solution)/shard_map/all_to_all | solution.py:359
  31.5 0.0 collective-permute-start.3
  31.5 0.1 select_reduce_fusion.1
  31.7 0.1 copy.9
  31.7 0.1 slice.18
  31.8 0.1 slice.19
  32.0 0.1 pad_add_fusion.sc
  32.0 1.6 %first_tile.1.first = bf16[1024,1024]{1,0:T(8,128)(2,1)S(1)} custom-call(bf16[4,1024,1024]{2,1,0:T(8,128)(2,1)} %delta_hbm), custom_call_target="tpu_custom_call" | custom-call | tf_op jit(solution)/shard_map/first_tile/pallas_call | solution.py:221
  33.6 0.2 collective-permute-done.3.refs_1_
  33.8 3.5 %tile_parts.1.refs_0_ = f32[200,128]{1,0:T(8,128)S(1)} custom-call(s32[20]{0:T(128)S(1)} %pad_add_fusion.sc, bf16[4,1024,1024]{2,1,0:T(8,128)(2,1)} %delta_hbm, bf16[1024,1024]{1,0:T(8,128)(2,1)S(1)} %first_tile.1.first, f32[64,24,128]{2,1,0:T(8,128)S(1)} %bitcast.5, f32[64,24,128]{2,1,0:T(8,128)S(1)} %collective-permute-done.3.refs_1_), custom_call_target="tpu_custom_call" | custom-call | tf_op jit(solution)/shard_map/tile_parts/pallas_call | solution.py:235
  37.4 10.1 %collective-permute-start.6 = (f32[200,128]{1,0:T(8,128)S(1)}, f32[200,128]{1,0:T(8,128)S(1)}, u32[]{:S(2)}, u32[]{:S(2)}) collective-permute-start(f32[200,128]{1,0:T(8,128)S(1)} %tile_parts.1.refs_0_), channel_id=1, source_target_pairs={{96,0},{97,1},{98,2},{99,3},{100,4},{101,5},{102,6},{103,7},{104,8... | collective-permute-start | bytes 307208 | tf_op jit(solution)/shard_map/ppermute | solution.py:49
  47.4 2.0 %collective-permute-start.5 = (f32[200,128]{1,0:T(8,128)S(1)}, f32[200,128]{1,0:T(8,128)S(1)}, u32[]{:S(2)}, u32[]{:S(2)}) collective-permute-start(f32[200,128]{1,0:T(8,128)S(1)} %tile_parts.1.refs_0_), channel_id=1, source_target_pairs={{64,0},{65,1},{66,2},{67,3},{68,4},{69,5},{70,6},{71,7},{72,8},{73... | collective-permute-start | bytes 307208 | tf_op jit(solution)/shard_map/ppermute | solution.py:49
  49.4 0.8 %collective-permute-start.4 = (f32[200,128]{1,0:T(8,128)S(1)}, f32[200,128]{1,0:T(8,128)S(1)}, u32[]{:S(2)}, u32[]{:S(2)}) collective-permute-start(f32[200,128]{1,0:T(8,128)S(1)} %tile_parts.1.refs_0_), channel_id=1, source_target_pairs={{32,0},{33,1},{34,2},{35,3},{36,4},{37,5},{38,6},{39,7},{40,8},{41... | collective-permute-start | bytes 307208 | tf_op jit(solution)/shard_map/ppermute | solution.py:49
  50.2 0.1 copy.8
  50.3 0.1 sub.32
  50.4 0.1 collective-permute-start.7
  50.5 0.1 collective-permute-done.6.refs_3_
  50.6 0.4 collective-permute-start.10
  51.0 2.6 %collective-permute-done.5.refs_2_ = f32[200,128]{1,0:T(8,128)S(1)} collective-permute-done((f32[200,128]{1,0:T(8,128)S(1)}, f32[200,128]{1,0:T(8,128)S(1)}, u32[]{:S(2)}, u32[]{:S(2)}) %collective-permute-start.5) | collective-permute-done | bytes 102432 | tf_op jit(solution)/shard_map/ppermute | solution.py:49
  53.6 0.0 collective-permute-start.9
  53.6 0.5 collective-permute-done.4.refs_1_
  54.1 0.0 collective-permute-start.8
  54.1 0.0 collective-permute-done.7.refs_4_
  54.2 0.0 collective-permute-done.10.refs_7_
  54.2 0.8 %collective-permute-done.9.refs_6_ = f32[200,128]{1,0:T(8,128)S(1)} collective-permute-done((f32[200,128]{1,0:T(8,128)S(1)}, f32[200,128]{1,0:T(8,128)S(1)}, u32[]{:S(2)}, u32[]{:S(2)}) %collective-permute-start.9) | collective-permute-done | bytes 102432 | tf_op jit(solution)/shard_map/ppermute | solution.py:44
  54.9 0.5 collective-permute-done.8.refs_5_
  55.4 1.1 %by_chip.1 = f32[16,32,128]{2,1,0:T(8,128)S(1)} custom-call(s32[64]{0:T(128)S(1)} %and_select_fusion.7.where, f32[200,128]{1,0:T(8,128)S(1)} %tile_parts.1.refs_0_, f32[200,128]{1,0:T(8,128)S(1)} %collective-permute-done.4.refs_1_, f32[200,128]{1,0:T(8,128)S(1)} %collective-permute-done.5.refs_2_, f32[200,128]{1,0:T(8,128)S(1)} %collective-permute-done.6.refs_3_, ...), custom_call_target="tpu_custom_call" | custom-call | tf_op jit(solution)/shard_map/by_chip/pallas_call | solution.py:282
  56.5 11.9 %all_to_all.10.pieces = f32[16,32,128]{2,1,0:T(8,128)S(1)} all-to-all(f32[16,32,128]{2,1,0:T(8,128)S(1)} %by_chip.1), channel_id=1, replica_groups={{0,2,4,6,8,10,12,14,16,18,20,22,24,26,28,30},{1,3,5,7,9,11,13,15,17,19,..., dimensions={0} | all-to-all | bytes 524288 | tf_op jit(solution)/shard_map/all_to_all | solution.py:367
  68.4 0.6 total.1
  (7 shorter events, 0.1 us)
Async XLA Ops:
  0.6 8.4 %collective-permute-start = (f32[3,1024]{1,0:T(4,128)}, f32[3,1024]{1,0:T(4,128)S(1)}, u32[]{:S(2)}, u32[]{:S(2)}) collective-permute-start(f32[3,1024]{1,0:T(4,128)} %param.6), channel_id=1, source_target_pairs={{32,0},{33,1},{34,2},{35,3},{36,4},{37,5},{38,6},{39,7},{40,8},{41... | collective-permute-start | bytes 36872 | tf_op jit(solution)/shard_map/ppermute | solution.py:49
  3.5 5.5 %collective-permute-start.2 = (f32[3,1024]{1,0:T(4,128)}, f32[3,1024]{1,0:T(4,128)S(1)}, u32[]{:S(2)}, u32[]{:S(2)}) collective-permute-start(f32[3,1024]{1,0:T(4,128)} %param.6), channel_id=1, source_target_pairs={{96,0},{97,1},{98,2},{99,3},{100,4},{101,5},{102,6},{103,7},{104,8... | collective-permute-start | bytes 36872 | tf_op jit(solution)/shard_map/ppermute | solution.py:49
  3.5 5.5 %collective-permute-start.1 = (f32[3,1024]{1,0:T(4,128)}, f32[3,1024]{1,0:T(4,128)S(1)}, u32[]{:S(2)}, u32[]{:S(2)}) collective-permute-start(f32[3,1024]{1,0:T(4,128)} %param.6), channel_id=1, source_target_pairs={{64,0},{65,1},{66,2},{67,3},{68,4},{69,5},{70,6},{71,7},{72,8},{73... | collective-permute-start | bytes 36872 | tf_op jit(solution)/shard_map/ppermute | solution.py:49
  10.0 21.5 %all-to-all-start = ((f32[16,96,128]{2,1,0:T(8,128)}), f32[16,96,128]{2,1,0:T(8,128)S(1)}, u32[]{:S(2)}, u32[]{:S(2)}) async-start(f32[16,96,128]{2,1,0:T(8,128)} %spread.1), calls=%async_computation | async-start | bytes 1572864 | tf_op jit(solution)/shard_map/all_to_all | solution.py:359
  31.5 2.3 %collective-permute-start.3 = (f32[64,24,128]{2,1,0:T(8,128)S(1)}, f32[64,24,128]{2,1,0:T(8,128)S(1)}, u32[]{:S(2)}, u32[]{:S(2)}) collective-permute-start(f32[64,24,128]{2,1,0:T(8,128)S(1)} %bitcast.4), channel_id=1, source_target_pairs={{0,1},{1,0},{2,3},{3,2},{4,5},{5,4},{6,7},{7,6},{8,9},{9,8},{10,11... | collective-permute-start | bytes 2359304 | tf_op jit(solution)/shard_map/ppermute | solution.py:44
  37.4 13.3 %collective-permute-start.6 = (f32[200,128]{1,0:T(8,128)S(1)}, f32[200,128]{1,0:T(8,128)S(1)}, u32[]{:S(2)}, u32[]{:S(2)}) collective-permute-start(f32[200,128]{1,0:T(8,128)S(1)} %tile_parts.1.refs_0_), channel_id=1, source_target_pairs={{96,0},{97,1},{98,2},{99,3},{100,4},{101,5},{102,6},{103,7},{104,8... | collective-permute-start | bytes 307208 | tf_op jit(solution)/shard_map/ppermute | solution.py:49
  47.4 6.2 %collective-permute-start.5 = (f32[200,128]{1,0:T(8,128)S(1)}, f32[200,128]{1,0:T(8,128)S(1)}, u32[]{:S(2)}, u32[]{:S(2)}) collective-permute-start(f32[200,128]{1,0:T(8,128)S(1)} %tile_parts.1.refs_0_), channel_id=1, source_target_pairs={{64,0},{65,1},{66,2},{67,3},{68,4},{69,5},{70,6},{71,7},{72,8},{73... | collective-permute-start | bytes 307208 | tf_op jit(solution)/shard_map/ppermute | solution.py:49
  49.4 4.7 %collective-permute-start.4 = (f32[200,128]{1,0:T(8,128)S(1)}, f32[200,128]{1,0:T(8,128)S(1)}, u32[]{:S(2)}, u32[]{:S(2)}) collective-permute-start(f32[200,128]{1,0:T(8,128)S(1)} %tile_parts.1.refs_0_), channel_id=1, source_target_pairs={{32,0},{33,1},{34,2},{35,3},{36,4},{37,5},{38,6},{39,7},{40,8},{41... | collective-permute-start | bytes 307208 | tf_op jit(solution)/shard_map/ppermute | solution.py:49
  50.4 3.7 %collective-permute-start.7 = (f32[200,128]{1,0:T(8,128)S(1)}, f32[200,128]{1,0:T(8,128)S(1)}, u32[]{:S(2)}, u32[]{:S(2)}) collective-permute-start(f32[200,128]{1,0:T(8,128)S(1)} %tile_parts.1.refs_0_), channel_id=1, source_target_pairs={{0,1},{1,0},{2,3},{3,2},{4,5},{5,4},{6,7},{7,6},{8,9},{9,8},{10,11... | collective-permute-start | bytes 307208 | tf_op jit(solution)/shard_map/ppermute | solution.py:44
  50.6 3.6 %collective-permute-start.10 = (f32[200,128]{1,0:T(8,128)S(1)}, f32[200,128]{1,0:T(8,128)S(1)}, u32[]{:S(2)}, u32[]{:S(2)}) collective-permute-start(f32[200,128]{1,0:T(8,128)S(1)} %collective-permute-done.6.refs_3_), channel_id=1, source_target_pairs={{0,1},{1,0},{2,3},{3,2},{4,5},{5,4},{6,7},{7,6},{8,9},{9,8},{10,11... | collective-permute-start | bytes 307208 | tf_op jit(solution)/shard_map/ppermute | solution.py:44
  53.6 1.3 %collective-permute-start.9 = (f32[200,128]{1,0:T(8,128)S(1)}, f32[200,128]{1,0:T(8,128)S(1)}, u32[]{:S(2)}, u32[]{:S(2)}) collective-permute-start(f32[200,128]{1,0:T(8,128)S(1)} %collective-permute-done.5.refs_2_), channel_id=1, source_target_pairs={{0,1},{1,0},{2,3},{3,2},{4,5},{5,4},{6,7},{7,6},{8,9},{9,8},{10,11... | collective-permute-start | bytes 307208 | tf_op jit(solution)/shard_map/ppermute | solution.py:44
  54.1 1.3 %collective-permute-start.8 = (f32[200,128]{1,0:T(8,128)S(1)}, f32[200,128]{1,0:T(8,128)S(1)}, u32[]{:S(2)}, u32[]{:S(2)}) collective-permute-start(f32[200,128]{1,0:T(8,128)S(1)} %collective-permute-done.4.refs_1_), channel_id=1, source_target_pairs={{0,1},{1,0},{2,3},{3,2},{4,5},{5,4},{6,7},{7,6},{8,9},{9,8},{10,11... | collective-permute-start | bytes 307208 | tf_op jit(solution)/shard_map/ppermute | solution.py:44

commit v5 on v4

--- a/solution.py
+++ b/solution.py
@@ -94,7 +94,7 @@
     def delta_copy(k):
         return pltpu.make_async_copy(delta_hbm.at[k], delta.at[k], delta_sem.at[k])
 
-    @pl.when(sc[0] > 0)
+    @pl.when(sc[6, 0] > 0)
     def _():
         pltpu.make_async_copy(first, delta.at[0], delta_sem.at[0]).start()
 
@@ -104,18 +104,18 @@
         ref[...] = jnp.zeros(ref.shape, f32)
 
     def one_tile(k, _):
-        @pl.when(sc[k] > 0)
+        @pl.when(sc[6, k] > 0)
         def _():
             delta_copy(k).wait()
             later = jnp.minimum(k + 1, slots - 1)
-            pl.when((k + 1 < slots) & (sc[later] > 0))(lambda: delta_copy(later).start())
-
-            def block(i):
-                twin, at = sc[slots + i] > 0, sc[3 * slots + i]
+            pl.when((k + 1 < slots) & (sc[6, later] > 0))(lambda: delta_copy(later).start())
+
+            def block(side):
+                twin, at = sc[4 + side, k] > 0, sc[side, k]
                 found = jnp.where(twin, sources[1][at], sources[0][at])
                 return [found[c * chunks : (c + 1) * chunks, :] for c in range(DIM)]
 
-            xa, xb = block(2 * k), block(2 * k + 1)
+            xa, xb = block(0), block(1)
             mean = [jnp.sum(a, keepdims=True) * (1.0 / width) for a in xa]
             xa = [a - m for a, m in zip(xa, mean)]
             xb = [b - m for b, m in zip(xb, mean)]
@@ -266,7 +266,7 @@
         out[chip, block_rows:, :] = stress
     for s in range(len(sources)):
         for i in range(count):
-            chip = where[s * count + i]
+            chip = where[2 + i % 2, s * (count // 2) + i // 2]
 
             @pl.when(chip >= 0)
             def _(s=s, i=i, chip=chip):
@@ -275,9 +275,9 @@
                 ]
 
 
-def by_chip(where, sources, chips):
+def by_chip(where, sources, chips, slots):
     rows = sources[0].shape[0] - 8
-    count = where.shape[0] // len(sources)
+    count = 2 * slots
     block_rows = rows // count
     return pl.pallas_call(
         functools.partial(gather_body, count, block_rows),
@@ -320,29 +320,80 @@
     )(pieces)
 
 
-def tables(tile_list, holder, groups, devs, slots):
+def tables_body(groups, devs, slots, tiles_hbm, holder_hbm, coords_hbm, out, own, *scratch):
+    tiles, holder, coords, sem = scratch
+    copies = [
+        pltpu.make_async_copy(source, target, sem.at[i])
+        for i, (source, target) in enumerate(
+            ((tiles_hbm, tiles), (holder_hbm, holder), (coords_hbm, coords))
+        )
+    ]
+    for copy in copies:
+        copy.start()
+    for copy in copies:
+        copy.wait()
+    chunks = coords.shape[1] // LANES
+    for c in range(DIM):
+        for j in range(chunks):
+            own[c * chunks + j : c * chunks + j + 1, :] = coords[
+                c : c + 1, j * LANES : (j + 1) * LANES
+            ]
+    f32, i32 = jnp.float32, jnp.int32
     group, dev = lax.axis_index("grp"), lax.axis_index("dev")
-    owners = tile_list[:, 2]
-    indices = jnp.arange(owners.shape[0], dtype=jnp.int32)
-    earlier = (owners[:, None] == owners[None, :]) & (indices[None, :] < indices[:, None])
-    rank = jnp.sum(earlier.astype(jnp.int32), axis=1)
-    blocks = jnp.arange(holder.shape[0], dtype=jnp.int32)
-    position = jnp.sum(
-        jnp.where(tile_list[:, :2, None] == blocks, holder, 0), axis=2
+    count, blocks = tiles.shape[1], holder.shape[1]
+    bits = devs.bit_length() - 1
+
+    def column(row):
+        return jnp.transpose(jnp.broadcast_to(row, (LANES, count)))[:, :1]
+
+    owner = column(tiles[2:3, :])
+    same = owner == tiles[2:3, :]
+    later = lax.broadcasted_iota(i32, (count, count), 0) > lax.broadcasted_iota(
+        i32, (count, count), 1
     )
-    order = jnp.arange(2 * groups, dtype=jnp.int32)
-    line = (group + order) % groups * devs + (dev ^ (order // groups))
-    wanted = (line[:, None] * slots + jnp.arange(slots, dtype=jnp.int32)).reshape(-1)
-    chosen = wanted[:, None] == (owners * slots + rank)[None, :]
-    held = jnp.sum(jnp.where(chosen[:, :, None], position + 1, 0), axis=1).reshape(-1) - 1
-    mine = held[: 2 * slots]
-    present = (mine[::2] >= 0).astype(jnp.int32)
-    at = jnp.maximum(mine, 0)
-    place = at % devs // 2 * groups + (at // devs - group) % groups
-    for_tiles = jnp.concatenate([present, at % 2 ^ dev % 2, place])
-    here = (held >= 0) & (held // devs == group) & (held % 2 == dev % 2)
-    where = jnp.where(here, held % devs // 2, -1)
-    return for_tiles, where
+    rank = jnp.sum(jnp.where(same & later, 1.0, 0.0), axis=1, keepdims=True)
+    code = owner.astype(f32) * slots + rank
+    lane = lax.broadcasted_iota(i32, (1, LANES), 1)
+    order = lane // slots
+    line = ((group + order) & (groups - 1)) * devs + (dev ^ (order // groups))
+    wanted = (line * slots + (lane & (slots - 1))).astype(f32)
+    chosen = (code == wanted) & (lane < 2 * groups * slots)
+    numbers = lax.broadcasted_iota(i32, (count, blocks), 1)
+    places = holder[...].astype(f32) + 1.0
+    rows = []
+    for side in range(2):
+        found = jnp.where(column(tiles[side : side + 1, :]) == numbers, places, 0.0)
+        found = jnp.sum(found, axis=1, keepdims=True)
+        rows.append(jnp.sum(jnp.where(chosen, found, 0.0), axis=0, keepdims=True))
+    held = [r.astype(i32) - 1 for r in rows]
+    at = [jnp.maximum(h, 0) for h in held]
+    chip = [(a & (devs - 1)) >> 1 for a in at]
+    from_group = [(a >> bits) - group & (groups - 1) for a in at]
+    twin = [(a ^ dev) & 1 for a in at]
+    for side in range(2):
+        here = (held[side] >= 0) & (from_group[side] == 0) & (twin[side] == 0)
+        out[side : side + 1, :] = chip[side] * groups + from_group[side]
+        out[2 + side : 3 + side, :] = jnp.where(here, chip[side], -1)
+        out[4 + side : 5 + side, :] = twin[side]
+    out[6:7, :] = jnp.where(held[0] >= 0, 1, 0)
+    out[7:8, :] = jnp.zeros((1, LANES), i32)
+
+
+def tables(tile_list, holder, coordinates, groups, devs, slots):
+    arrays = [tile_list.T, holder.reshape(1, -1), coordinates]
+    return pl.pallas_call(
+        functools.partial(tables_body, groups, devs, slots),
+        out_shape=(
+            jax.ShapeDtypeStruct((8, LANES), jnp.int32),
+            jax.ShapeDtypeStruct((coordinates.size // LANES, LANES), jnp.float32),
+        ),
+        in_specs=[pl.BlockSpec(memory_space=pltpu.HBM)] * 3,
+        out_specs=[pl.BlockSpec(memory_space=pltpu.VMEM)] * 2,
+        scratch_shapes=[pltpu.VMEM(a.shape, a.dtype) for a in arrays]
+        + [pltpu.SemaphoreType.DMA((3,))],
+        compiler_params=pltpu.CompilerParams(vmem_limit_bytes=SMALL_LIMIT),
+        name="tables",
+    )(*[pltpu.with_memory_space_constraint(a, pltpu.HBM) for a in arrays])
 
 
 def on_device(tile_list, holder, coordinates, dissim):
@@ -351,19 +402,19 @@
     width = coordinates.shape[1]
     slots = dissim.shape[0]
     block_rows = DIM * width // LANES
-    for_tiles, where = tables(tile_list, holder, groups, devs, slots)
+    places, rows = tables(tile_list, holder, coordinates, groups, devs, slots)
     plane = plane_groups(groups, devs)
     line = from_line(coordinates, groups, devs)
-    line[0] = coordinates.reshape(block_rows, LANES)
+    line[0] = rows
     sent = spread(line, chips)
     own = lax.all_to_all(sent, AXES, 0, 0, tiled=True, axis_index_groups=plane)
     own, dissim = lax.optimization_barrier((own, dissim))
     own = own.reshape(groups * chips, block_rows, LANES)
     twin = to_twin(own, groups * devs)
-    parts = tile_parts(for_tiles, dissim, first_tile(dissim), [own, twin])
+    parts = tile_parts(places, dissim, first_tile(dissim), [own, twin])
     line = from_line(parts, groups, devs)
     line = line + [to_twin(a, groups * devs) for a in line]
-    pieces = by_chip(where, line, chips)
+    pieces = by_chip(places, line, chips, slots)
     pieces = lax.all_to_all(pieces, AXES, 0, 0, tiled=True, axis_index_groups=plane)
     guttman, stress = total_of(pieces, width)
     return guttman, stress[0, 0]

time: 69.5 us -> 68.5 us (0.986)
  blocking collectives: 11.9 us -> 32.8 us
  starting transfers between devices: 26.6 us -> 9.69 us
  waiting for transfers between devices: 17.8 us -> 8.25 us
  Pallas kernels: 7.86 us -> 16.8 us
  local copies, waits for them, and re-layouts: 2.66 us -> 0 us
  other arithmetic: 1.48 us -> 0 us
    all_to_all x0 -> x1, blocking collectives: none -> 20.5 us  [on_device(): own = lax.all_to_all(sent, AXES, 0, 0, tiled=True, axis_index_groups=plane)]
    all_to_all x1 -> x0, waiting for transfers between devices: 13.2 us -> none  [on_device(): own = lax.all_to_all(sent, AXES, 0, 0, tiled=True, axis_index_groups=plane)]
    ppermute x6, starting transfers between devices: 18.1 us -> 9.68 us  [from_line(): lax.ppermute(array, AXES, line_perm(groups, devs, d))]
    pallas_call x1, Pallas kernels: 3.54 us -> 11.8 us  [tile_parts(): pl.pallas_call(functools.partial(tile_body, rows, width), out_shape=jax.S...]
    all_to_all x1 -> x0, starting transfers between devices: 8.05 us -> none  [on_device(): own = lax.all_to_all(sent, AXES, 0, 0, tiled=True, axis_index_groups=plane)]
    ppermute x6, waiting for transfers between devices: 3.21 us -> 6.27 us  [from_line(): lax.ppermute(array, AXES, line_perm(groups, devs, d))]
    slice x5 -> x0, local copies, waits for them, and re-layouts: 1.66 us -> none  [the longest x1 0.7 us: tables(): owners = tile_list[:, 2]]
    pallas_call x0 -> x1, Pallas kernels: none -> 1.52 us  [tables(): pl.pallas_call(functools.partial(tables_body, groups, devs, slots), out_s...]
  transfers between devices with their start and end apart: 12 -> 11, of which waited for: 7 -> 8; matrix products, arithmetic and copies ran while one was open for 6% -> 0% of each run, Pallas kernels for 2% -> 5%
where the time goes in v5:
time: 68.5 us; the launch traced here: 68.2 us
  blocking collectives  32.8 us (48%)
  Pallas kernels  16.8 us (25%)
  starting transfers between devices  9.69 us (14%)
  waiting for transfers between devices  8.25 us (12%)
  between operations  0.7 us (1%)
    all_to_all x1, blocking collectives, on_device(): own = lax.all_to_all(sent, AXES, 0, 0, tiled=True, axis_index_groups=plane)  20.5 us
    all_to_all x1, blocking collectives, on_device(): lax.all_to_all(pieces, AXES, 0, 0, tiled=True, axis_index_groups=plane)  12.2 us
    pallas_call x1, Pallas kernels, tile_parts(): pl.pallas_call(functools.partial(tile_body, rows, width), out_shape=jax.S...  11.8 us
    ppermute x6, starting transfers between devices, from_line(): lax.ppermute(array, AXES, line_perm(groups, devs, d))  9.68 us
    ppermute x6, waiting for transfers between devices, from_line(): lax.ppermute(array, AXES, line_perm(groups, devs, d))  6.27 us
    ppermute x5, waiting for transfers between devices, to_twin(): return lax.ppermute(array, AXES, core_perm(devices))  1.97 us
    pallas_call x1, Pallas kernels, first_tile(): pl.pallas_call(fetch_body, out_shape=pltpu.VMEM(dissim.shape[1:], dissim....  1.6 us
    pallas_call x1, Pallas kernels, tables(): pl.pallas_call(functools.partial(tables_body, groups, devs, slots), out_s...  1.52 us
  transfers between devices with their start and end apart: 11, of which 8 were waited for; matrix products, arithmetic and copies ran while one was open for 0% of the time, Pallas kernels for 5%

profile of v5, /device:TPU:0, one launch (start us, length us, event | category | flops | bytes accessed | tf_op | source)
XLA Modules:
  0.0 68.2 jit_solution(10534229356875513318)
XLA Ops:
  0.6 2.9 %collective-permute-start = (f32[3,1024]{1,0:T(4,128)}, f32[3,1024]{1,0:T(4,128)S(1)}, u32[]{:S(2)}, u32[]{:S(2)}) collective-permute-start(f32[3,1024]{1,0:T(4,128)} %coords_hbm.1), channel_id=1, source_target_pairs={{32,0},{33,1},{34,2},{35,3},{36,4},{37,5},{38,6},{39,7},{40,8},{41... | collective-permute-start | bytes 36872 | tf_op jit(solution)/shard_map/ppermute | solution.py:49
  3.5 0.0 collective-permute-start.2
  3.5 2.3 %collective-permute-start.1 = (f32[3,1024]{1,0:T(4,128)}, f32[3,1024]{1,0:T(4,128)S(1)}, u32[]{:S(2)}, u32[]{:S(2)}) collective-permute-start(f32[3,1024]{1,0:T(4,128)} %coords_hbm.1), channel_id=1, source_target_pairs={{64,0},{65,1},{66,2},{67,3},{68,4},{69,5},{70,6},{71,7},{72,8},{73... | collective-permute-start | bytes 36872 | tf_op jit(solution)/shard_map/ppermute | solution.py:49
  5.8 1.5 %tables.1 = (s32[8,128]{1,0:T(8,128)S(1)}, f32[24,128]{1,0:T(8,128)S(1)}) custom-call(s32[3,256]{1,0:T(4,128)} %bitcast.6, s32[1,128]{1,0:T(1,128)} %bitcast.7, f32[3,1024]{1,0:T(4,128)} %coords_hbm.1), custom_call_target="tpu_custom_call" | custom-call | tf_op jit(solution)/shard_map/tables/pallas_call | solution.py:384
  7.4 0.0 collective-permute-done.refs_1_
  7.4 1.3 %collective-permute-done.2.refs_3_ = f32[3,1024]{1,0:T(4,128)S(1)} collective-permute-done((f32[3,1024]{1,0:T(4,128)}, f32[3,1024]{1,0:T(4,128)S(1)}, u32[]{:S(2)}, u32[]{:S(2)}) %collective-permute-start.2) | collective-permute-done | bytes 12320 | tf_op jit(solution)/shard_map/ppermute | solution.py:49
  8.7 0.3 collective-permute-done.1.refs_2_
  9.0 0.1 spread.1
  9.1 20.5 %all_to_all.10 = f32[16,96,128]{2,1,0:T(8,128)S(1)} all-to-all(f32[16,96,128]{2,1,0:T(8,128)S(1)} %spread.1), channel_id=1, replica_groups={{0,2,4,6,8,10,12,14,16,18,20,22,24,26,28,30},{1,3,5,7,9,11,13,15,17,19,..., dimensions={0} | all-to-all | bytes 1572864 | tf_op jit(solution)/shard_map/all_to_all | solution.py:410
  29.6 0.0 collective-permute-start.3
  29.6 1.6 %first_tile.1.first = bf16[1024,1024]{1,0:T(8,128)(2,1)S(1)} custom-call(bf16[4,1024,1024]{2,1,0:T(8,128)(2,1)} %delta_hbm), custom_call_target="tpu_custom_call" | custom-call | tf_op jit(solution)/shard_map/first_tile/pallas_call | solution.py:221
  31.2 0.7 collective-permute-done.3.refs_1_
  31.9 11.8 %tile_parts.1.refs_0_ = f32[200,128]{1,0:T(8,128)S(1)} custom-call(s32[8,128]{1,0:T(8,128)S(1)} %get-tuple-element.8.sc.where, bf16[4,1024,1024]{2,1,0:T(8,128)(2,1)} %delta_hbm, bf16[1024,1024]{1,0:T(8,128)(2,1)S(1)} %first_tile.1.first, f32[64,24,128]{2,1,0:T(8,128)S(1)} %bitcast.5, f32[64,24,128]{2,1,0:T(8,128)S(1)} %collective-permute-done.3.refs_1_), custom_call_target="tpu_custom_call" | custom-call | tf_op jit(solution)/shard_map/tile_parts/pallas_call | solution.py:235
  43.7 0.1 collective-permute-start.6
  43.8 4.4 %collective-permute-start.5 = (f32[200,128]{1,0:T(8,128)S(1)}, f32[200,128]{1,0:T(8,128)S(1)}, u32[]{:S(2)}, u32[]{:S(2)}) collective-permute-start(f32[200,128]{1,0:T(8,128)S(1)} %tile_parts.1.refs_0_), channel_id=1, source_target_pairs={{64,0},{65,1},{66,2},{67,3},{68,4},{69,5},{70,6},{71,7},{72,8},{73... | collective-permute-start | bytes 307208 | tf_op jit(solution)/shard_map/ppermute | solution.py:49
  48.2 0.0 collective-permute-start.4
  48.2 0.0 collective-permute-start.7
  48.2 1.9 %collective-permute-done.6.refs_3_ = f32[200,128]{1,0:T(8,128)S(1)} collective-permute-done((f32[200,128]{1,0:T(8,128)S(1)}, f32[200,128]{1,0:T(8,128)S(1)}, u32[]{:S(2)}, u32[]{:S(2)}) %collective-permute-start.6) | collective-permute-done | bytes 102432 | tf_op jit(solution)/shard_map/ppermute | solution.py:49
  50.1 0.0 collective-permute-start.10
  50.1 1.9 %collective-permute-done.5.refs_2_ = f32[200,128]{1,0:T(8,128)S(1)} collective-permute-done((f32[200,128]{1,0:T(8,128)S(1)}, f32[200,128]{1,0:T(8,128)S(1)}, u32[]{:S(2)}, u32[]{:S(2)}) %collective-permute-start.5) | collective-permute-done | bytes 102432 | tf_op jit(solution)/shard_map/ppermute | solution.py:49
  51.9 0.0 collective-permute-start.9
  51.9 0.9 %collective-permute-done.4.refs_1_ = f32[200,128]{1,0:T(8,128)S(1)} collective-permute-done((f32[200,128]{1,0:T(8,128)S(1)}, f32[200,128]{1,0:T(8,128)S(1)}, u32[]{:S(2)}, u32[]{:S(2)}) %collective-permute-start.4) | collective-permute-done | bytes 102432 | tf_op jit(solution)/shard_map/ppermute | solution.py:49
  52.9 0.0 collective-permute-start.8
  52.9 0.0 collective-permute-done.7.refs_4_
  52.9 0.0 collective-permute-done.10.refs_7_
  52.9 0.4 collective-permute-done.9.refs_6_
  53.2 0.9 %collective-permute-done.8.refs_5_ = f32[200,128]{1,0:T(8,128)S(1)} collective-permute-done((f32[200,128]{1,0:T(8,128)S(1)}, f32[200,128]{1,0:T(8,128)S(1)}, u32[]{:S(2)}, u32[]{:S(2)}) %collective-permute-start.8) | collective-permute-done | bytes 102432 | tf_op jit(solution)/shard_map/ppermute | solution.py:44
  54.2 1.1 %by_chip.1 = f32[16,32,128]{2,1,0:T(8,128)S(1)} custom-call(s32[8,128]{1,0:T(8,128)S(1)} %get-tuple-element.8.sc.where, f32[200,128]{1,0:T(8,128)S(1)} %tile_parts.1.refs_0_, f32[200,128]{1,0:T(8,128)S(1)} %collective-permute-done.4.refs_1_, f32[200,128]{1,0:T(8,128)S(1)} %collective-permute-done.5.refs_2_, f32[200,128]{1,0:T(8,128)S(1)} %collective-permute-done.6.refs_3_, ...), custom_call_target="tpu_custom_call" | custom-call | tf_op jit(solution)/shard_map/by_chip/pallas_call | solution.py:282
  55.3 12.2 %all_to_all.11.pieces = f32[16,32,128]{2,1,0:T(8,128)S(1)} all-to-all(f32[16,32,128]{2,1,0:T(8,128)S(1)} %by_chip.1), channel_id=1, replica_groups={{0,2,4,6,8,10,12,14,16,18,20,22,24,26,28,30},{1,3,5,7,9,11,13,15,17,19,..., dimensions={0} | all-to-all | bytes 524288 | tf_op jit(solution)/shard_map/all_to_all | solution.py:418
  67.6 0.6 total.1
Async XLA Ops:
  0.6 6.7 %collective-permute-start = (f32[3,1024]{1,0:T(4,128)}, f32[3,1024]{1,0:T(4,128)S(1)}, u32[]{:S(2)}, u32[]{:S(2)}) collective-permute-start(f32[3,1024]{1,0:T(4,128)} %coords_hbm.1), channel_id=1, source_target_pairs={{32,0},{33,1},{34,2},{35,3},{36,4},{37,5},{38,6},{39,7},{40,8},{41... | collective-permute-start | bytes 36872 | tf_op jit(solution)/shard_map/ppermute | solution.py:49
  3.5 5.2 %collective-permute-start.2 = (f32[3,1024]{1,0:T(4,128)}, f32[3,1024]{1,0:T(4,128)S(1)}, u32[]{:S(2)}, u32[]{:S(2)}) collective-permute-start(f32[3,1024]{1,0:T(4,128)} %coords_hbm.1), channel_id=1, source_target_pairs={{96,0},{97,1},{98,2},{99,3},{100,4},{101,5},{102,6},{103,7},{104,8... | collective-permute-start | bytes 36872 | tf_op jit(solution)/shard_map/ppermute | solution.py:49
  3.5 5.5 %collective-permute-start.1 = (f32[3,1024]{1,0:T(4,128)}, f32[3,1024]{1,0:T(4,128)S(1)}, u32[]{:S(2)}, u32[]{:S(2)}) collective-permute-start(f32[3,1024]{1,0:T(4,128)} %coords_hbm.1), channel_id=1, source_target_pairs={{64,0},{65,1},{66,2},{67,3},{68,4},{69,5},{70,6},{71,7},{72,8},{73... | collective-permute-start | bytes 36872 | tf_op jit(solution)/shard_map/ppermute | solution.py:49
  29.6 2.3 %collective-permute-start.3 = (f32[64,24,128]{2,1,0:T(8,128)S(1)}, f32[64,24,128]{2,1,0:T(8,128)S(1)}, u32[]{:S(2)}, u32[]{:S(2)}) collective-permute-start(f32[64,24,128]{2,1,0:T(8,128)S(1)} %bitcast.4), channel_id=1, source_target_pairs={{0,1},{1,0},{2,3},{3,2},{4,5},{5,4},{6,7},{7,6},{8,9},{9,8},{10,11... | collective-permute-start | bytes 2359304 | tf_op jit(solution)/shard_map/ppermute | solution.py:44
  43.7 6.4 %collective-permute-start.6 = (f32[200,128]{1,0:T(8,128)S(1)}, f32[200,128]{1,0:T(8,128)S(1)}, u32[]{:S(2)}, u32[]{:S(2)}) collective-permute-start(f32[200,128]{1,0:T(8,128)S(1)} %tile_parts.1.refs_0_), channel_id=1, source_target_pairs={{96,0},{97,1},{98,2},{99,3},{100,4},{101,5},{102,6},{103,7},{104,8... | collective-permute-start | bytes 307208 | tf_op jit(solution)/shard_map/ppermute | solution.py:49
  43.8 8.1 %collective-permute-start.5 = (f32[200,128]{1,0:T(8,128)S(1)}, f32[200,128]{1,0:T(8,128)S(1)}, u32[]{:S(2)}, u32[]{:S(2)}) collective-permute-start(f32[200,128]{1,0:T(8,128)S(1)} %tile_parts.1.refs_0_), channel_id=1, source_target_pairs={{64,0},{65,1},{66,2},{67,3},{68,4},{69,5},{70,6},{71,7},{72,8},{73... | collective-permute-start | bytes 307208 | tf_op jit(solution)/shard_map/ppermute | solution.py:49
  48.2 4.7 %collective-permute-start.4 = (f32[200,128]{1,0:T(8,128)S(1)}, f32[200,128]{1,0:T(8,128)S(1)}, u32[]{:S(2)}, u32[]{:S(2)}) collective-permute-start(f32[200,128]{1,0:T(8,128)S(1)} %tile_parts.1.refs_0_), channel_id=1, source_target_pairs={{32,0},{33,1},{34,2},{35,3},{36,4},{37,5},{38,6},{39,7},{40,8},{41... | collective-permute-start | bytes 307208 | tf_op jit(solution)/shard_map/ppermute | solution.py:49
  48.2 4.7 %collective-permute-start.7 = (f32[200,128]{1,0:T(8,128)S(1)}, f32[200,128]{1,0:T(8,128)S(1)}, u32[]{:S(2)}, u32[]{:S(2)}) collective-permute-start(f32[200,128]{1,0:T(8,128)S(1)} %tile_parts.1.refs_0_), channel_id=1, source_target_pairs={{0,1},{1,0},{2,3},{3,2},{4,5},{5,4},{6,7},{7,6},{8,9},{9,8},{10,11... | collective-permute-start | bytes 307208 | tf_op jit(solution)/shard_map/ppermute | solution.py:44
  50.1 2.8 %collective-permute-start.10 = (f32[200,128]{1,0:T(8,128)S(1)}, f32[200,128]{1,0:T(8,128)S(1)}, u32[]{:S(2)}, u32[]{:S(2)}) collective-permute-start(f32[200,128]{1,0:T(8,128)S(1)} %collective-permute-done.6.refs_3_), channel_id=1, source_target_pairs={{0,1},{1,0},{2,3},{3,2},{4,5},{5,4},{6,7},{7,6},{8,9},{9,8},{10,11... | collective-permute-start | bytes 307208 | tf_op jit(solution)/shard_map/ppermute | solution.py:44
  51.9 1.3 %collective-permute-start.9 = (f32[200,128]{1,0:T(8,128)S(1)}, f32[200,128]{1,0:T(8,128)S(1)}, u32[]{:S(2)}, u32[]{:S(2)}) collective-permute-start(f32[200,128]{1,0:T(8,128)S(1)} %collective-permute-done.5.refs_2_), channel_id=1, source_target_pairs={{0,1},{1,0},{2,3},{3,2},{4,5},{5,4},{6,7},{7,6},{8,9},{9,8},{10,11... | collective-permute-start | bytes 307208 | tf_op jit(solution)/shard_map/ppermute | solution.py:44
  52.9 1.3 %collective-permute-start.8 = (f32[200,128]{1,0:T(8,128)S(1)}, f32[200,128]{1,0:T(8,128)S(1)}, u32[]{:S(2)}, u32[]{:S(2)}) collective-permute-start(f32[200,128]{1,0:T(8,128)S(1)} %collective-permute-done.4.refs_1_), channel_id=1, source_target_pairs={{0,1},{1,0},{2,3},{3,2},{4,5},{5,4},{6,7},{7,6},{8,9},{9,8},{10,11... | collective-permute-start | bytes 307208 | tf_op jit(solution)/shard_map/ppermute | solution.py:44

commit v6 on v5

--- a/solution.py
+++ b/solution.py
@@ -50,30 +50,48 @@
     ]
 
 
-def spread_body(*refs):
-    sources, out = refs[:-1], refs[-1]
-    chunks = sources[1].shape[1] // LANES
+def spread_body(coords, out):
     rows = [
-        s[c : c + 1, j * LANES : (j + 1) * LANES]
-        for s in sources[1:]
+        coords[c : c + 1, j * LANES : (j + 1) * LANES]
         for c in range(DIM)
-        for j in range(chunks)
-    ]
-    block = jnp.concatenate([sources[0][...]] + rows, axis=0)
+        for j in range(coords.shape[1] // LANES)
+    ]
+    block = jnp.concatenate(rows, axis=0)
     for chip in range(out.shape[0]):
         out[chip] = block
 
 
-def spread(sources, chips):
-    rows = len(sources) * sources[0].size // LANES
+def spread(coordinates, chips):
     return pl.pallas_call(
         spread_body,
-        out_shape=jax.ShapeDtypeStruct((chips, rows, LANES), jnp.float32),
-        in_specs=[pl.BlockSpec(memory_space=pltpu.VMEM)] * len(sources),
+        out_shape=jax.ShapeDtypeStruct(
+            (chips, coordinates.size // LANES, LANES), jnp.float32
+        ),
+        in_specs=[pl.BlockSpec(memory_space=pltpu.VMEM)],
         out_specs=pl.BlockSpec(memory_space=pltpu.VMEM),
         compiler_params=pltpu.CompilerParams(vmem_limit_bytes=SMALL_LIMIT),
         name="spread",
-    )(*sources)
+    )(coordinates)
+
+
+def pick_body(groups, slots, places, own, twin, *outs):
+    for d in range(1, groups):
+        for i in range(2 * slots):
+            side, w = i % 2, (groups - d) * slots + i // 2
+            chip = lax.div(places[side, w], groups)
+            outs[d - 1][i] = jnp.where(places[4 + side, w] > 0, twin[chip], own[chip])
+
+
+def pick(places, own, twin, groups, slots):
+    return pl.pallas_call(
+        functools.partial(pick_body, groups, slots),
+        out_shape=[jax.ShapeDtypeStruct((2 * slots, *own.shape[1:]), jnp.float32)] * (groups - 1),
+        in_specs=[pl.BlockSpec(memory_space=pltpu.SMEM)]
+        + [pl.BlockSpec(memory_space=pltpu.VMEM)] * 2,
+        out_specs=[pl.BlockSpec(memory_space=pltpu.VMEM)] * (groups - 1),
+        compiler_params=pltpu.CompilerParams(vmem_limit_bytes=SMALL_LIMIT),
+        name="pick",
+    )(places, own, twin)
 
 
 def split3(x):
@@ -85,8 +103,8 @@
 
 
 def tile_body(rows, width, sc, delta_hbm, first, *refs):
-    sources = refs[:2]
-    parts, delta, near, far, left, right, delta_sem = refs[2:]
+    mine_here, twin_here, *others = refs[:-7]
+    parts, delta, near, far, left, right, delta_sem = refs[-7:]
     slots = delta.shape[0]
     chunks = width // LANES
     f32, bf16 = jnp.float32, jnp.bfloat16
@@ -111,8 +129,11 @@
             pl.when((k + 1 < slots) & (sc[6, later] > 0))(lambda: delta_copy(later).start())
 
             def block(side):
-                twin, at = sc[4 + side, k] > 0, sc[side, k]
-                found = jnp.where(twin, sources[1][at], sources[0][at])
+                groups = len(others) + 1
+                chip, step = lax.div(sc[side, k], groups), lax.rem(sc[side, k], groups)
+                found = jnp.where(sc[4 + side, k] > 0, twin_here[chip], mine_here[chip])
+                for n, other in enumerate(others):
+                    found = jnp.where(step == n + 1, other[2 * k + side], found)
                 return [found[c * chunks : (c + 1) * chunks, :] for c in range(DIM)]
 
             xa, xb = block(0), block(1)
@@ -211,24 +232,6 @@
     lax.fori_loop(0, slots, one_tile, 0)
 
 
-def fetch_body(source, out, sem):
-    copy = pltpu.make_async_copy(source.at[0], out, sem)
-    copy.start()
-    copy.wait()
-
-
-def first_tile(dissim):
-    return pl.pallas_call(
-        fetch_body,
-        out_shape=pltpu.VMEM(dissim.shape[1:], dissim.dtype),
-        in_specs=[pl.BlockSpec(memory_space=pltpu.HBM)],
-        out_specs=pl.BlockSpec(memory_space=pltpu.VMEM),
-        scratch_shapes=[pltpu.SemaphoreType.DMA],
-        compiler_params=pltpu.CompilerParams(vmem_limit_bytes=SMALL_LIMIT),
-        name="first_tile",
-    )(pltpu.with_memory_space_constraint(dissim, pltpu.HBM))
-
-
 def tile_parts(scalars, dissim, first, sources):
     slots, rows, width = dissim.shape
     block_rows = DIM * width // LANES
@@ -236,7 +239,7 @@
         functools.partial(tile_body, rows, width),
         out_shape=jax.ShapeDtypeStruct((2 * slots * block_rows + 8, LANES), jnp.float32),
     in_specs=[pl.BlockSpec(memory_space=pltpu.SMEM), pl.BlockSpec(memory_space=pltpu.HBM)]
-        + [pl.BlockSpec(memory_space=pltpu.VMEM)] * 3,
+        + [pl.BlockSpec(memory_space=pltpu.VMEM)] * (1 + len(sources)),
         out_specs=pl.BlockSpec(memory_space=pltpu.VMEM),
         scratch_shapes=[
             pltpu.VMEM((slots, rows, width), jnp.bfloat16),
@@ -320,24 +323,17 @@
     )(pieces)
 
 
-def tables_body(groups, devs, slots, tiles_hbm, holder_hbm, coords_hbm, out, own, *scratch):
-    tiles, holder, coords, sem = scratch
+def prepare_body(groups, devs, slots, tiles_hbm, holder_hbm, delta_hbm, out, first, *scratch):
+    tiles, holder, sem = scratch
+    sources = (tiles_hbm, holder_hbm, delta_hbm.at[0])
     copies = [
         pltpu.make_async_copy(source, target, sem.at[i])
-        for i, (source, target) in enumerate(
-            ((tiles_hbm, tiles), (holder_hbm, holder), (coords_hbm, coords))
-        )
+        for i, (source, target) in enumerate(zip(sources, (tiles, holder, first)))
     ]
     for copy in copies:
         copy.start()
-    for copy in copies:
+    for copy in copies[:2]:
         copy.wait()
-    chunks = coords.shape[1] // LANES
-    for c in range(DIM):
-        for j in range(chunks):
-            own[c * chunks + j : c * chunks + j + 1, :] = coords[
-                c : c + 1, j * LANES : (j + 1) * LANES
-            ]
     f32, i32 = jnp.float32, jnp.int32
     group, dev = lax.axis_index("grp"), lax.axis_index("dev")
     count, blocks = tiles.shape[1], holder.shape[1]
@@ -377,23 +373,24 @@
         out[4 + side : 5 + side, :] = twin[side]
     out[6:7, :] = jnp.where(held[0] >= 0, 1, 0)
     out[7:8, :] = jnp.zeros((1, LANES), i32)
-
-
-def tables(tile_list, holder, coordinates, groups, devs, slots):
-    arrays = [tile_list.T, holder.reshape(1, -1), coordinates]
-    return pl.pallas_call(
-        functools.partial(tables_body, groups, devs, slots),
+    copies[2].wait()
+
+
+def prepare(tile_list, holder, dissim, groups, devs):
+    arrays = [tile_list.T, holder.reshape(1, -1)]
+    return pl.pallas_call(
+        functools.partial(prepare_body, groups, devs, dissim.shape[0]),
         out_shape=(
             jax.ShapeDtypeStruct((8, LANES), jnp.int32),
-            jax.ShapeDtypeStruct((coordinates.size // LANES, LANES), jnp.float32),
+            pltpu.VMEM(dissim.shape[1:], dissim.dtype),
         ),
         in_specs=[pl.BlockSpec(memory_space=pltpu.HBM)] * 3,
         out_specs=[pl.BlockSpec(memory_space=pltpu.VMEM)] * 2,
         scratch_shapes=[pltpu.VMEM(a.shape, a.dtype) for a in arrays]
         + [pltpu.SemaphoreType.DMA((3,))],
         compiler_params=pltpu.CompilerParams(vmem_limit_bytes=SMALL_LIMIT),
-        name="tables",
-    )(*[pltpu.with_memory_space_constraint(a, pltpu.HBM) for a in arrays])
+        name="prepare",
+    )(*[pltpu.with_memory_space_constraint(a, pltpu.HBM) for a in arrays + [dissim]])
 
 
 def on_device(tile_list, holder, coordinates, dissim):
@@ -402,16 +399,17 @@
     width = coordinates.shape[1]
     slots = dissim.shape[0]
     block_rows = DIM * width // LANES
-    places, rows = tables(tile_list, holder, coordinates, groups, devs, slots)
     plane = plane_groups(groups, devs)
-    line = from_line(coordinates, groups, devs)
-    line[0] = rows
-    sent = spread(line, chips)
+    sent = spread(coordinates, chips)
     own = lax.all_to_all(sent, AXES, 0, 0, tiled=True, axis_index_groups=plane)
     own, dissim = lax.optimization_barrier((own, dissim))
-    own = own.reshape(groups * chips, block_rows, LANES)
     twin = to_twin(own, groups * devs)
-    parts = tile_parts(places, dissim, first_tile(dissim), [own, twin])
+    places, first = prepare(tile_list, holder, dissim, groups, devs)
+    picked = pick(places, own, twin, groups, slots)
+    others = [
+        lax.ppermute(picked[d - 1], AXES, line_perm(groups, devs, d)) for d in range(1, groups)
+    ]
+    parts = tile_parts(places, dissim, first, [own, twin, *others])
     line = from_line(parts, groups, devs)
     line = line + [to_twin(a, groups * devs) for a in line]
     pieces = by_chip(places, line, chips, slots)

time: 68.5 us -> 66.7 us (0.974)
  blocking collectives: 32.8 us -> 28.6 us
  waiting for transfers between devices: 8.25 us -> 12.3 us
  starting transfers between devices: 9.69 us -> 8.32 us
  Pallas kernels: 16.8 us -> 16 us
  local copies, waits for them, and re-layouts: 0 us -> 0.71 us
    ppermute x0 -> x3, waiting for transfers between devices: none -> 6.85 us  [on_device(): lax.ppermute(picked[d - 1], AXES, line_perm(groups, devs, d))]
    ppermute x6 -> x3, starting transfers between devices: 9.68 us -> 3.29 us  [from_line(): lax.ppermute(array, AXES, line_perm(groups, devs, d))]
    ppermute x0 -> x3, starting transfers between devices: none -> 4.51 us  [on_device(): lax.ppermute(picked[d - 1], AXES, line_perm(groups, devs, d))]
    all_to_all x1, blocking collectives: 20.5 us -> 16.1 us  [on_device(): own = lax.all_to_all(sent, AXES, 0, 0, tiled=True, axis_index_groups=plane)]
    ppermute x6 -> x3, waiting for transfers between devices: 6.27 us -> 4.11 us  [from_line(): lax.ppermute(array, AXES, line_perm(groups, devs, d))]
    pallas_call x3, Pallas kernels: 3.19 us -> 2.36 us  [the longest x1 1.65 us: prepare(): pl.pallas_call(functools.partial(prepare_body, groups, devs, dissim.shape...]
    unnamed x0 -> x2, local copies, waits for them, and re-layouts: none -> 0.71 us
  transfers between devices with their start and end apart: 11 -> 11, of which waited for: 8 -> 8; matrix products, arithmetic and copies ran while one was open for 0% -> 0% of each run, Pallas kernels for 5% -> 2%
where the time goes in v6:
time: 66.7 us; the launch traced here: 66.5 us
  blocking collectives  28.6 us (43%)
  Pallas kernels  16 us (24%)
  waiting for transfers between devices  12.3 us (18%)
  starting transfers between devices  8.32 us (12%)
  local copies, waits for them, and re-layouts  0.71 us (1%)
  between operations  0.71 us (1%)
    all_to_all x1, blocking collectives, on_device(): own = lax.all_to_all(sent, AXES, 0, 0, tiled=True, axis_index_groups=plane)  16.1 us
    all_to_all x1, blocking collectives, on_device(): lax.all_to_all(pieces, AXES, 0, 0, tiled=True, axis_index_groups=plane)  12.5 us
    pallas_call x1, Pallas kernels, tile_parts(): pl.pallas_call(functools.partial(tile_body, rows, width), out_shape=jax.S...  11.8 us
    ppermute x3, waiting for transfers between devices, on_device(): lax.ppermute(picked[d - 1], AXES, line_perm(groups, devs, d))  6.85 us
    ppermute x3, starting transfers between devices, on_device(): lax.ppermute(picked[d - 1], AXES, line_perm(groups, devs, d))  4.51 us
    ppermute x3, waiting for transfers between devices, from_line(): lax.ppermute(array, AXES, line_perm(groups, devs, d))  4.11 us
    ppermute x3, starting transfers between devices, from_line(): lax.ppermute(array, AXES, line_perm(groups, devs, d))  3.29 us
    pallas_call x1, Pallas kernels, prepare(): pl.pallas_call(functools.partial(prepare_body, groups, devs, dissim.shape...  1.65 us
  transfers between devices with their start and end apart: 11, of which 8 were waited for; matrix products, arithmetic and copies ran while one was open for 0% of the time, Pallas kernels for 2%

profile of v6, /device:TPU:0, one launch (start us, length us, event | category | flops | bytes accessed | tf_op | source)
XLA Modules:
  0.0 66.5 jit_solution(9632078477614209345)
XLA Ops:
  0.6 0.0 copy-start
  0.6 0.7 %copy-done = f32[3,1024]{1,0:T(4,128)S(1)} copy-done((f32[3,1024]{1,0:T(4,128)S(1)}, f32[3,1024]{1,0:T(4,128)}, u32[]{:S(2)}) %copy-start) | copy-done | bytes 12312
  1.4 16.1 %all_to_all.10.own.refs_0_ = f32[16,24,128]{2,1,0:T(8,128)S(1)} all-to-all(f32[16,24,128]{2,1,0:T(8,128)S(1)} %spread.1), channel_id=1, replica_groups={{0,2,4,6,8,10,12,14,16,18,20,22,24,26,28,30},{1,3,5,7,9,11,13,15,17,19,..., dimensions={0} | all-to-all | bytes 393216 | tf_op jit(solution)/shard_map/all_to_all | solution.py:404
  17.5 0.0 collective-permute-start
  17.5 1.6 %prepare.1 = (s32[8,128]{1,0:T(8,128)S(1)}, bf16[1024,1024]{1,0:T(8,128)(2,1)S(1)}) custom-call(s32[3,256]{1,0:T(4,128)} %bitcast.3, s32[1,128]{1,0:T(1,128)} %bitcast.4, bf16[4,1024,1024]{2,1,0:T(8,128)(2,1)} %delta_hbm.1), custom_call_target="tpu_custom_call" | custom-call | tf_op jit(solution)/shard_map/prepare/pallas_call | solution.py:381
  19.1 0.0 collective-permute-done.twin.refs_1_
  19.1 0.7 %pick.1 = (f32[8,24,128]{2,1,0:T(8,128)S(1)}, f32[8,24,128]{2,1,0:T(8,128)S(1)}, f32[8,24,128]{2,1,0:T(8,128)S(1)}) custom-call(s32[8,128]{1,0:T(8,128)S(1)} %get-tuple-element.12.places.sc.where, f32[16,24,128]{2,1,0:T(8,128)S(1)} %all_to_all.10.own.refs_0_, f32[16,24,128]{2,1,0:T(8,128)S(1)} %collective-permute-done.twin.refs_1_), custom_call_target="tpu_custom_call" | custom-call | tf_op jit(solution)/shard_map/pick/pallas_call | solution.py:86
  19.8 2.8 %collective-permute-start.1 = (f32[8,24,128]{2,1,0:T(8,128)S(1)}, f32[8,24,128]{2,1,0:T(8,128)S(1)}, u32[]{:S(2)}, u32[]{:S(2)}) collective-permute-start(f32[8,24,128]{2,1,0:T(8,128)S(1)} %get-tuple-element.15), channel_id=1, source_target_pairs={{32,0},{33,1},{34,2},{35,3},{36,4},{37,5},{38,6},{39,7},{40,8},{41... | collective-permute-start | bytes 294920 | tf_op jit(solution)/shard_map/ppermute | solution.py:410
  22.7 0.8 %collective-permute-start.2 = (f32[8,24,128]{2,1,0:T(8,128)S(1)}, f32[8,24,128]{2,1,0:T(8,128)S(1)}, u32[]{:S(2)}, u32[]{:S(2)}) collective-permute-start(f32[8,24,128]{2,1,0:T(8,128)S(1)} %get-tuple-element.16), channel_id=1, source_target_pairs={{64,0},{65,1},{66,2},{67,3},{68,4},{69,5},{70,6},{71,7},{72,8},{73... | collective-permute-start | bytes 294920 | tf_op jit(solution)/shard_map/ppermute | solution.py:410
  23.5 0.9 %collective-permute-start.3 = (f32[8,24,128]{2,1,0:T(8,128)S(1)}, f32[8,24,128]{2,1,0:T(8,128)S(1)}, u32[]{:S(2)}, u32[]{:S(2)}) collective-permute-start(f32[8,24,128]{2,1,0:T(8,128)S(1)} %get-tuple-element.17), channel_id=1, source_target_pairs={{96,0},{97,1},{98,2},{99,3},{100,4},{101,5},{102,6},{103,7},{104,8... | collective-permute-start | bytes 294920 | tf_op jit(solution)/shard_map/ppermute | solution.py:410
  24.4 3.2 %collective-permute-done.1.refs_2_ = f32[8,24,128]{2,1,0:T(8,128)S(1)} collective-permute-done((f32[8,24,128]{2,1,0:T(8,128)S(1)}, f32[8,24,128]{2,1,0:T(8,128)S(1)}, u32[]{:S(2)}, u32[]{:S(2)}) %collective-permute-start.1) | collective-permute-done | bytes 98336 | tf_op jit(solution)/shard_map/ppermute | solution.py:410
  27.5 2.3 %collective-permute-done.2.refs_3_ = f32[8,24,128]{2,1,0:T(8,128)S(1)} collective-permute-done((f32[8,24,128]{2,1,0:T(8,128)S(1)}, f32[8,24,128]{2,1,0:T(8,128)S(1)}, u32[]{:S(2)}, u32[]{:S(2)}) %collective-permute-start.2) | collective-permute-done | bytes 98336 | tf_op jit(solution)/shard_map/ppermute | solution.py:410
  29.8 1.4 %collective-permute-done.3.refs_4_ = f32[8,24,128]{2,1,0:T(8,128)S(1)} collective-permute-done((f32[8,24,128]{2,1,0:T(8,128)S(1)}, f32[8,24,128]{2,1,0:T(8,128)S(1)}, u32[]{:S(2)}, u32[]{:S(2)}) %collective-permute-start.3) | collective-permute-done | bytes 98336 | tf_op jit(solution)/shard_map/ppermute | solution.py:410
  31.2 11.8 %tile_parts.1.refs_0_ = f32[200,128]{1,0:T(8,128)S(1)} custom-call(s32[8,128]{1,0:T(8,128)S(1)} %get-tuple-element.12.places.sc.where, bf16[4,1024,1024]{2,1,0:T(8,128)(2,1)} %delta_hbm.1, bf16[1024,1024]{1,0:T(8,128)(2,1)S(1)} %get-tuple-element.13.first, f32[16,24,128]{2,1,0:T(8,128)S(1)} %all_to_all.10.own.refs_0_, ...), custom_call_target="tpu_custom_call" | custom-call | tf_op jit(solution)/shard_map/tile_parts/pallas_call | solution.py:238
  43.0 0.1 collective-permute-start.6
  43.1 0.1 collective-permute-start.5
  43.2 3.1 %collective-permute-start.4 = (f32[200,128]{1,0:T(8,128)S(1)}, f32[200,128]{1,0:T(8,128)S(1)}, u32[]{:S(2)}, u32[]{:S(2)}) collective-permute-start(f32[200,128]{1,0:T(8,128)S(1)} %tile_parts.1.refs_0_), channel_id=1, source_target_pairs={{32,0},{33,1},{34,2},{35,3},{36,4},{37,5},{38,6},{39,7},{40,8},{41... | collective-permute-start | bytes 307208 | tf_op jit(solution)/shard_map/ppermute | solution.py:49
  46.3 0.0 collective-permute-start.7
  46.3 3.7 %collective-permute-done.6.refs_3_ = f32[200,128]{1,0:T(8,128)S(1)} collective-permute-done((f32[200,128]{1,0:T(8,128)S(1)}, f32[200,128]{1,0:T(8,128)S(1)}, u32[]{:S(2)}, u32[]{:S(2)}) %collective-permute-start.6) | collective-permute-done | bytes 102432 | tf_op jit(solution)/shard_map/ppermute | solution.py:49
  50.1 0.0 collective-permute-start.10
  50.1 0.0 collective-permute-done.5.refs_2_
  50.1 0.5 collective-permute-start.9
  50.6 0.4 collective-permute-done.4.refs_1_
  51.0 0.0 collective-permute-start.8
  51.0 0.0 collective-permute-done.7.refs_4_
  51.0 0.4 collective-permute-done.10.refs_7_
  51.4 0.2 collective-permute-done.9.refs_6_
  51.5 0.7 %collective-permute-done.8.refs_5_ = f32[200,128]{1,0:T(8,128)S(1)} collective-permute-done((f32[200,128]{1,0:T(8,128)S(1)}, f32[200,128]{1,0:T(8,128)S(1)}, u32[]{:S(2)}, u32[]{:S(2)}) %collective-permute-start.8) | collective-permute-done | bytes 102432 | tf_op jit(solution)/shard_map/ppermute | solution.py:44
  52.3 1.1 %by_chip.1 = f32[16,32,128]{2,1,0:T(8,128)S(1)} custom-call(s32[8,128]{1,0:T(8,128)S(1)} %get-tuple-element.12.places.sc.where, f32[200,128]{1,0:T(8,128)S(1)} %tile_parts.1.refs_0_, f32[200,128]{1,0:T(8,128)S(1)} %collective-permute-done.4.refs_1_, f32[200,128]{1,0:T(8,128)S(1)} %collective-permute-done.5.refs_2_, ...), custom_call_target="tpu_custom_call" | custom-call | tf_op jit(solution)/shard_map/by_chip/pallas_call | solution.py:285
  53.4 12.5 %all_to_all.11.pieces = f32[16,32,128]{2,1,0:T(8,128)S(1)} all-to-all(f32[16,32,128]{2,1,0:T(8,128)S(1)} %by_chip.1), channel_id=1, replica_groups={{0,2,4,6,8,10,12,14,16,18,20,22,24,26,28,30},{1,3,5,7,9,11,13,15,17,19,..., dimensions={0} | all-to-all | bytes 524288 | tf_op jit(solution)/shard_map/all_to_all | solution.py:416
  65.9 0.6 total.1
  (1 shorter events, 0.0 us)
Async XLA Ops:
  0.6 0.7 %copy-start = (f32[3,1024]{1,0:T(4,128)S(1)}, f32[3,1024]{1,0:T(4,128)}, u32[]{:S(2)}) copy-start(f32[3,1024]{1,0:T(4,128)} %coords.1) | copy-start | bytes 36868
  17.5 1.7 %collective-permute-start = (f32[16,24,128]{2,1,0:T(8,128)S(1)}, f32[16,24,128]{2,1,0:T(8,128)S(1)}, u32[]{:S(2)}, u32[]{:S(2)}) collective-permute-start(f32[16,24,128]{2,1,0:T(8,128)S(1)} %all_to_all.10.own.refs_0_), channel_id=1, source_target_pairs={{0,1},{1,0},{2,3},{3,2},{4,5},{5,4},{6,7},{7,6},{8,9},{9,8},{10,11... | collective-permute-start | bytes 589832 | tf_op jit(solution)/shard_map/ppermute | solution.py:44
  19.8 7.7 %collective-permute-start.1 = (f32[8,24,128]{2,1,0:T(8,128)S(1)}, f32[8,24,128]{2,1,0:T(8,128)S(1)}, u32[]{:S(2)}, u32[]{:S(2)}) collective-permute-start(f32[8,24,128]{2,1,0:T(8,128)S(1)} %get-tuple-element.15), channel_id=1, source_target_pairs={{32,0},{33,1},{34,2},{35,3},{36,4},{37,5},{38,6},{39,7},{40,8},{41... | collective-permute-start | bytes 294920 | tf_op jit(solution)/shard_map/ppermute | solution.py:410
  22.7 7.1 %collective-permute-start.2 = (f32[8,24,128]{2,1,0:T(8,128)S(1)}, f32[8,24,128]{2,1,0:T(8,128)S(1)}, u32[]{:S(2)}, u32[]{:S(2)}) collective-permute-start(f32[8,24,128]{2,1,0:T(8,128)S(1)} %get-tuple-element.16), channel_id=1, source_target_pairs={{64,0},{65,1},{66,2},{67,3},{68,4},{69,5},{70,6},{71,7},{72,8},{73... | collective-permute-start | bytes 294920 | tf_op jit(solution)/shard_map/ppermute | solution.py:410
  23.5 7.7 %collective-permute-start.3 = (f32[8,24,128]{2,1,0:T(8,128)S(1)}, f32[8,24,128]{2,1,0:T(8,128)S(1)}, u32[]{:S(2)}, u32[]{:S(2)}) collective-permute-start(f32[8,24,128]{2,1,0:T(8,128)S(1)} %get-tuple-element.17), channel_id=1, source_target_pairs={{96,0},{97,1},{98,2},{99,3},{100,4},{101,5},{102,6},{103,7},{104,8... | collective-permute-start | bytes 294920 | tf_op jit(solution)/shard_map/ppermute | solution.py:410
  43.0 7.0 %collective-permute-start.6 = (f32[200,128]{1,0:T(8,128)S(1)}, f32[200,128]{1,0:T(8,128)S(1)}, u32[]{:S(2)}, u32[]{:S(2)}) collective-permute-start(f32[200,128]{1,0:T(8,128)S(1)} %tile_parts.1.refs_0_), channel_id=1, source_target_pairs={{96,0},{97,1},{98,2},{99,3},{100,4},{101,5},{102,6},{103,7},{104,8... | collective-permute-start | bytes 307208 | tf_op jit(solution)/shard_map/ppermute | solution.py:49
  43.1 7.0 %collective-permute-start.5 = (f32[200,128]{1,0:T(8,128)S(1)}, f32[200,128]{1,0:T(8,128)S(1)}, u32[]{:S(2)}, u32[]{:S(2)}) collective-permute-start(f32[200,128]{1,0:T(8,128)S(1)} %tile_parts.1.refs_0_), channel_id=1, source_target_pairs={{64,0},{65,1},{66,2},{67,3},{68,4},{69,5},{70,6},{71,7},{72,8},{73... | collective-permute-start | bytes 307208 | tf_op jit(solution)/shard_map/ppermute | solution.py:49
  43.2 7.8 %collective-permute-start.4 = (f32[200,128]{1,0:T(8,128)S(1)}, f32[200,128]{1,0:T(8,128)S(1)}, u32[]{:S(2)}, u32[]{:S(2)}) collective-permute-start(f32[200,128]{1,0:T(8,128)S(1)} %tile_parts.1.refs_0_), channel_id=1, source_target_pairs={{32,0},{33,1},{34,2},{35,3},{36,4},{37,5},{38,6},{39,7},{40,8},{41... | collective-permute-start | bytes 307208 | tf_op jit(solution)/shard_map/ppermute | solution.py:49
  46.3 4.6 %collective-permute-start.7 = (f32[200,128]{1,0:T(8,128)S(1)}, f32[200,128]{1,0:T(8,128)S(1)}, u32[]{:S(2)}, u32[]{:S(2)}) collective-permute-start(f32[200,128]{1,0:T(8,128)S(1)} %tile_parts.1.refs_0_), channel_id=1, source_target_pairs={{0,1},{1,0},{2,3},{3,2},{4,5},{5,4},{6,7},{7,6},{8,9},{9,8},{10,11... | collective-permute-start | bytes 307208 | tf_op jit(solution)/shard_map/ppermute | solution.py:44
  50.1 1.3 %collective-permute-start.10 = (f32[200,128]{1,0:T(8,128)S(1)}, f32[200,128]{1,0:T(8,128)S(1)}, u32[]{:S(2)}, u32[]{:S(2)}) collective-permute-start(f32[200,128]{1,0:T(8,128)S(1)} %collective-permute-done.6.refs_3_), channel_id=1, source_target_pairs={{0,1},{1,0},{2,3},{3,2},{4,5},{5,4},{6,7},{7,6},{8,9},{9,8},{10,11... | collective-permute-start | bytes 307208 | tf_op jit(solution)/shard_map/ppermute | solution.py:44
  50.1 1.5 %collective-permute-start.9 = (f32[200,128]{1,0:T(8,128)S(1)}, f32[200,128]{1,0:T(8,128)S(1)}, u32[]{:S(2)}, u32[]{:S(2)}) collective-permute-start(f32[200,128]{1,0:T(8,128)S(1)} %collective-permute-done.5.refs_2_), channel_id=1, source_target_pairs={{0,1},{1,0},{2,3},{3,2},{4,5},{5,4},{6,7},{7,6},{8,9},{9,8},{10,11... | collective-permute-start | bytes 307208 | tf_op jit(solution)/shard_map/ppermute | solution.py:44
  51.0 1.3 %collective-permute-start.8 = (f32[200,128]{1,0:T(8,128)S(1)}, f32[200,128]{1,0:T(8,128)S(1)}, u32[]{:S(2)}, u32[]{:S(2)}) collective-permute-start(f32[200,128]{1,0:T(8,128)S(1)} %collective-permute-done.4.refs_1_), channel_id=1, source_target_pairs={{0,1},{1,0},{2,3},{3,2},{4,5},{5,4},{6,7},{7,6},{8,9},{9,8},{10,11... | collective-permute-start | bytes 307208 | tf_op jit(solution)/shard_map/ppermute | solution.py:44

commit v7 on v6

--- a/solution.py
+++ b/solution.py
@@ -110,126 +110,143 @@
     f32, bf16 = jnp.float32, jnp.bfloat16
 
     def delta_copy(k):
-        return pltpu.make_async_copy(delta_hbm.at[k], delta.at[k], delta_sem.at[k])
-
-    @pl.when(sc[6, 0] > 0)
-    def _():
-        pltpu.make_async_copy(first, delta.at[0], delta_sem.at[0]).start()
-
+        source = first.at[k] if k < 2 else delta_hbm.at[k]
+        return pltpu.make_async_copy(source, delta.at[k], delta_sem.at[k])
+
+    def await_delta(k):
+        pltpu.make_async_copy(delta_hbm.at[k], delta.at[k], delta_sem.at[k]).wait()
+
+    def held(m):
+        both = (sc[6, 2 * m] > 0) & (sc[6, 2 * m + 1] > 0)
+        return both, (sc[6, 2 * m] > 0) & jnp.logical_not(both)
+
+    for m in range(slots // 2):
+        both, alone = held(m)
+        pl.when(both | alone)(lambda m=m: delta_copy(2 * m).start())
+        pl.when(both)(lambda m=m: delta_copy(2 * m + 1).start())
 
     parts[2 * slots * DIM * chunks :, :] = jnp.zeros((8, LANES), f32)
     for ref in (near, far, left, right):
         ref[...] = jnp.zeros(ref.shape, f32)
 
-    def one_tile(k, _):
-        @pl.when(sc[6, k] > 0)
+    def one_tile(k, left, right, near, far):
+        def block(side):
+            groups = len(others) + 1
+            chip, step = lax.div(sc[side, k], groups), lax.rem(sc[side, k], groups)
+            found = jnp.where(sc[4 + side, k] > 0, twin_here[chip], mine_here[chip])
+            for n, other in enumerate(others):
+                found = jnp.where(step == n + 1, other[2 * k + side], found)
+            return [found[c * chunks : (c + 1) * chunks, :] for c in range(DIM)]
+
+        xa, xb = block(0), block(1)
+        mean = [jnp.sum(a, keepdims=True) * (1.0 / width) for a in xa]
+        xa = [a - m for a, m in zip(xa, mean)]
+        xb = [b - m for b, m in zip(xb, mean)]
+        one = jnp.ones((chunks, LANES), f32)
+
+        def terms(x):
+            pieces = [split3(v) for v in x]
+            norms = split3(x[0] * x[0] + x[1] * x[1] + x[2] * x[2])
+            return pieces, list(norms)
+
+        (pa, na), (pb, nb) = terms(xa), terms(xb)
+        pairs = [(s, t) for s in range(3) for t in range(3)]
+        la = [p[s] * -2.0 for p in pa for s, _ in pairs] + na + [one] * 3
+        lb = [p[t] for p in pb for _, t in pairs] + [one] * 3 + nb
+        va = [v for p in pa for v in p] + [one]
+        vb = [v for p in pb for v in p] + [one]
+        for ref, values in ((left, la), (right, lb), (near, va), (far, vb)):
+            for n, v in enumerate(values):
+                ref[n] = v
+        count = rows // STEP
+        pieces = width // DEPTH
+
+        def wide(ref, g):
+            each = DEPTH // LANES
+            return jnp.concatenate(
+                [ref[:, g * each + e, :] for e in range(each)], axis=1
+            ).astype(bf16)
+
+        lhs = [jnp.transpose(left[:, n, :]).astype(bf16) for n in range(count)]
+        mine = [near[:, n, :].astype(bf16) for n in range(count)]
+        mine = [jnp.concatenate([m, m], axis=1) for m in mine]
+        cols = [wide(right, g) for g in range(pieces)]
+        weights = [wide(far, g) for g in range(pieces)]
+        stress = jnp.zeros((16, LANES), f32)
+        row, col = [None] * count, [None] * pieces
+
+        def front(n, g):
+            return lax.dot_general(
+                lhs[n], cols[g], (((1,), (0,)), ((), ())), preferred_element_type=f32
+            )
+
+        def back(n, g, squared, stress):
+            lanes = slice(g * DEPTH, (g + 1) * DEPTH)
+            target = delta[k, n * STEP : (n + 1) * STEP, lanes].astype(f32)
+            squared = jnp.maximum(squared, FLOOR_SQUARED)
+            inverse = lax.rsqrt(squared)
+            error = target - squared * inverse
+            error = error * error
+            for a in range(0, STEP, 16):
+                for b in range(0, DEPTH, LANES):
+                    stress = stress + error[a : a + 16, b : b + LANES]
+            ratio = target * inverse
+            high = ratio.astype(bf16)
+            low = (ratio - high.astype(f32)).astype(bf16)
+            return stress, jnp.concatenate([high, low], axis=0)
+
+        def last(n, g, both):
+            a = lax.dot_general(
+                mine[n], both, (((1,), (0,)), ((), ())), preferred_element_type=f32
+            )
+            col[g] = a if col[g] is None else col[g] + a
+            a = lax.dot_general(
+                weights[g], both, (((1,), (1,)), ((), ())), preferred_element_type=f32
+            )
+            row[n] = a if row[n] is None else row[n] + a
+
+        order = [(n, g) for n in range(count) for g in range(pieces)]
+        ahead = [front(*order[t]) for t in range(AHEAD)]
+        held = []
+        for t, (n, g) in enumerate(order):
+            if t + AHEAD < len(order):
+                ahead.append(front(*order[t + AHEAD]))
+            if len(held) > LAG - 1:
+                last(*held.pop(0))
+            stress, both = back(n, g, ahead.pop(0), stress)
+            held.append((n, g, both))
+        for h in held:
+            last(*h)
+        row = [r[:, :STEP] + r[:, STEP:] for r in row]
+        col = [c[:, e * LANES : (e + 1) * LANES] for c in col for e in range(DEPTH // LANES)]
+        for side, own, total in ((0, xa, row), (1, xb, col)):
+            first_row = (2 * k + side) * DIM * chunks
+            for c in range(DIM):
+                for j in range(chunks):
+                    t = total[j]
+                    cross = t[3 * c : 3 * c + 1] + t[3 * c + 1 : 3 * c + 2] + t[3 * c + 2 : 3 * c + 3]
+                    value = own[c][j : j + 1] * t[9:10] - cross
+                    parts[pl.ds(first_row + c * chunks + j, 1), :] = value
+        parts[2 * slots * DIM * chunks :, :] += stress[:8] + stress[8:]
+
+    def two_slots(m, _):
+        both, alone = held(m)
+
+        @pl.when(both)
         def _():
-            delta_copy(k).wait()
-            later = jnp.minimum(k + 1, slots - 1)
-            pl.when((k + 1 < slots) & (sc[6, later] > 0))(lambda: delta_copy(later).start())
-
-            def block(side):
-                groups = len(others) + 1
-                chip, step = lax.div(sc[side, k], groups), lax.rem(sc[side, k], groups)
-                found = jnp.where(sc[4 + side, k] > 0, twin_here[chip], mine_here[chip])
-                for n, other in enumerate(others):
-                    found = jnp.where(step == n + 1, other[2 * k + side], found)
-                return [found[c * chunks : (c + 1) * chunks, :] for c in range(DIM)]
-
-            xa, xb = block(0), block(1)
-            mean = [jnp.sum(a, keepdims=True) * (1.0 / width) for a in xa]
-            xa = [a - m for a, m in zip(xa, mean)]
-            xb = [b - m for b, m in zip(xb, mean)]
-            one = jnp.ones((chunks, LANES), f32)
-
-            def terms(x):
-                pieces = [split3(v) for v in x]
-                norms = split3(x[0] * x[0] + x[1] * x[1] + x[2] * x[2])
-                return pieces, list(norms)
-
-            (pa, na), (pb, nb) = terms(xa), terms(xb)
-            pairs = [(s, t) for s in range(3) for t in range(3)]
-            la = [p[s] * -2.0 for p in pa for s, _ in pairs] + na + [one] * 3
-            lb = [p[t] for p in pb for _, t in pairs] + [one] * 3 + nb
-            va = [v for p in pa for v in p] + [one]
-            vb = [v for p in pb for v in p] + [one]
-            for ref, values in ((left, la), (right, lb), (near, va), (far, vb)):
-                for n, v in enumerate(values):
-                    ref[n] = v
-            count = rows // STEP
-            pieces = width // DEPTH
-
-            def wide(ref, g):
-                each = DEPTH // LANES
-                return jnp.concatenate(
-                    [ref[:, g * each + e, :] for e in range(each)], axis=1
-                ).astype(bf16)
-
-            lhs = [jnp.transpose(left[:, n, :]).astype(bf16) for n in range(count)]
-            mine = [near[:, n, :].astype(bf16) for n in range(count)]
-            mine = [jnp.concatenate([m, m], axis=1) for m in mine]
-            cols = [wide(right, g) for g in range(pieces)]
-            weights = [wide(far, g) for g in range(pieces)]
-            stress = jnp.zeros((16, LANES), f32)
-            row, col = [None] * count, [None] * pieces
-
-            def front(n, g):
-                return lax.dot_general(
-                    lhs[n], cols[g], (((1,), (0,)), ((), ())), preferred_element_type=f32
-                )
-
-            def back(n, g, squared, stress):
-                lanes = slice(g * DEPTH, (g + 1) * DEPTH)
-                target = delta[k, n * STEP : (n + 1) * STEP, lanes].astype(f32)
-                squared = jnp.maximum(squared, FLOOR_SQUARED)
-                inverse = lax.rsqrt(squared)
-                error = target - squared * inverse
-                error = error * error
-                for a in range(0, STEP, 16):
-                    for b in range(0, DEPTH, LANES):
-                        stress = stress + error[a : a + 16, b : b + LANES]
-                ratio = target * inverse
-                high = ratio.astype(bf16)
-                low = (ratio - high.astype(f32)).astype(bf16)
-                return stress, jnp.concatenate([high, low], axis=0)
-
-            def last(n, g, both):
-                a = lax.dot_general(
-                    mine[n], both, (((1,), (0,)), ((), ())), preferred_element_type=f32
-                )
-                col[g] = a if col[g] is None else col[g] + a
-                a = lax.dot_general(
-                    weights[g], both, (((1,), (1,)), ((), ())), preferred_element_type=f32
-                )
-                row[n] = a if row[n] is None else row[n] + a
-
-            order = [(n, g) for n in range(count) for g in range(pieces)]
-            ahead = [front(*order[t]) for t in range(AHEAD)]
-            held = []
-            for t, (n, g) in enumerate(order):
-                if t + AHEAD < len(order):
-                    ahead.append(front(*order[t + AHEAD]))
-                if len(held) > LAG - 1:
-                    last(*held.pop(0))
-                stress, both = back(n, g, ahead.pop(0), stress)
-                held.append((n, g, both))
-            for h in held:
-                last(*h)
-            row = [r[:, :STEP] + r[:, STEP:] for r in row]
-            col = [c[:, e * LANES : (e + 1) * LANES] for c in col for e in range(DEPTH // LANES)]
-            for side, own, total in ((0, xa, row), (1, xb, col)):
-                first_row = (2 * k + side) * DIM * chunks
-                for c in range(DIM):
-                    for j in range(chunks):
-                        t = total[j]
-                        cross = t[3 * c : 3 * c + 1] + t[3 * c + 1 : 3 * c + 2] + t[3 * c + 2 : 3 * c + 3]
-                        value = own[c][j : j + 1] * t[9:10] - cross
-                        parts[pl.ds(first_row + c * chunks + j, 1), :] = value
-            parts[2 * slots * DIM * chunks :, :] += stress[:8] + stress[8:]
+            for s in range(2):
+                await_delta(2 * m + s)
+            for s in range(2):
+                one_tile(2 * m + s, left.at[s], right.at[s], near.at[s], far.at[s])
+
+        @pl.when(alone)
+        def _():
+            await_delta(2 * m)
+            one_tile(2 * m, left.at[0], right.at[0], near.at[0], far.at[0])
 
         return 0
 
-    lax.fori_loop(0, slots, one_tile, 0)
+    lax.fori_loop(0, slots // 2, two_slots, 0)
 
 
 def tile_parts(scalars, dissim, first, sources):
@@ -243,10 +260,10 @@
         out_specs=pl.BlockSpec(memory_space=pltpu.VMEM),
         scratch_shapes=[
             pltpu.VMEM((slots, rows, width), jnp.bfloat16),
-            pltpu.VMEM((16, rows // LANES, LANES), jnp.float32),
-            pltpu.VMEM((16, width // LANES, LANES), jnp.float32),
-            pltpu.VMEM((KDIM, rows // LANES, LANES), jnp.float32),
-            pltpu.VMEM((KDIM, width // LANES, LANES), jnp.float32),
+            pltpu.VMEM((2, 16, rows // LANES, LANES), jnp.float32),
+            pltpu.VMEM((2, 16, width // LANES, LANES), jnp.float32),
+            pltpu.VMEM((2, KDIM, rows // LANES, LANES), jnp.float32),
+            pltpu.VMEM((2, KDIM, width // LANES, LANES), jnp.float32),
             pltpu.SemaphoreType.DMA((slots,)),
         ],
         compiler_params=pltpu.CompilerParams(vmem_limit_bytes=VMEM_LIMIT),
@@ -323,16 +340,16 @@
     )(pieces)
 
 
-def prepare_body(groups, devs, slots, tiles_hbm, holder_hbm, delta_hbm, out, first, *scratch):
+def tables_body(groups, devs, slots, tiles_hbm, holder_hbm, out, *scratch):
     tiles, holder, sem = scratch
-    sources = (tiles_hbm, holder_hbm, delta_hbm.at[0])
+    sources = (tiles_hbm, holder_hbm)
     copies = [
         pltpu.make_async_copy(source, target, sem.at[i])
-        for i, (source, target) in enumerate(zip(sources, (tiles, holder, first)))
+        for i, (source, target) in enumerate(zip(sources, (tiles, holder)))
     ]
     for copy in copies:
         copy.start()
-    for copy in copies[:2]:
+    for copy in copies:
         copy.wait()
     f32, i32 = jnp.float32, jnp.int32
     group, dev = lax.axis_index("grp"), lax.axis_index("dev")
@@ -373,24 +390,38 @@
         out[4 + side : 5 + side, :] = twin[side]
     out[6:7, :] = jnp.where(held[0] >= 0, 1, 0)
     out[7:8, :] = jnp.zeros((1, LANES), i32)
-    copies[2].wait()
-
-
-def prepare(tile_list, holder, dissim, groups, devs):
+
+
+def tables(tile_list, holder, groups, devs, slots):
     arrays = [tile_list.T, holder.reshape(1, -1)]
     return pl.pallas_call(
-        functools.partial(prepare_body, groups, devs, dissim.shape[0]),
-        out_shape=(
-            jax.ShapeDtypeStruct((8, LANES), jnp.int32),
-            pltpu.VMEM(dissim.shape[1:], dissim.dtype),
-        ),
-        in_specs=[pl.BlockSpec(memory_space=pltpu.HBM)] * 3,
-        out_specs=[pl.BlockSpec(memory_space=pltpu.VMEM)] * 2,
+        functools.partial(tables_body, groups, devs, slots),
+        out_shape=jax.ShapeDtypeStruct((8, LANES), jnp.int32),
+        in_specs=[pl.BlockSpec(memory_space=pltpu.HBM)] * 2,
+        out_specs=pl.BlockSpec(memory_space=pltpu.VMEM),
         scratch_shapes=[pltpu.VMEM(a.shape, a.dtype) for a in arrays]
-        + [pltpu.SemaphoreType.DMA((3,))],
-        compiler_params=pltpu.CompilerParams(vmem_limit_bytes=SMALL_LIMIT),
-        name="prepare",
-    )(*[pltpu.with_memory_space_constraint(a, pltpu.HBM) for a in arrays + [dissim]])
+        + [pltpu.SemaphoreType.DMA((2,))],
+        compiler_params=pltpu.CompilerParams(vmem_limit_bytes=SMALL_LIMIT),
+        name="tables",
+    )(*[pltpu.with_memory_space_constraint(a, pltpu.HBM) for a in arrays])
+
+
+def fetch_body(source, out, sem):
+    copy = pltpu.make_async_copy(source.at[:2], out, sem)
+    copy.start()
+    copy.wait()
+
+
+def first_tiles(dissim):
+    return pl.pallas_call(
+        fetch_body,
+        out_shape=pltpu.VMEM((2, *dissim.shape[1:]), dissim.dtype),
+        in_specs=[pl.BlockSpec(memory_space=pltpu.HBM)],
+        out_specs=pl.BlockSpec(memory_space=pltpu.VMEM),
+        scratch_shapes=[pltpu.SemaphoreType.DMA],
+        compiler_params=pltpu.CompilerParams(vmem_limit_bytes=SMALL_LIMIT),
+        name="first_tiles",
+    )(pltpu.with_memory_space_constraint(dissim, pltpu.HBM))
 
 
 def on_device(tile_list, holder, coordinates, dissim):
@@ -402,10 +433,12 @@
     plane = plane_groups(groups, devs)
     sent = spread(coordinates, chips)
     own = lax.all_to_all(sent, AXES, 0, 0, tiled=True, axis_index_groups=plane)
-    own, dissim = lax.optimization_barrier((own, dissim))
+    own, tile_list, holder = lax.optimization_barrier((own, tile_list, holder))
     twin = to_twin(own, groups * devs)
-    places, first = prepare(tile_list, holder, dissim, groups, devs)
+    places = tables(tile_list, holder, groups, devs, slots)
     picked = pick(places, own, twin, groups, slots)
+    *picked, dissim = lax.optimization_barrier((*picked, dissim))
+    first = first_tiles(dissim)
     others = [
         lax.ppermute(picked[d - 1], AXES, line_perm(groups, devs, d)) for d in range(1, groups)
     ]

time: 66.7 us -> 66.3 us (level)
  Pallas kernels: 16 us -> 9.79 us
  blocking collectives: 28.6 us -> 34 us
  starting transfers between devices: 8.32 us -> 13.6 us
  waiting for transfers between devices: 12.3 us -> 7.2 us
    pallas_call x1, Pallas kernels: 11.8 us -> 3.64 us  [tile_parts(): pl.pallas_call(functools.partial(tile_body, rows, width), out_shape=jax.S...]
    all_to_all x1, blocking collectives: 12.5 us -> 17.9 us  [on_device(): lax.all_to_all(pieces, AXES, 0, 0, tiled=True, axis_index_groups=plane)]
    ppermute x5, starting transfers between devices: 0.52 us -> 4.41 us  [to_twin(): return lax.ppermute(array, AXES, core_perm(devices))]
    ppermute x3, waiting for transfers between devices: 4.11 us -> 1.25 us  [from_line(): lax.ppermute(array, AXES, line_perm(groups, devs, d))]
    ppermute x3, waiting for transfers between devices: 6.85 us -> 4.65 us  [on_device(): lax.ppermute(picked[d - 1], AXES, line_perm(groups, devs, d))]
    pallas_call x1 -> x2, Pallas kernels: 1.65 us -> 3.64 us  [the longest x1 2.2 us: first_tiles(): pl.pallas_call(fetch_body, out_shape=pltpu.VMEM((2, *dissim.shape[1:]), d...]
    ppermute x3, starting transfers between devices: 3.29 us -> 4.72 us  [from_line(): lax.ppermute(array, AXES, line_perm(groups, devs, d))]
  transfers between devices with their start and end apart: 11 -> 11, of which waited for: 8 -> 8; matrix products, arithmetic and copies ran while one was open for 0% -> 0% of each run, Pallas kernels for 2% -> 6%
where the time goes in v7:
time: 66.3 us; the launch traced here: 66.1 us
  blocking collectives  34 us (51%)
  starting transfers between devices  13.6 us (21%)
  Pallas kernels  9.79 us (15%)
  waiting for transfers between devices  7.2 us (11%)
  local copies, waits for them, and re-layouts  0.71 us (1%)
  between operations  0.71 us (1%)
    all_to_all x1, blocking collectives, on_device(): lax.all_to_all(pieces, AXES, 0, 0, tiled=True, axis_index_groups=plane)  17.9 us
    all_to_all x1, blocking collectives, on_device(): own = lax.all_to_all(sent, AXES, 0, 0, tiled=True, axis_index_groups=plane)  16.1 us
    ppermute x3, starting transfers between devices, from_line(): lax.ppermute(array, AXES, line_perm(groups, devs, d))  4.72 us
    ppermute x3, waiting for transfers between devices, on_device(): lax.ppermute(picked[d - 1], AXES, line_perm(groups, devs, d))  4.65 us
    ppermute x3, starting transfers between devices, on_device(): lax.ppermute(picked[d - 1], AXES, line_perm(groups, devs, d))  4.51 us
    ppermute x5, starting transfers between devices, to_twin(): return lax.ppermute(array, AXES, core_perm(devices))  4.41 us
    pallas_call x1, Pallas kernels, tile_parts(): pl.pallas_call(functools.partial(tile_body, rows, width), out_shape=jax.S...  3.64 us
    pallas_call x1, Pallas kernels, first_tiles(): pl.pallas_call(fetch_body, out_shape=pltpu.VMEM((2, *dissim.shape[1:]), d...  2.2 us
  transfers between devices with their start and end apart: 11, of which 8 were waited for; matrix products, arithmetic and copies ran while one was open for 0% of the time, Pallas kernels for 6%

profile of v7, /device:TPU:0, one launch (start us, length us, event | category | flops | bytes accessed | tf_op | source)
XLA Modules:
  0.0 66.1 jit_solution(16514332142523157091)
XLA Ops:
  0.6 0.0 copy-start
  0.6 0.7 %copy-done = f32[3,1024]{1,0:T(4,128)S(1)} copy-done((f32[3,1024]{1,0:T(4,128)S(1)}, f32[3,1024]{1,0:T(4,128)}, u32[]{:S(2)}) %copy-start) | copy-done | bytes 12312
  1.4 16.1 %all_to_all.10.own.refs_0_ = f32[16,24,128]{2,1,0:T(8,128)S(1)} all-to-all(f32[16,24,128]{2,1,0:T(8,128)S(1)} %spread.1), channel_id=1, replica_groups={{0,2,4,6,8,10,12,14,16,18,20,22,24,26,28,30},{1,3,5,7,9,11,13,15,17,19,..., dimensions={0} | all-to-all | bytes 393216 | tf_op jit(solution)/shard_map/all_to_all | solution.py:435
  17.5 0.0 collective-permute-start
  17.5 1.4 %tables.1.places.sc.where = s32[8,128]{1,0:T(8,128)S(1)} custom-call(s32[3,256]{1,0:T(4,128)} %bitcast.3, s32[1,128]{1,0:T(1,128)} %bitcast.4), custom_call_target="tpu_custom_call" | custom-call | tf_op jit(solution)/shard_map/tables/pallas_call | solution.py:397
  18.9 0.0 collective-permute-done.twin.refs_1_
  18.9 0.7 %pick.1 = (f32[8,24,128]{2,1,0:T(8,128)S(1)}, f32[8,24,128]{2,1,0:T(8,128)S(1)}, f32[8,24,128]{2,1,0:T(8,128)S(1)}) custom-call(s32[8,128]{1,0:T(8,128)S(1)} %tables.1.places.sc.where, f32[16,24,128]{2,1,0:T(8,128)S(1)} %all_to_all.10.own.refs_0_, f32[16,24,128]{2,1,0:T(8,128)S(1)} %collective-permute-done.twin.refs_1_), custom_call_target="tpu_custom_call" | custom-call | tf_op jit(solution)/shard_map/pick/pallas_call | solution.py:86
  19.6 2.8 %collective-permute-start.1 = (f32[8,24,128]{2,1,0:T(8,128)S(1)}, f32[8,24,128]{2,1,0:T(8,128)S(1)}, u32[]{:S(2)}, u32[]{:S(2)}) collective-permute-start(f32[8,24,128]{2,1,0:T(8,128)S(1)} %get-tuple-element.21), channel_id=1, source_target_pairs={{32,0},{33,1},{34,2},{35,3},{36,4},{37,5},{38,6},{39,7},{40,8},{41... | collective-permute-start | bytes 294920 | tf_op jit(solution)/shard_map/ppermute | solution.py:443
  22.5 0.8 %collective-permute-start.2 = (f32[8,24,128]{2,1,0:T(8,128)S(1)}, f32[8,24,128]{2,1,0:T(8,128)S(1)}, u32[]{:S(2)}, u32[]{:S(2)}) collective-permute-start(f32[8,24,128]{2,1,0:T(8,128)S(1)} %get-tuple-element.22), channel_id=1, source_target_pairs={{64,0},{65,1},{66,2},{67,3},{68,4},{69,5},{70,6},{71,7},{72,8},{73... | collective-permute-start | bytes 294920 | tf_op jit(solution)/shard_map/ppermute | solution.py:443
  23.3 0.9 %collective-permute-start.3 = (f32[8,24,128]{2,1,0:T(8,128)S(1)}, f32[8,24,128]{2,1,0:T(8,128)S(1)}, u32[]{:S(2)}, u32[]{:S(2)}) collective-permute-start(f32[8,24,128]{2,1,0:T(8,128)S(1)} %get-tuple-element.23), channel_id=1, source_target_pairs={{96,0},{97,1},{98,2},{99,3},{100,4},{101,5},{102,6},{103,7},{104,8... | collective-permute-start | bytes 294920 | tf_op jit(solution)/shard_map/ppermute | solution.py:443
  24.2 2.2 %first_tiles.1.first = bf16[2,1024,1024]{2,1,0:T(8,128)(2,1)S(1)} custom-call(bf16[4,1024,1024]{2,1,0:T(8,128)(2,1)} %delta_hbm), custom_call_target="tpu_custom_call" | custom-call | tf_op jit(solution)/shard_map/first_tiles/pallas_call | solution.py:416
  26.4 1.0 %collective-permute-done.1.refs_2_ = f32[8,24,128]{2,1,0:T(8,128)S(1)} collective-permute-done((f32[8,24,128]{2,1,0:T(8,128)S(1)}, f32[8,24,128]{2,1,0:T(8,128)S(1)}, u32[]{:S(2)}, u32[]{:S(2)}) %collective-permute-start.1) | collective-permute-done | bytes 98336 | tf_op jit(solution)/shard_map/ppermute | solution.py:443
  27.3 2.3 %collective-permute-done.2.refs_3_ = f32[8,24,128]{2,1,0:T(8,128)S(1)} collective-permute-done((f32[8,24,128]{2,1,0:T(8,128)S(1)}, f32[8,24,128]{2,1,0:T(8,128)S(1)}, u32[]{:S(2)}, u32[]{:S(2)}) %collective-permute-start.2) | collective-permute-done | bytes 98336 | tf_op jit(solution)/shard_map/ppermute | solution.py:443
  29.6 1.4 %collective-permute-done.3.refs_4_ = f32[8,24,128]{2,1,0:T(8,128)S(1)} collective-permute-done((f32[8,24,128]{2,1,0:T(8,128)S(1)}, f32[8,24,128]{2,1,0:T(8,128)S(1)}, u32[]{:S(2)}, u32[]{:S(2)}) %collective-permute-start.3) | collective-permute-done | bytes 98336 | tf_op jit(solution)/shard_map/ppermute | solution.py:443
  31.0 3.6 %tile_parts.1.refs_0_ = f32[200,128]{1,0:T(8,128)S(1)} custom-call(s32[8,128]{1,0:T(8,128)S(1)} %tables.1.places.sc.where, bf16[4,1024,1024]{2,1,0:T(8,128)(2,1)} %delta_hbm, bf16[2,1024,1024]{2,1,0:T(8,128)(2,1)S(1)} %first_tiles.1.first, f32[16,24,128]{2,1,0:T(8,128)S(1)} %all_to_all.10.own.refs_0_, f32[16,24,128]{2,1,0:T(8,128)S(1)} %collective-permute-done.twin.refs_1_, ...), custom_call_target="tpu_custom_call" | custom-call | tf_op jit(solution)/shard_map/tile_parts/pallas_call | solution.py:255
  34.7 0.1 collective-permute-start.6
  34.7 4.6 %collective-permute-start.5 = (f32[200,128]{1,0:T(8,128)S(1)}, f32[200,128]{1,0:T(8,128)S(1)}, u32[]{:S(2)}, u32[]{:S(2)}) collective-permute-start(f32[200,128]{1,0:T(8,128)S(1)} %tile_parts.1.refs_0_), channel_id=1, source_target_pairs={{64,0},{65,1},{66,2},{67,3},{68,4},{69,5},{70,6},{71,7},{72,8},{73... | collective-permute-start | bytes 307208 | tf_op jit(solution)/shard_map/ppermute | solution.py:49
  39.4 0.0 collective-permute-start.4
  39.4 0.7 %collective-permute-start.7 = (f32[200,128]{1,0:T(8,128)S(1)}, f32[200,128]{1,0:T(8,128)S(1)}, u32[]{:S(2)}, u32[]{:S(2)}) collective-permute-start(f32[200,128]{1,0:T(8,128)S(1)} %tile_parts.1.refs_0_), channel_id=1, source_target_pairs={{0,1},{1,0},{2,3},{3,2},{4,5},{5,4},{6,7},{7,6},{8,9},{9,8},{10,11... | collective-permute-start | bytes 307208 | tf_op jit(solution)/shard_map/ppermute | solution.py:44
  40.1 0.5 collective-permute-done.6.refs_3_
  40.6 3.7 %collective-permute-start.10 = (f32[200,128]{1,0:T(8,128)S(1)}, f32[200,128]{1,0:T(8,128)S(1)}, u32[]{:S(2)}, u32[]{:S(2)}) collective-permute-start(f32[200,128]{1,0:T(8,128)S(1)} %collective-permute-done.6.refs_3_), channel_id=1, source_target_pairs={{0,1},{1,0},{2,3},{3,2},{4,5},{5,4},{6,7},{7,6},{8,9},{9,8},{10,11... | collective-permute-start | bytes 307208 | tf_op jit(solution)/shard_map/ppermute | solution.py:44
  44.3 0.0 collective-permute-done.5.refs_2_
  44.3 0.0 collective-permute-start.9
  44.3 0.7 %collective-permute-done.4.refs_1_ = f32[200,128]{1,0:T(8,128)S(1)} collective-permute-done((f32[200,128]{1,0:T(8,128)S(1)}, f32[200,128]{1,0:T(8,128)S(1)}, u32[]{:S(2)}, u32[]{:S(2)}) %collective-permute-start.4) | collective-permute-done | bytes 102432 | tf_op jit(solution)/shard_map/ppermute | solution.py:49
  45.1 0.0 collective-permute-start.8
  45.1 0.0 collective-permute-done.7.refs_4_
  45.1 0.2 collective-permute-done.10.refs_7_
  45.3 0.4 collective-permute-done.9.refs_6_
  45.6 0.7 %collective-permute-done.8.refs_5_ = f32[200,128]{1,0:T(8,128)S(1)} collective-permute-done((f32[200,128]{1,0:T(8,128)S(1)}, f32[200,128]{1,0:T(8,128)S(1)}, u32[]{:S(2)}, u32[]{:S(2)}) %collective-permute-start.8) | collective-permute-done | bytes 102432 | tf_op jit(solution)/shard_map/ppermute | solution.py:44
  46.4 1.1 %by_chip.1 = f32[16,32,128]{2,1,0:T(8,128)S(1)} custom-call(s32[8,128]{1,0:T(8,128)S(1)} %tables.1.places.sc.where, f32[200,128]{1,0:T(8,128)S(1)} %tile_parts.1.refs_0_, f32[200,128]{1,0:T(8,128)S(1)} %collective-permute-done.4.refs_1_, f32[200,128]{1,0:T(8,128)S(1)} %collective-permute-done.5.refs_2_, f32[200,128]{1,0:T(8,128)S(1)} %collective-permute-done.6.refs_3_, ...), custom_call_target="tpu_custom_call" | custom-call | tf_op jit(solution)/shard_map/by_chip/pallas_call | solution.py:302
  47.5 17.9 %all_to_all.11.pieces = f32[16,32,128]{2,1,0:T(8,128)S(1)} all-to-all(f32[16,32,128]{2,1,0:T(8,128)S(1)} %by_chip.1), channel_id=1, replica_groups={{0,2,4,6,8,10,12,14,16,18,20,22,24,26,28,30},{1,3,5,7,9,11,13,15,17,19,..., dimensions={0} | all-to-all | bytes 524288 | tf_op jit(solution)/shard_map/all_to_all | solution.py:449
  65.4 0.6 total.1
  (1 shorter events, 0.0 us)
Async XLA Ops:
  0.6 0.7 %copy-start = (f32[3,1024]{1,0:T(4,128)S(1)}, f32[3,1024]{1,0:T(4,128)}, u32[]{:S(2)}) copy-start(f32[3,1024]{1,0:T(4,128)} %coords.1) | copy-start | bytes 36868
  17.5 1.5 %collective-permute-start = (f32[16,24,128]{2,1,0:T(8,128)S(1)}, f32[16,24,128]{2,1,0:T(8,128)S(1)}, u32[]{:S(2)}, u32[]{:S(2)}) collective-permute-start(f32[16,24,128]{2,1,0:T(8,128)S(1)} %all_to_all.10.own.refs_0_), channel_id=1, source_target_pairs={{0,1},{1,0},{2,3},{3,2},{4,5},{5,4},{6,7},{7,6},{8,9},{9,8},{10,11... | collective-permute-start | bytes 589832 | tf_op jit(solution)/shard_map/ppermute | solution.py:44
  19.6 7.7 %collective-permute-start.1 = (f32[8,24,128]{2,1,0:T(8,128)S(1)}, f32[8,24,128]{2,1,0:T(8,128)S(1)}, u32[]{:S(2)}, u32[]{:S(2)}) collective-permute-start(f32[8,24,128]{2,1,0:T(8,128)S(1)} %get-tuple-element.21), channel_id=1, source_target_pairs={{32,0},{33,1},{34,2},{35,3},{36,4},{37,5},{38,6},{39,7},{40,8},{41... | collective-permute-start | bytes 294920 | tf_op jit(solution)/shard_map/ppermute | solution.py:443
  22.5 7.1 %collective-permute-start.2 = (f32[8,24,128]{2,1,0:T(8,128)S(1)}, f32[8,24,128]{2,1,0:T(8,128)S(1)}, u32[]{:S(2)}, u32[]{:S(2)}) collective-permute-start(f32[8,24,128]{2,1,0:T(8,128)S(1)} %get-tuple-element.22), channel_id=1, source_target_pairs={{64,0},{65,1},{66,2},{67,3},{68,4},{69,5},{70,6},{71,7},{72,8},{73... | collective-permute-start | bytes 294920 | tf_op jit(solution)/shard_map/ppermute | solution.py:443
  23.3 7.7 %collective-permute-start.3 = (f32[8,24,128]{2,1,0:T(8,128)S(1)}, f32[8,24,128]{2,1,0:T(8,128)S(1)}, u32[]{:S(2)}, u32[]{:S(2)}) collective-permute-start(f32[8,24,128]{2,1,0:T(8,128)S(1)} %get-tuple-element.23), channel_id=1, source_target_pairs={{96,0},{97,1},{98,2},{99,3},{100,4},{101,5},{102,6},{103,7},{104,8... | collective-permute-start | bytes 294920 | tf_op jit(solution)/shard_map/ppermute | solution.py:443
  34.7 5.9 %collective-permute-start.6 = (f32[200,128]{1,0:T(8,128)S(1)}, f32[200,128]{1,0:T(8,128)S(1)}, u32[]{:S(2)}, u32[]{:S(2)}) collective-permute-start(f32[200,128]{1,0:T(8,128)S(1)} %tile_parts.1.refs_0_), channel_id=1, source_target_pairs={{96,0},{97,1},{98,2},{99,3},{100,4},{101,5},{102,6},{103,7},{104,8... | collective-permute-start | bytes 307208 | tf_op jit(solution)/shard_map/ppermute | solution.py:49
  34.7 9.6 %collective-permute-start.5 = (f32[200,128]{1,0:T(8,128)S(1)}, f32[200,128]{1,0:T(8,128)S(1)}, u32[]{:S(2)}, u32[]{:S(2)}) collective-permute-start(f32[200,128]{1,0:T(8,128)S(1)} %tile_parts.1.refs_0_), channel_id=1, source_target_pairs={{64,0},{65,1},{66,2},{67,3},{68,4},{69,5},{70,6},{71,7},{72,8},{73... | collective-permute-start | bytes 307208 | tf_op jit(solution)/shard_map/ppermute | solution.py:49
  39.4 5.7 %collective-permute-start.4 = (f32[200,128]{1,0:T(8,128)S(1)}, f32[200,128]{1,0:T(8,128)S(1)}, u32[]{:S(2)}, u32[]{:S(2)}) collective-permute-start(f32[200,128]{1,0:T(8,128)S(1)} %tile_parts.1.refs_0_), channel_id=1, source_target_pairs={{32,0},{33,1},{34,2},{35,3},{36,4},{37,5},{38,6},{39,7},{40,8},{41... | collective-permute-start | bytes 307208 | tf_op jit(solution)/shard_map/ppermute | solution.py:49
  39.4 5.7 %collective-permute-start.7 = (f32[200,128]{1,0:T(8,128)S(1)}, f32[200,128]{1,0:T(8,128)S(1)}, u32[]{:S(2)}, u32[]{:S(2)}) collective-permute-start(f32[200,128]{1,0:T(8,128)S(1)} %tile_parts.1.refs_0_), channel_id=1, source_target_pairs={{0,1},{1,0},{2,3},{3,2},{4,5},{5,4},{6,7},{7,6},{8,9},{9,8},{10,11... | collective-permute-start | bytes 307208 | tf_op jit(solution)/shard_map/ppermute | solution.py:44
  40.6 4.7 %collective-permute-start.10 = (f32[200,128]{1,0:T(8,128)S(1)}, f32[200,128]{1,0:T(8,128)S(1)}, u32[]{:S(2)}, u32[]{:S(2)}) collective-permute-start(f32[200,128]{1,0:T(8,128)S(1)} %collective-permute-done.6.refs_3_), channel_id=1, source_target_pairs={{0,1},{1,0},{2,3},{3,2},{4,5},{5,4},{6,7},{7,6},{8,9},{9,8},{10,11... | collective-permute-start | bytes 307208 | tf_op jit(solution)/shard_map/ppermute | solution.py:44
  44.3 1.3 %collective-permute-start.9 = (f32[200,128]{1,0:T(8,128)S(1)}, f32[200,128]{1,0:T(8,128)S(1)}, u32[]{:S(2)}, u32[]{:S(2)}) collective-permute-start(f32[200,128]{1,0:T(8,128)S(1)} %collective-permute-done.5.refs_2_), channel_id=1, source_target_pairs={{0,1},{1,0},{2,3},{3,2},{4,5},{5,4},{6,7},{7,6},{8,9},{9,8},{10,11... | collective-permute-start | bytes 307208 | tf_op jit(solution)/shard_map/ppermute | solution.py:44
  45.1 1.3 %collective-permute-start.8 = (f32[200,128]{1,0:T(8,128)S(1)}, f32[200,128]{1,0:T(8,128)S(1)}, u32[]{:S(2)}, u32[]{:S(2)}) collective-permute-start(f32[200,128]{1,0:T(8,128)S(1)} %collective-permute-done.4.refs_1_), channel_id=1, source_target_pairs={{0,1},{1,0},{2,3},{3,2},{4,5},{5,4},{6,7},{7,6},{8,9},{9,8},{10,11... | collective-permute-start | bytes 307208 | tf_op jit(solution)/shard_map/ppermute | solution.py:44
